TPU v7x, 32 devices: a whole 2x2x4 slice. The times are simulated.
32 devices in a mesh: section: 16 (over z, x, core), row: 2 (over y).
Axes of the slice: x: 2, y: 2, z: 4, core: 2. Of those that a mesh axis runs over, the one named last changes fastest.
Arguments:
- fwd_queue: bfloat16 [16, 3, 8, 32, 320], P('section', None, 'row'), may hold values from -45 to 45
- bwd_queue: bfloat16 [16, 3, 8, 32, 320], P('section', None, 'row'), may hold values from -6 to 6
- mirror_queue: bfloat16 [16, 3, 8, 32, 320], P('section', None, 'row'), may hold values from -45 to 45
- stash: bfloat16 [16, 3, 2, 8, 32, 320], P('section', None, None, 'row'), may hold values from -45 to 45
- weights: bfloat16 [16, 2, 3, 3, 320, 320], P('section', None, None, None, 'row'), may hold values from -0.109375 to 0.109375
- grad_acc: float32 [16, 2, 3, 3, 320, 320], P('section', None, None, None, 'row'), may hold values from -6 to 6
- fwd_slot: int32 [16, 2], replicated, may hold values from 0 to 2
- bwd_slot: int32 [16, 2], replicated, may hold values from 0 to 2
Outputs:
- forward_queue_after: bfloat16 [16, 3, 8, 32, 320], P('section', None, 'row')
- next_grads: bfloat16 [16, 3, 8, 32, 320], P('section', None, 'row')
- next_mirror: bfloat16 [16, 3, 8, 32, 320], P('section', None, 'row')
- next_stash: bfloat16 [16, 3, 2, 8, 32, 320], P('section', None, None, 'row')
- grad_total: float32 [16, 2, 3, 3, 320, 320], P('section', None, None, None, 'row')
- section_outputs: bfloat16 [16, 2, 8, 32, 320], P('section', None, 'row')
All inputs are finite; a program needn't handle non-finite values.
Results may differ from a plain program's by a relative error of at most 0.012.
Values may be sent and summed in bfloat16 or wider, within the bound.
No kernel may reach another device: no remote copies, remote signals or barrier semaphores. Data moves between devices by JAX's collectives and lax.ppermute only.
A program may use at most 128 MiB of HBM per device.

v0:
```python
import functools

import jax
import jax.numpy as jnp
from jax import lax
from jax.experimental import pallas as pl
from jax.experimental.pallas import tpu as pltpu
from jax.sharding import PartitionSpec as P

GROUPS = 32
TICKS = 2
FOLD = 4
EPSILON = 1e-05
BF, F32 = jnp.bfloat16, jnp.float32
VMEM_LIMIT = 24 * 2**20


class Sizes:
    def __init__(self, queue, sections, rows):
        self.sections, self.parts = sections, rows
        self.cols = queue.shape[2]
        self.channels = queue.shape[3]
        self.local = queue.shape[1] * queue.shape[2]
        self.cells = self.local * rows
        self.share = self.channels // rows
        self.group = self.channels // GROUPS
        self.count = self.cells * self.group


def where_am_i():
    return lax.axis_index("section"), lax.axis_index("row")


def share_of(z, value, part):
    value = value.astype(F32)
    out = value[:, : z.share]
    for j in range(1, z.parts):
        out = jnp.where(part == j, value[:, j * z.share : (j + 1) * z.share], out)
    return out


def all_shares(z, own, others, row):
    out = []
    for j in range(z.parts):
        value = own
        for d in range(1, z.parts):
            value = jnp.where(lax.rem(row + z.parts - d, z.parts) == j, others[d - 1], value)
        out.append(value)
    return out


def side_by_side(values):
    return jnp.concatenate([value.astype(F32) for value in values], axis=1)


def folded(value, blocks):
    rows = value.shape[0] // blocks
    return side_by_side([value[j * rows : (j + 1) * rows] for j in range(blocks)])


def unfolded(value, blocks):
    value, width = value.astype(F32), value.shape[1] // blocks
    return jnp.concatenate([value[:, j * width : (j + 1) * width] for j in range(blocks)], axis=0)


def fold(z, ref, value):
    ref[...] = folded(value, FOLD).astype(BF)


def unfold(z, ref):
    return unfolded(ref[...], FOLD)


def source(z, row, d):
    return lax.rem(row + z.parts - d, z.parts)


def target(z, row, d):
    return lax.rem(row + d, z.parts)


def part_rows(z, part):
    return pl.ds(pl.multiple_of(part * z.local, z.local), z.local)


def assemble(z, ref, pieces, row, start, width):
    for d, piece in enumerate(pieces):
        value = (piece if isinstance(piece, jax.Array) else piece[...]).astype(F32)
        value = value[:, start : start + width]
        ref[part_rows(z, source(z, row, d)), :] = value.astype(BF)


def group_sums(z, first, second):
    width = first.shape[1]
    line = lax.broadcasted_iota(jnp.int32, (8, width), 0)
    both = jnp.where(line == 0, first, jnp.where(line == 1, second, 0.0))
    across = lax.broadcasted_iota(jnp.int32, (width, width), 1).astype(F32)
    down = lax.broadcasted_iota(jnp.int32, (width, width), 0).astype(F32)
    same = jnp.floor((across + 0.5) * (1.0 / z.group)) == jnp.floor((down + 0.5) * (1.0 / z.group))
    sums = jnp.dot(
        both, same.astype(F32), precision=lax.Precision.HIGHEST, preferred_element_type=F32
    )
    return sums[0:1], sums[1:2]


def normalize(z, x):
    total, square = group_sums(
        z, jnp.sum(x, axis=0, keepdims=True), jnp.sum(x * x, axis=0, keepdims=True)
    )
    center = total / z.count
    factor = lax.rsqrt(square / z.count - center * center + EPSILON)
    return (x - center) * factor, factor


def sigmoid(y):
    return 1.0 / (1.0 + jnp.exp(-y))


def norm_back(z, y, factor, logistic, upstream):
    e = upstream * logistic * (1.0 + y * (1.0 - logistic))
    first, second = group_sums(
        z, jnp.sum(e, axis=0, keepdims=True), jnp.sum(e * y, axis=0, keepdims=True)
    )
    return factor * (e - first / z.count - y * (second / z.count))


def spread(z, x, line_ref, pad_ref):
    cells, cols = z.cells, z.cols
    width = x.shape[1]
    line_ref[8 : 8 + cells, :] = x
    column = lax.rem(lax.broadcasted_iota(jnp.int32, (cells, 1), 0), cols)
    edge = jnp.zeros((cols, width), BF)
    for b in range(3):
        pad_ref[b, :cols, :] = edge
        pad_ref[b, cols + cells :, :] = edge
    pad_ref[1, cols : cols + cells, :] = x.astype(BF)
    left = jnp.where(column > 0, line_ref[7 : 7 + cells, :], 0.0)
    pad_ref[0, cols : cols + cells, :] = left.astype(BF)
    right = jnp.where(column < cols - 1, line_ref[9 : 9 + cells, :], 0.0)
    pad_ref[2, cols : cols + cells, :] = right.astype(BF)


def convolve(z, pad_ref, kernel_ref, which):
    total = None
    for a in range(3):
        for b in range(3):
            term = jnp.dot(
                pad_ref[b, a * z.cols : a * z.cols + z.cells, :],
                kernel_ref[9 * which + 3 * a + b],
                preferred_element_type=F32,
            )
            total = term if total is None else total + term
    return total


def convolve_back(z, pad_ref, kernel_ref, which):
    total = None
    for a in range(3):
        for b in range(3):
            term = lax.dot_general(
                pad_ref[b, a * z.cols : a * z.cols + z.cells, :],
                kernel_ref[9 * which + 3 * (2 - a) + 2 - b],
                (((1,), (1,)), ((), ())),
                preferred_element_type=F32,
            )
            total = term if total is None else total + term
    return total


def pad_shapes(z, width):
    return [
        pltpu.VMEM((z.cells + 16, width), F32),
        pltpu.VMEM((3, z.cells + 2 * z.cols, width), BF),
    ]


def call(body, name, scalars, arrays, outs, scratch=(), after=(), remote=0, far_outs=0, aliases=None):
    near, far = pl.BlockSpec(memory_space=pltpu.VMEM), pl.BlockSpec(memory_space=pltpu.HBM)

    def inner(*refs):
        given = len(scalars) + len(arrays)
        body(*refs[:given], *refs[given + len(after) :])

    arrays = [
        pltpu.with_memory_space_constraint(x, pltpu.HBM) if j < remote else x
        for j, x in enumerate(arrays)
    ]
    near_outs = len(outs) - far_outs
    return pl.pallas_call(
        inner,
        name=name,
        out_shape=[
            jax.ShapeDtypeStruct(shape, dtype) if j < near_outs else pltpu.HBM(shape, dtype)
            for j, (shape, dtype) in enumerate(outs)
        ],
        in_specs=[pl.BlockSpec(memory_space=pltpu.SMEM)] * len(scalars)
        + [far] * remote
        + [near] * (len(arrays) - remote)
        + [pl.BlockSpec(memory_space=pl.ANY)] * len(after),
        out_specs=[near] * near_outs + [far] * far_outs,
        scratch_shapes=list(scratch),
        input_output_aliases=aliases or {},
        compiler_params=pltpu.CompilerParams(vmem_limit_bytes=VMEM_LIMIT),
        cost_estimate=pl.CostEstimate(flops=1, bytes_accessed=1, transcendentals=0),
    )(*scalars, *arrays, *after)


def held_until(values, earlier):
    return lax.optimization_barrier((tuple(values), earlier))[0]


def fetch(pairs, sems):
    copies = [pltpu.make_async_copy(a, b, sems.at[j]) for j, (a, b) in enumerate(pairs)]
    for copy in copies:
        copy.start()
    for copy in copies:
        copy.wait()


def pack_first(z, fs_far, bs_far, fwd_far, bwd_far, mir_far, stash_far, *refs):
    n = z.parts
    heads = refs[:n]
    fwd, bwd, mir, stash, fs, bs, sems = refs[n:]
    fetch(
        [
            (fs_far, fs),
            (bs_far, bs),
            (fwd_far, fwd),
            (bwd_far, bwd),
            (mir_far, mir),
            (stash_far, stash),
        ],
        sems,
    )
    s, row = where_am_i()
    h = fwd[fs[0, s]]
    for d in range(n):
        fold(z, heads[d], share_of(z, h, target(z, row, d)))


def taken_back(z, bs, s):
    later, partner = jnp.minimum(s + 1, z.sections - 1), z.sections - 1 - s
    return (
        jnp.logical_and(s < z.sections - 1, bs[0, later] == bs[1, s]),
        jnp.logical_and(s < z.sections // 2, bs[0, partner] == bs[1, s]),
    )


def pack_later(z, fs_far, bs_far, fwd, bwd, mir, stash, *refs):
    n = z.parts
    pieces, groups = refs[:n], [refs[j * n : (j + 1) * n] for j in range(1, 5)]
    fs, bs, sems = refs[5 * n :]
    fetch([(fs_far, fs), (bs_far, bs)], sems)
    s, row = where_am_i()
    f1, b1 = fs[1, s], bs[1, s]
    grad_taken, skip_taken = taken_back(z, bs, s)
    skip_kept = jnp.logical_and(s < z.sections // 2, jnp.logical_not(skip_taken))
    kept = jnp.where(grad_taken, 0.0, bwd[b1].astype(F32))
    kept = kept + jnp.where(skip_kept, mir[b1].astype(F32), 0.0)
    f0, b0 = fs[0, s], bs[0, s]
    g = bwd[b0].astype(F32) + jnp.where(s < z.sections // 2, mir[b0].astype(F32), 0.0)
    for d, piece in enumerate(pieces):
        part = target(z, row, d)
        shares = [share_of(z, stash[2 * b0 + 1], part), share_of(z, mir[f0], part)]
        piece[...] = side_by_side(shares + [g]).astype(BF)
    values = [stash[2 * b0], stash[2 * b1], fwd[f1], stash[2 * b1 + 1], mir[f1]]
    rows = z.local // FOLD
    for d in range(n):
        shares = [share_of(z, value, target(z, row, d)) for value in values]
        grads = [kept[:, j * z.share : (j + 1) * z.share] for j in range(n)]
        for outs, parts in zip(groups, (shares[:2], shares[2:4], grads, shares[4:])):
            for j, value in enumerate(parts):
                outs[d][j * rows : (j + 1) * rows, :] = folded(value, FOLD).astype(BF)


def send_partials(z, row, total, own, sends, extra):
    own[...] = share_of(z, total, row)
    for d, send in enumerate(sends, 1):
        part = folded(share_of(z, total, target(z, row, d)), FOLD).astype(BF)
        send[: part.shape[0], :] = part
        send[part.shape[0] :, :] = extra[d][...]


def first_forward(z, *refs):
    n = z.parts
    pieces, extra, kernel = refs[:n], refs[n : 2 * n], refs[2 * n]
    own, h_out = refs[2 * n + 1 : 2 * n + 3]
    sends, (line, pad) = refs[2 * n + 3 : 3 * n + 2], refs[3 * n + 2 :]
    _, row = where_am_i()
    assemble(z, h_out, [unfold(z, piece) for piece in pieces], row, 0, z.share)
    y, _ = normalize(z, h_out[...].astype(F32))
    spread(z, y * sigmoid(y), line, pad)
    send_partials(z, row, convolve(z, pad, kernel, 0), own, sends, extra)


def enclosed(z, own, received, j):
    rows, base = z.local // FOLD, z.cells // FOLD
    at, there = slice(j * rows, (j + 1) * rows), slice(base + j * rows, base + (j + 1) * rows)
    return [unfolded(own[at, :], FOLD)] + [unfolded(x[there, :], FOLD) for x in received]


def later_forward(z, fs, *refs):
    n = z.parts
    arrivals, nexts, received = refs[:n], refs[n], refs[n + 1 : 2 * n]
    lasts, kernel = refs[2 * n : 3 * n], refs[3 * n]
    own, h_out, arrived, onward = refs[3 * n + 1 : 3 * n + 5]
    sends = refs[3 * n + 5 : 4 * n + 4]
    line, pad = refs[4 * n + 4 :]
    s, row = where_am_i()
    total = unfold(z, arrivals[0])
    for other in arrivals[1:]:
        total = total + unfold(z, other)
    total = total.astype(BF).astype(F32)
    arrived[...] = total.astype(BF)
    fold(z, onward, total)
    assemble(z, h_out, enclosed(z, nexts, received, 0), row, 0, z.share)
    prior = jnp.maximum(s - 1, 0)
    taken = jnp.logical_and(s > 0, fs[0, prior] == fs[1, s])
    h = jnp.where(taken, total, h_out[...].astype(F32))
    h_out[...] = h.astype(BF)
    y, _ = normalize(z, h)
    spread(z, y * sigmoid(y), line, pad)
    send_partials(z, row, convolve(z, pad, kernel, 0), own, sends, lasts)


def back_through_second(z, i, g, kernel, q_out, q_send, act_out, pad, line):
    y, factor = normalize(z, i.astype(F32))
    logistic = sigmoid(y)
    act_out[...] = (y * logistic).astype(BF)
    spread(z, g, line, pad)
    q = norm_back(z, y, factor, logistic, convolve_back(z, pad, kernel, 1)).astype(BF)
    q_out[...] = q
    fold(z, q_send, q.astype(F32))


def first_backward(z, *refs):
    n = z.parts
    pieces, heads, kernel = refs[:n], refs[n : 2 * n], refs[2 * n]
    q_out, q_send, pad, act_out = refs[2 * n + 1 : 2 * n + 5]
    sends, (i_ref, g_ref, line) = refs[2 * n + 5 : 3 * n + 4], refs[3 * n + 4 :]
    _, row = where_am_i()
    assemble(z, i_ref, pieces, row, 0, z.share)
    assemble(z, g_ref, pieces, row, 2 * z.share, z.channels)
    back_through_second(
        z, i_ref[...], g_ref[...].astype(F32), kernel, q_out, q_send, act_out, pad, line
    )
    rows = z.cells // FOLD
    for d, send in enumerate(sends, 1):
        send[:rows, :] = q_send[...]
        send[rows:, :] = heads[d][...]


def later_backward(z, fs, bs, *refs):
    n = z.parts
    arrivals, mirror, received, kept = refs[:n], refs[n], refs[n + 1 : 2 * n], refs[2 * n]
    nexts, others = refs[2 * n + 1], refs[2 * n + 2 : 3 * n + 1]
    i_before, arrived, kernel = refs[3 * n + 1 : 3 * n + 4]
    q_out, pad, act_out, grad_in, skip_in = refs[3 * n + 4 : 3 * n + 9]
    rows_own, sends = refs[3 * n + 9], refs[3 * n + 10 : 4 * n + 9]
    q_send, i_ref, full, line = refs[4 * n + 9 :]
    s, row = where_am_i()
    w = z.share
    shares = [unfold(z, part) for part in arrivals]
    grad = side_by_side(all_shares(z, shares[0], shares[1:], row))
    grad_in[...] = grad.astype(BF)
    shares = [unfolded(x[: z.cells // FOLD, :], FOLD) for x in received]
    skip = side_by_side(all_shares(z, unfold(z, mirror), shares, row))
    skip_in[...] = skip.astype(BF)
    grad_taken, skip_taken = taken_back(z, bs, s)
    for j in range(n):
        assemble(z, full.at[j], enclosed(z, kept, received, j), row, 0, w)
    g = side_by_side([full[j] for j in range(n)]) + jnp.where(grad_taken, grad, 0.0)
    g = g + jnp.where(skip_taken, skip, 0.0)
    g = g.astype(BF).astype(F32)
    assemble(z, i_ref, enclosed(z, nexts, others, 1), row, 0, w)
    i = jnp.where(fs[0, s] == bs[1, s], i_before[...].astype(F32), i_ref[...].astype(F32))
    back_through_second(z, i, g, kernel, q_out, q_send, act_out, pad, line)
    for d, out in enumerate([rows_own, *sends]):
        at = part_rows(z, target(z, row, d))
        part = folded(side_by_side([i_before[at, :], arrived[at, :]]), 2).astype(BF)
        out[out.shape[0] - part.shape[0] :, :] = part
    for send in sends:
        send[: q_send.shape[0], :] = q_send[...]


def second_convolution(z, encoder, row, own, received, skip, h, kernel, i_out, full, line, pad):
    c0 = own[...]
    for other in received:
        c0 = c0 + unfolded(other[: z.cells // FOLD, :], FOLD)
    i = jnp.where(encoder, c0, skip.astype(F32)).astype(BF)
    i_out[...] = i
    y, _ = normalize(z, i.astype(F32))
    spread(z, y * sigmoid(y), line, pad)
    total = convolve(z, pad, kernel, 1)
    base = h[...].astype(F32) + jnp.where(encoder, 0.0, c0)
    full[...] = total + side_by_side([jnp.where(row == j, base, 0.0) for j in range(z.parts)])


def middle(z, pad):
    return pad[1, z.cols : z.cols + z.cells, :].astype(F32)


def second_forward(z, *refs):
    n = z.parts
    own, received, h, pieces, kernel = refs[0], refs[1:n], refs[n], refs[n + 1 : 2 * n + 1], refs[2 * n + 1]
    i_out, full_out = refs[2 * n + 2 : 2 * n + 4]
    sends = refs[2 * n + 4 : 3 * n + 4]
    skip, full, line, pad = refs[3 * n + 4 :]
    s, row = where_am_i()
    encoder = s < z.sections // 2
    assemble(z, skip, pieces, row, z.share, z.share)
    second_convolution(
        z, encoder, row, own, received, skip[...], h, kernel, i_out, full, line, pad
    )
    full_out[...] = full[...].astype(BF)
    for d in range(n):
        fold(z, sends[d], share_of(z, full[...], target(z, row, d)))


def last_forward(z, fs, *refs):
    n = z.parts
    own, received, h = refs[0], refs[1:n], refs[n]
    lasts, arrived, kernel = refs[n + 1 : n + 4]
    sends = refs[n + 4 : 2 * n + 4]
    i_out, skip, full, line, pad = refs[2 * n + 4 :]
    s, row = where_am_i()
    encoder = s < z.sections // 2
    partner = z.sections - 1 - s
    assemble(z, skip, enclosed(z, lasts, received, 0), row, 0, z.share)
    now = jnp.where(
        fs[0, partner] == fs[1, s], unfold(z, arrived), skip[...].astype(F32)
    )
    second_convolution(z, encoder, row, own, received, now, h, kernel, i_out, full, line, pad)
    for d, send in enumerate(sends):
        at = part_rows(z, target(z, row, d))
        send[...] = side_by_side([full[at, :], i_out[at, :]]).astype(BF)


def joined_shares(z, own, received, row):
    others = [unfolded(other[: z.cells // FOLD, :], FOLD) for other in received]
    return side_by_side(all_shares(z, own[...].astype(F32), others, row))


def back_through_first(z, encoder, row, q, received, g_pad, h, kernel, act_out, pad, line):
    g = middle(z, g_pad)
    whole = joined_shares(z, q, received, row)
    now = jnp.where(encoder, whole, g)
    y, factor = normalize(z, h.astype(F32))
    logistic = sigmoid(y)
    act_out[...] = (y * logistic).astype(BF)
    spread(z, now, line, pad)
    back = norm_back(z, y, factor, logistic, convolve_back(z, pad, kernel, 0))
    return share_of(z, g, row) + back, whole


def second_backward(z, *refs):
    n = z.parts
    q, received, g = refs[0], refs[1:n], refs[n]
    heads, others, mirror = refs[n + 1], refs[n + 2 : 2 * n + 1], refs[2 * n + 1]
    grads, kernel = refs[2 * n + 2 : 3 * n + 2], refs[3 * n + 2]
    send, pad, act_out = refs[3 * n + 3 : 3 * n + 6]
    relays, (h, line) = refs[3 * n + 6 : 4 * n + 5], refs[4 * n + 5 :]
    s, row = where_am_i()
    for d, relay in enumerate(relays, 1):
        relay[: z.cells // FOLD, :] = mirror[...]
        relay[z.cells // FOLD :, :] = grads[d][...]
    assemble(z, h, enclosed(z, heads, others, 0), row, 0, z.share)
    value, _ = back_through_first(
        z, s < z.sections // 2, row, q, received, g, h[...], kernel, act_out, pad, line
    )
    fold(z, send, value)


def last_backward(z, fs, bs, *refs):
    n = z.parts
    q, received, g = refs[0], refs[1:n], refs[n]
    heads, others = refs[n + 1], refs[n + 2 : 2 * n + 1]
    h_before, kernel = refs[2 * n + 1 : 2 * n + 3]
    sends = refs[2 * n + 3 : 3 * n + 3]
    pad, act_out, h, value, line = refs[3 * n + 3 :]
    s, row = where_am_i()
    assemble(z, h, enclosed(z, heads, others, 1), row, 0, z.share)
    now = jnp.where(fs[0, s] == bs[1, s], h_before[...], h[...])
    result, _ = back_through_first(
        z, s < z.sections // 2, row, q, received, g, now, kernel, act_out, pad, line
    )
    value[...] = result.astype(BF)
    for d, send in enumerate(sends):
        fold(z, send, value[part_rows(z, target(z, row, d)), :])


def pack_rows(z, *refs):
    n = z.parts
    full, mirror = refs[:2]
    sends, skip = refs[2 : n + 2], refs[n + 2]
    _, row = where_am_i()
    skip[...] = unfold(z, mirror).astype(BF)
    for d, send in enumerate(sends):
        at = part_rows(z, target(z, row, d))
        send[...] = side_by_side([ref[at, :] for ref in (full, skip)]).astype(BF)


def add_rows(z, *refs):
    n = z.parts
    pieces, q, received = refs[:n], refs[n], refs[n + 1 : 2 * n]
    out, mirror, i_rows, whole = refs[2 * n :]
    s, row = where_am_i()
    c = z.channels
    whole[...] = joined_shares(z, q, received, row)
    values = [piece[...].astype(F32) for piece in pieces]
    total = sum(value[:, :c] for value in values)
    out[...] = total.astype(BF)
    mine = whole[part_rows(z, row), :]
    mirror[...] = jnp.where(s < z.sections // 2, total, mine).astype(BF)
    shares = all_shares(z, values[0][:, c:], [value[:, c:] for value in values[1:]], row)
    i_rows[...] = side_by_side(shares).astype(BF)


def write_queues(z, fs, bs, *refs):
    n = z.parts
    fwd, bwd, mir, stash, grad_in, skip_in = refs[:6]
    pieces = refs[6 : n + 6]
    token, outs, held = refs[n + 6], refs[n + 7 : n + 11], refs[n + 11 : n + 15]
    sems = refs[n + 15]
    token[...] = jnp.zeros_like(token)
    s, row = where_am_i()
    w = z.share
    prior, later = jnp.maximum(s - 1, 0), jnp.minimum(s + 1, z.sections - 1)
    partner = z.sections - 1 - s
    f0, f1 = fs[0, s], fs[1, s]
    mine = part_rows(z, row)
    copies = [pltpu.make_async_copy(a, b, sems.at[j]) for j, (a, b) in enumerate(zip(held, outs))]
    for ref, queue in zip(held, (fwd, bwd, mir, stash)):
        ref[...] = queue[...]

    @pl.when(s < z.sections - 1)
    def _():
        held[1][bs[0, later]] = grad_in[mine, :]

    copies[1].start()

    @pl.when(s < z.sections // 2)
    def _():
        held[2][bs[0, partner]] = skip_in[mine, :]

    copies[2].start()
    values = [unfolded(piece[piece.shape[0] - z.local // 2 :, :], 2) for piece in pieces]

    def joined(at):
        shares = [value[:, at : at + w] for value in values]
        return side_by_side(all_shares(z, shares[0], shares[1:], row)).astype(BF)

    fwd_in = joined(w)

    @pl.when(s > 0)
    def _():
        held[0][fs[0, prior]] = fwd_in

    copies[0].start()
    held[3][2 * f0] = fwd[f0]
    held[3][2 * f0 + 1] = joined(0)
    held[3][2 * f1] = fwd[f1]

    @pl.when(jnp.logical_and(s > 0, fs[0, prior] == f1))
    def _():
        held[3][2 * f1] = fwd_in

    copies[3].start()
    for copy in copies:
        copy.wait()


def finish(z, fs, bs, *refs):
    n = z.parts
    out1, i1, fwd1, mir1 = refs[4:8]
    rows0, grads1 = refs[8 : n + 8], refs[n + 8 : 2 * n + 8]
    fwd_out, bwd_out, mir_out, stash_out, emitted = refs[2 * n + 8 : 2 * n + 13]
    out0, skip, grads, sems = refs[2 * n + 13 :]
    s, row = where_am_i()
    c = z.channels
    prior, later = jnp.maximum(s - 1, 0), jnp.minimum(s + 1, z.sections - 1)
    partner = z.sections - 1 - s
    encoder, has_prior, has_later = s < z.sections // 2, s > 0, s < z.sections - 1
    first = jnp.where(encoder, bs[0, partner], fs[0, partner])
    second = jnp.where(encoder, bs[1, partner], fs[1, partner])
    skip_stays = jnp.logical_and(jnp.logical_not(encoder), first != second)

    def put(source, place, j):
        return pltpu.make_async_copy(source, place, sems.at[j])

    always = [
        put(out1, emitted.at[1], 0),
        put(i1, stash_out.at[2 * fs[1, s] + 1], 1),
        put(mir1, mir_out.at[second], 2),
        put(out0, emitted.at[0], 3),
    ]
    for copy in always[:3]:
        copy.start()
    onward, back = put(fwd1, fwd_out.at[fs[1, prior]], 4), put(grads, bwd_out.at[bs[1, later]], 5)
    aside = put(skip, mir_out.at[first], 6)
    pl.when(has_prior)(onward.start)
    pieces = [unfold(z, piece) for piece in grads1]
    grads[...] = side_by_side(all_shares(z, pieces[0], pieces[1:], row)).astype(BF)
    pl.when(has_later)(back.start)
    pieces = [piece[...].astype(F32) for piece in rows0]
    out0[...] = sum(piece[:, :c] for piece in pieces).astype(BF)
    always[3].start()
    shares = [piece[:, c:] for piece in pieces]
    skip[...] = side_by_side(all_shares(z, shares[0], shares[1:], row)).astype(BF)
    pl.when(skip_stays)(aside.start)
    for copy in always:
        copy.wait()
    pl.when(has_prior)(onward.wait)
    pl.when(has_later)(back.wait)
    pl.when(skip_stays)(aside.wait)


def add_taps(z, act, pad, before, store):
    turned = jnp.transpose(act[...].astype(F32)).astype(BF)
    for tap in range(9):
        a, b = divmod(tap, 3)
        at = (2 - a) * z.cols
        moved = pad[2 - b, at : at + z.cells, :]
        store(tap, before(tap) + jnp.dot(turned, moved, preferred_element_type=F32))


def kernel_grads_add(z, start, acc, act, pad, out):
    def store(tap, value):
        out[tap] = value

    add_taps(z, act, pad, lambda tap: acc[start + tap], store)


def kernel_grads_last(z, total, other, act, pad, token, out, held, sems):
    token[...] = jnp.zeros_like(token)
    copies = [pltpu.make_async_copy(other, out.at[9:], sems.at[9])]
    copies[0].start()

    def store(tap, value):
        held[tap] = value
        copies.append(pltpu.make_async_copy(held.at[tap], out.at[tap], sems.at[tap]))
        copies[-1].start()

    add_taps(z, act, pad, lambda tap: total[tap], store)
    for copy in copies:
        copy.wait()


def per_device(fwd_queue, bwd_queue, mirror_queue, stash, weights, grad_acc, fwd_slot, bwd_slot):
    sections, n = lax.axis_size("section"), lax.axis_size("row")
    z = Sizes(fwd_queue[0], sections, n)
    slots = fwd_queue.shape[1]
    c, w, local, cells = z.channels, z.share, z.local, z.cells
    fwd, bwd, mir = (x.reshape(slots, local, c) for x in (fwd_queue, bwd_queue, mirror_queue))
    kept = stash.reshape(2 * slots, local, c)
    kernels = weights.reshape(18, w, c)
    acc = grad_acc.reshape(18, w, c)
    fs, bs = fwd_slot.T, bwd_slot.T
    fold_shape, wide = (cells // FOLD, FOLD * w), (cells, c)
    half = (cells, w)

    def with_shares(k):
        return ((cells + k * local) // FOLD, FOLD * w)

    padded = (3, cells + 2 * z.cols, c)

    def move(x, d, step):
        route = [
            (s * n + r, step(s) * n + (r + d) % n) for s in range(sections) for r in range(n)
        ]
        return lax.ppermute(x, ("section", "row"), route)

    across = functools.partial(move, step=lambda s: s)
    onward = functools.partial(move, step=lambda s: (s + 1) % sections)
    backward = functools.partial(move, step=lambda s: (s - 1) % sections)
    crossed = functools.partial(move, step=lambda s: (sections - s) % sections)
    mirrored = functools.partial(move, step=lambda s: sections - 1 - s)

    def run(body, scalars, arrays, outs, scratch=(), **options):
        return call(
            functools.partial(body, z), body.__name__, scalars, arrays, outs, scratch, **options
        )

    def exchange(pieces):
        return [pieces[0]] + [across(piece, d) for d, piece in enumerate(pieces[1:], 1)]

    narrow_pad = pad_shapes(z, w)
    wide_line = pltpu.VMEM((cells + 16, c), F32)
    queues = (fwd, bwd, mir, kept)
    rows = (local, c)
    sems = pltpu.SemaphoreType.DMA
    packed = run(
        pack_first,
        (),
        (fs, bs, *queues),
        [((local // FOLD, FOLD * w), BF)] * n
        + [(x.shape, BF) for x in queues],
        [pltpu.SMEM(fs.shape, jnp.int32)] * 2 + [sems((6,))],
        remote=6,
    )
    inputs, held = exchange(packed[:n]), packed[n:]

    packed = run(
        pack_later,
        (),
        (fs, bs, *held),
        [((local, 2 * w + c), BF)] * n
        + [((k * (local // FOLD), FOLD * w), BF) for k in (2, 2, n, 1) for _ in range(n)],
        [pltpu.SMEM(fs.shape, jnp.int32)] * 2 + [sems((2,))],
        remote=2,
        after=(inputs[0],),
    )
    pieces, heads, nexts, grads, lasts = (packed[j * n : (j + 1) * n] for j in range(5))
    first = exchange(held_until(pieces, inputs))

    own, h0, *sends = run(
        first_forward,
        (),
        (*inputs, *heads, kernels),
        [(half, F32), (half, BF)] + [(with_shares(2), BF)] * (n - 1),
        narrow_pad,
    )
    sums = [across(x, d) for d, x in enumerate(sends, 1)]
    q0, q_send, g_pad0, act_i0, *sends = run(
        first_backward,
        (),
        (*first, *nexts, kernels),
        [(half, BF), (fold_shape, BF), (padded, BF), (half, BF)]
        + [(with_shares(2), BF)] * (n - 1),
        [pltpu.VMEM(half, BF), pltpu.VMEM(wide, BF), wide_line],
        after=(own,),
    )
    q_received = [across(x, d) for d, x in enumerate(sends, 1)]
    skip_in = mirrored(q_send, 0)

    def add_grads(start, total, act, pad, after):
        [out] = call(
            functools.partial(kernel_grads_add, z, start),
            f"kernel_grads_add_{start}",
            (),
            (total, act, pad),
            [((9, w, c), F32)],
            after=after,
        )
        return out

    sum_i = add_grads(9, acc, act_i0, g_pad0, (q0,))
    i0, full0, *sends = run(
        second_forward,
        (),
        (own, *sums, h0, *first, kernels),
        [(half, BF), (wide, BF)] + [(fold_shape, BF)] * n,
        [pltpu.VMEM(half, BF), pltpu.VMEM(wide, F32)] + narrow_pad,
        after=(sum_i,),
    )
    fwd_in = [onward(x, d) for d, x in enumerate(sends)]
    dh_send, f_pad0, act_h0, *relays = run(
        second_backward,
        (),
        (q0, *q_received, g_pad0, heads[0], *sums, skip_in, *grads, kernels),
        [(fold_shape, BF), (padded, BF), (half, BF)] + [(with_shares(n), BF)] * (n - 1),
        [pltpu.VMEM(half, BF), wide_line],
        after=(i0,),
    )
    dh_in = [backward(dh_send, d) for d in range(n)]
    relayed = [across(x, d) for d, x in enumerate(relays, 1)]

    own, h1, arrived, turned, *sends = run(
        later_forward,
        (fs,),
        (*fwd_in, nexts[0], *q_received, *lasts, kernels),
        [(half, F32), (half, BF), (half, BF), (fold_shape, BF)]
        + [(with_shares(1), BF)] * (n - 1),
        narrow_pad,
        after=(dh_send,),
    )
    received = [across(x, d) for d, x in enumerate(sends, 1)]
    mir_in = crossed(turned, 0)
    sum_h = add_grads(0, acc, act_h0, f_pad0, (own,))
    q1, g_pad1, act_i1, grad_in, skip_full, rows_own, *sends = run(
        later_backward,
        (fs, bs),
        (*dh_in, skip_in, *relayed, grads[0], nexts[0], *q_received, i0, arrived, kernels),
        [(half, BF), (padded, BF), (half, BF), (wide, BF), (wide, BF), ((local // 2, 4 * w), BF)]
        + [((cells // FOLD + local // 2, FOLD * w), BF)] * (n - 1),
        [pltpu.VMEM(fold_shape, BF), pltpu.VMEM(half, BF), pltpu.VMEM((n, *half), BF), wide_line],
        after=(sum_h,),
    )
    q_received = [across(x, d) for d, x in enumerate(sends, 1)]
    sends = run(
        last_forward,
        (fs,),
        (own, *received, h1, lasts[0], mir_in, kernels),
        [((local, c + w), BF)] * n,
        [pltpu.VMEM(half, BF), pltpu.VMEM(half, BF), pltpu.VMEM(wide, F32)] + narrow_pad,
        after=(q1,),
    )
    rows1 = exchange(sends)
    part_i = add_grads(0, sum_i, act_i1, g_pad1, (sends[0],))
    packed = run(
        pack_rows,
        (),
        (full0, mir_in),
        [((local, c + w), BF)] * n,
        [pltpu.VMEM(half, BF)],
        after=(part_i,),
    )
    token, *written = run(
        write_queues,
        (fs, bs),
        (*held, grad_in, skip_full, rows_own, *q_received),
        [((8, 128), F32)] + [(x.shape, BF) for x in queues],
        [pltpu.VMEM(x.shape, BF) for x in queues] + [sems((4,))],
        far_outs=4,
        after=(packed[0],),
    )
    rows0 = exchange(held_until(packed, (rows1, token)))
    out1, mirror1, i1 = run(
        add_rows,
        (),
        (*rows1, q1, *q_received),
        [(rows, BF)] * 3,
        [pltpu.VMEM(wide, F32)],
        after=(token,),
    )
    fwd1, mir1 = onward(out1, 0), mirrored(mirror1, 0)
    *dh_sends, f_pad1, act_h1 = run(
        last_backward,
        (fs, bs),
        (q1, *q_received, g_pad1, heads[0], *sums, h0, kernels),
        [((local // FOLD, FOLD * w), BF)] * n + [(padded, BF), (half, BF)],
        [pltpu.VMEM(half, BF), pltpu.VMEM(half, BF), wide_line],
        after=(out1,),
    )
    dh1_in = [backward(x, d) for d, x in enumerate(dh_sends)]
    token, grad_total = run(
        kernel_grads_last,
        (),
        (sum_h, part_i, act_h1, f_pad1),
        [((8, 128), F32), ((18, w, c), F32)],
        [pltpu.VMEM((9, w, c), F32), sems((10,))],
        far_outs=1,
    )
    fwd_out, bwd_out, mir_out, stash_out, emitted = run(
        finish,
        (fs, bs),
        (*written, out1, i1, fwd1, mir1, *rows0, *dh1_in),
        [(x.shape, BF) for x in queues] + [((TICKS, local, c), BF)],
        [pltpu.VMEM(rows, BF)] * 3 + [sems((7,))],
        remote=4,
        far_outs=5,
        aliases={j + 2: j for j in range(4)},
        after=(token,),
    )
    return (
        fwd_out.reshape(fwd_queue.shape),
        bwd_out.reshape(bwd_queue.shape),
        mir_out.reshape(mirror_queue.shape),
        stash_out.reshape(stash.shape),
        grad_total.reshape(grad_acc.shape),
        emitted.reshape((1, TICKS) + fwd_queue.shape[2:]),
    )


def solution(mesh):
    return jax.shard_map(
        per_device,
        mesh=mesh,
        in_specs=(
            P("section", None, "row", None, None),
            P("section", None, "row", None, None),
            P("section", None, "row", None, None),
            P("section", None, None, "row", None, None),
            P("section", None, None, None, "row", None),
            P("section", None, None, None, "row", None),
            P(),
            P(),
        ),
        out_specs=(
            P("section", None, "row", None, None),
            P("section", None, "row", None, None),
            P("section", None, "row", None, None),
            P("section", None, None, "row", None, None),
            P("section", None, None, None, "row", None),
            P("section", None, "row", None, None),
        ),
        check_vma=False,
    )
```

profile of v0, /device:TPU:0, one launch (start us, length us, event | category | flops | bytes accessed | tf_op | source)
XLA Modules:
  0.0 64.7 jit_solution(7226169317741070860)
XLA Ops:
  0.6 1.7 %pack_first.1 = (bf16[32,640]{1,0:T(8,128)(2,1)S(1)}, bf16[32,640]{1,0:T(8,128)(2,1)S(1)}, bf16[3,128,320]{2,1,0:T(8,128)(2,1)S(1)}, bf16[3,128,320]{2,1,0:T(8,1...) custom-call(s32[2,16]{1,0:T(2,128)} %bitcast.24, s32[2,16]{1,0:T(2,128)} %bitcast.32, ...), custom_call_target="tpu_custom_call" | custom-call | flops 1 | bytes 1 | tf_op jit(solution)/shard_map/pack_first/pallas_call | solution.py:189
  2.4 3.0 %collective-permute-start = (bf16[32,640]{1,0:T(8,128)(2,1)S(1)}, bf16[32,640]{1,0:T(8,128)(2,1)S(1)}, u32[]{:S(2)}, u32[]{:S(2)}) collective-permute-start(bf16[32,640]{1,0:T(8,128)(2,1)S(1)} %get-tuple-element.84), channel_id=1, source_target_pairs={{0,1},{1,0},{2,3},{3,2},{4,5},{5,4},{6,7},{7,6},{8,9},{9,8},{10,11... | collective-permute-start | bytes 122888 | tf_op jit(solution)/shard_map/ppermute | solution.py:671
  5.4 1.2 %pack_later.1 = (bf16[128,640]{1,0:T(8,128)(2,1)S(1)}, bf16[128,640]{1,0:T(8,128)(2,1)S(1)}, bf16[64,640]{1,0:T(8,128)(2,1)S(1)}, bf16[64,640]{1,0:T(8,128)(2,1)...) custom-call(s32[2,16]{1,0:T(2,128)} %bitcast.25, ...), custom_call_target="tpu_custom_call" | custom-call | flops 1 | bytes 1 | tf_op jit(solution)/shard_map/pack_later/pallas_call | solution.py:189
  6.6 0.7 %collective-permute-done.refs_1_ = bf16[32,640]{1,0:T(8,128)(2,1)S(1)} collective-permute-done((bf16[32,640]{1,0:T(8,128)(2,1)S(1)}, bf16[32,640]{1,0:T(8,128)(2,1)S(1)}, u32[]{:S(2)}, u32[]{:S(2)}) %collective-permute-start) | collective-permute-done | bytes 40992 | tf_op jit(solution)/shard_map/ppermute | solution.py:671
  7.4 2.0 %collective-permute-start.1 = (bf16[128,640]{1,0:T(8,128)(2,1)S(1)}, bf16[128,640]{1,0:T(8,128)(2,1)S(1)}, u32[]{:S(2)}, u32[]{:S(2)}) collective-permute-start(bf16[128,640]{1,0:T(8,128)(2,1)S(1)} %get-tuple-element.86), channel_id=1, source_target_pairs={{0,1},{1,0},{2,3},{3,2},{4,5},{5,4},{6,7},{7,6},{8,9},{9,8},{10,11... | collective-permute-start | bytes 491528 | tf_op jit(solution)/shard_map/ppermute | solution.py:671
  9.4 1.4 %first_forward.1 = (f32[256,160]{1,0:T(8,128)S(1)}, bf16[256,160]{1,0:T(8,128)(2,1)S(1)}, bf16[128,640]{1,0:T(8,128)(2,1)S(1)}) custom-call(bf16[32,640]{1,0:T(8,128)(2,1)S(1)} %get-tuple-element.81.refs_6_.refs_0_, bf16[32,640]{1,0:T(8,128)(2,1)S(1)} %collective-permute-done.refs_1_, bf16[64,640]{1,0:T(8,128)(2,1)S(1)} %get-tuple-element.89.refs_2_.refs_3_.refs_5_, ...), custom_call_target="tpu_custom_call" | custom-call | flops 1 | bytes 1 | tf_op jit(solution)/shard_map/first_forward/pallas_call | solution.py:189
  10.8 0.1 collective-permute-start.3
  10.9 2.6 %collective-permute-done.1.refs_1_.refs_4_ = bf16[128,640]{1,0:T(8,128)(2,1)S(1)} collective-permute-done((bf16[128,640]{1,0:T(8,128)(2,1)S(1)}, bf16[128,640]{1,0:T(8,128)(2,1)S(1)}, u32[]{:S(2)}, u32[]{:S(2)}) %collective-permute-start.1) | collective-permute-done | bytes 163872 | tf_op jit(solution)/shard_map/ppermute | solution.py:671
  13.5 1.4 %first_backward.1 = (bf16[256,160]{1,0:T(8,128)(2,1)S(1)}, bf16[64,640]{1,0:T(8,128)(2,1)S(1)}, bf16[3,320,320]{2,1,0:T(8,128)(2,1)S(1)}, bf16[256,160]{1,0:T(8,128)(2,1)S(1)}, bf16[128,640]{1,0:T(8,128)(2,1)S(1)}) custom-call(bf16[128,640]{1,0:T(8,128)(2,1)S(1)} %get-tuple-element.85.refs_0_.refs_3_, ...), custom_call_target="tpu_custom_call" | custom-call | flops 1 | bytes 1 | tf_op jit(solution)/shard_map/first_backward/pallas_call | solution.py:189
  14.9 2.5 %collective-permute-start.2 = (bf16[128,640]{1,0:T(8,128)(2,1)S(1)}, bf16[128,640]{1,0:T(8,128)(2,1)S(1)}, u32[]{:S(2)}, u32[]{:S(2)}) collective-permute-start(bf16[128,640]{1,0:T(8,128)(2,1)S(1)} %get-tuple-element.93), channel_id=1, source_target_pairs={{0,1},{1,0},{2,3},{3,2},{4,5},{5,4},{6,7},{7,6},{8,9},{9,8},{10,11... | collective-permute-start | bytes 491528 | tf_op jit(solution)/shard_map/ppermute | solution.py:671
  17.4 0.2 collective-permute-start.4
  17.6 0.6 kernel_grads_add_9.1.refs_6_.refs_0_
  18.2 0.0 collective-permute-done.3.refs_1_.refs_4_.refs_6_
  18.2 1.6 %second_forward.1 = (bf16[256,160]{1,0:T(8,128)(2,1)S(1)}, bf16[256,320]{1,0:T(8,128)(2,1)S(1)}, bf16[64,640]{1,0:T(8,128)(2,1)S(1)}, bf16[64,640]{1,0:T(8,128)(2,1)S(1)}) custom-call(f32[256,160]{1,0:T(8,128)S(1)} %get-tuple-element.91.refs_5_.refs_0_, bf16[128,640]{1,0:T(8,128)(2,1)S(1)} %collective-permute-done.3.refs_1_.refs_4_.refs_6_, ...), custom_call_target="tpu_custom_call" | custom-call | flops 1 | bytes 1 | tf_op jit(solution)/shard_map/second_forward/pallas_call | solution.py:189
  19.9 0.0 copy-start.2
  19.9 4.5 %collective-permute-start.8 = (bf16[64,640]{1,0:T(8,128)(2,1)S(1)}, bf16[64,640]{1,0:T(8,128)(2,1)S(1)}, u32[]{:S(2)}, u32[]{:S(2)}) collective-permute-start(bf16[64,640]{1,0:T(8,128)(2,1)S(1)} %get-tuple-element.104), channel_id=1, source_target_pairs={{0,2},{1,3},{2,4},{3,5},{4,6},{5,7},{6,8},{7,9},{8,10},{9,11},{10,... | collective-permute-start | bytes 245768 | tf_op jit(solution)/shard_map/ppermute | solution.py:671
  24.4 0.3 collective-permute-start.9
  24.7 0.0 collective-permute-done.2.refs_1_.refs_4_.refs_8_
  24.7 1.6 %second_backward.1 = (bf16[64,640]{1,0:T(8,128)(2,1)S(1)}, bf16[3,320,320]{2,1,0:T(8,128)(2,1)S(1)}, bf16[256,160]{1,0:T(8,128)(2,1)S(1)}, bf16[128,640]{1,0:T(8,128)(2,1)S(1)}) custom-call(bf16[256,160]{1,0:T(8,128)(2,1)S(1)} %get-tuple-element.92.refs_3_.refs_0_, bf16[128,640]{1,0:T(8,128)(2,1)S(1)} %collective-permute-done.2.refs_1_.refs_4_.refs_8_, ...), custom_call_target="tpu_custom_call" | custom-call | flops 1 | bytes 1 | tf_op jit(solution)/shard_map/second_backward/pallas_call | solution.py:189
  26.3 1.4 %collective-permute-start.7 = (bf16[128,640]{1,0:T(8,128)(2,1)S(1)}, bf16[128,640]{1,0:T(8,128)(2,1)S(1)}, u32[]{:S(2)}, u32[]{:S(2)}) collective-permute-start(bf16[128,640]{1,0:T(8,128)(2,1)S(1)} %get-tuple-element.103), channel_id=1, source_target_pairs={{0,1},{1,0},{2,3},{3,2},{4,5},{5,4},{6,7},{7,6},{8,9},{9,8},{10,11... | collective-permute-start | bytes 491528 | tf_op jit(solution)/shard_map/ppermute | solution.py:671
  27.8 4.0 %collective-permute-start.6 = (bf16[64,640]{1,0:T(8,128)(2,1)S(1)}, bf16[64,640]{1,0:T(8,128)(2,1)S(1)}, u32[]{:S(2)}, u32[]{:S(2)}) collective-permute-start(bf16[64,640]{1,0:T(8,128)(2,1)S(1)} %get-tuple-element.102.refs_8_), channel_id=1, source_target_pairs={{0,31},{1,30},{2,1},{3,0},{4,3},{5,2},{6,5},{7,4},{8,7},{9,6},{10,... | collective-permute-start | bytes 245768 | tf_op jit(solution)/shard_map/ppermute | solution.py:671
  31.8 0.3 collective-permute-start.5
  32.1 2.1 %later_forward.1 = (f32[256,160]{1,0:T(8,128)S(1)}, bf16[256,160]{1,0:T(8,128)(2,1)S(1)}, bf16[256,160]{1,0:T(8,128)(2,1)S(1)}, bf16[64,640]{1,0:T(8,128)(2,1)S(1)}, bf16[96,640]{1,0:T(8,128)(2,1)S(1)}) custom-call(s32[2,16]{1,0:T(2,128)S(1)} %bitcast.26, bf16[64,640]{1,0:T(8,128)(2,1)S(1)} %collective-permute-done.8.refs_1_, ...), custom_call_target="tpu_custom_call" | custom-call | flops 1 | bytes 1 | tf_op jit(solution)/shard_map/later_forward/pallas_call | solution.py:189
  34.2 1.2 %collective-permute-start.12 = (bf16[96,640]{1,0:T(8,128)(2,1)S(1)}, bf16[96,640]{1,0:T(8,128)(2,1)S(1)}, u32[]{:S(2)}, u32[]{:S(2)}) collective-permute-start(bf16[96,640]{1,0:T(8,128)(2,1)S(1)} %get-tuple-element.120), channel_id=1, source_target_pairs={{0,1},{1,0},{2,3},{3,2},{4,5},{5,4},{6,7},{7,6},{8,9},{9,8},{10,11... | collective-permute-start | bytes 368648 | tf_op jit(solution)/shard_map/ppermute | solution.py:671
  35.3 0.8 %collective-permute-start.11 = (bf16[64,640]{1,0:T(8,128)(2,1)S(1)}, bf16[64,640]{1,0:T(8,128)(2,1)S(1)}, u32[]{:S(2)}, u32[]{:S(2)}) collective-permute-start(bf16[64,640]{1,0:T(8,128)(2,1)S(1)} %get-tuple-element.117), channel_id=1, source_target_pairs={{0,0},{1,1},{2,30},{3,31},{4,28},{5,29},{6,26},{7,27},{8,24},{9,25... | collective-permute-start | bytes 245768 | tf_op jit(solution)/shard_map/ppermute | solution.py:671
  36.2 0.0 copy-start.3
  36.2 0.6 kernel_grads_add_0.2.refs_12_.refs_0_
  36.8 0.0 collective-permute-done.6.refs_3_
  36.8 0.0 collective-permute-done.7.refs_5_
  36.8 0.0 copy-done.3
  36.9 2.3 %later_backward.1 = (bf16[256,160]{1,0:T(8,128)(2,1)S(1)}, bf16[3,320,320]{2,1,0:T(8,128)(2,1)S(1)}, bf16[256,160]{1,0:T(8,128)(2,1)S(1)}, bf16[256,320]{1,0:T(8...) custom-call(s32[2,16]{1,0:T(2,128)S(1)} %bitcast.27, ...), custom_call_target="tpu_custom_call" | custom-call | flops 1 | bytes 1 | tf_op jit(solution)/shard_map/later_backward/pallas_call | solution.py:189
  39.2 1.0 %collective-permute-start.10 = (bf16[128,640]{1,0:T(8,128)(2,1)S(1)}, bf16[128,640]{1,0:T(8,128)(2,1)S(1)}, u32[]{:S(2)}, u32[]{:S(2)}) collective-permute-start(bf16[128,640]{1,0:T(8,128)(2,1)S(1)} %get-tuple-element.115), channel_id=1, source_target_pairs={{0,1},{1,0},{2,3},{3,2},{4,5},{5,4},{6,7},{7,6},{8,9},{9,8},{10,11... | collective-permute-start | bytes 491528 | tf_op jit(solution)/shard_map/ppermute | solution.py:671
  40.2 0.0 collective-permute-done.11.refs_5_.refs_1_
  40.2 2.0 %last_forward.1 = (bf16[128,480]{1,0:T(8,128)(2,1)S(1)}, bf16[128,480]{1,0:T(8,128)(2,1)S(1)}) custom-call(s32[2,16]{1,0:T(2,128)S(1)} %bitcast.28, f32[256,160]{1,0:T(8,128)S(1)} %get-tuple-element.111.refs_3_.refs_1_, bf16[96,640]{1,0:T(8,128)(2,1)S(1)} %collective-permute-done.12.refs_2_, bf16[256,160]{1,0:T(8,128)(2,1)S(1)} %get-tuple-element.121.refs_3_, ...), custom_call_target="tpu_custom_call" | custom-call | flops 1 | bytes 1 | tf_op jit(solution)/shard_map/last_forward/pallas_call | solution.py:189
  42.2 1.2 %collective-permute-start.13 = (bf16[128,480]{1,0:T(8,128)(2,1)S(1)}, bf16[128,480]{1,0:T(8,128)(2,1)S(1)}, u32[]{:S(2)}, u32[]{:S(2)}) collective-permute-start(bf16[128,480]{1,0:T(8,128)(2,1)S(1)} %get-tuple-element.129), channel_id=1, source_target_pairs={{0,1},{1,0},{2,3},{3,2},{4,5},{5,4},{6,7},{7,6},{8,9},{9,8},{10,11... | collective-permute-start | bytes 368648 | tf_op jit(solution)/shard_map/ppermute | solution.py:671
  43.4 0.6 kernel_grads_add_0.3.refs_2_.refs_1_
  44.0 0.2 pack_rows.1
  44.2 1.6 %collective-permute-done.10.refs_9_.refs_3_ = bf16[128,640]{1,0:T(8,128)(2,1)S(1)} collective-permute-done((bf16[128,640]{1,0:T(8,128)(2,1)S(1)}, bf16[128,640]{1,0:T(8,128)(2,1)S(1)}, u32[]{:S(2)}, u32[]{:S(2)}) %collective-permute-start.10) | collective-permute-done | bytes 163872 | tf_op jit(solution)/shard_map/ppermute | solution.py:671
  45.9 1.8 %write_queues.1 = (f32[8,128]{1,0:T(8,128)S(1)}, bf16[3,128,320]{2,1,0:T(8,128)(2,1)}, bf16[3,128,320]{2,1,0:T(8,128)(2,1)}, bf16[3,128,320]{2,1,0:T(8,128)(2,1)}, bf16[6,128,320]{2,1,0:T(8,128)(2,1)}) custom-call(s32[2,16]{1,0:T(2,128)S(1)} %bitcast.29, s32[2,16]{1,0:T(2,128)S(1)} %bitcast.35, bf16[3,128,320]{2,1,0:T(8,128)(2,1)S(1)} %get-tuple-element.77.refs_2_, ...), custom_call_target="tpu_custom_call" | custom-call | flops 1 | bytes 1 | tf_op jit(solution)/shard_map/write_queues/pallas_call | solution.py:189
  47.8 1.2 %collective-permute-start.16 = (bf16[128,480]{1,0:T(8,128)(2,1)S(1)}, bf16[128,480]{1,0:T(8,128)(2,1)S(1)}, u32[]{:S(2)}, u32[]{:S(2)}) collective-permute-start(bf16[128,480]{1,0:T(8,128)(2,1)S(1)} %get-tuple-element.136), channel_id=1, source_target_pairs={{0,1},{1,0},{2,3},{3,2},{4,5},{5,4},{6,7},{7,6},{8,9},{9,8},{10,11... | collective-permute-start | bytes 368648 | tf_op jit(solution)/shard_map/ppermute | solution.py:671
  48.9 0.2 add_rows.1
  49.2 3.7 %collective-permute-start.15 = (bf16[128,320]{1,0:T(8,128)(2,1)S(1)}, bf16[128,320]{1,0:T(8,128)(2,1)S(1)}, u32[]{:S(2)}, u32[]{:S(2)}) collective-permute-start(bf16[128,320]{1,0:T(8,128)(2,1)S(1)} %get-tuple-element.133), channel_id=1, source_target_pairs={{0,30},{1,31},{2,28},{3,29},{4,26},{5,27},{6,24},{7,25},{8,22},{9,... | collective-permute-start | bytes 245768 | tf_op jit(solution)/shard_map/ppermute | solution.py:671
  52.8 2.3 %last_backward.1 = (bf16[32,640]{1,0:T(8,128)(2,1)S(1)}, bf16[32,640]{1,0:T(8,128)(2,1)S(1)}, bf16[3,320,320]{2,1,0:T(8,128)(2,1)S(1)}, bf16[256,160]{1,0:T(8,128)(2,1)S(1)}) custom-call(s32[2,16]{1,0:T(2,128)S(1)} %bitcast.30, s32[2,16]{1,0:T(2,128)S(1)} %bitcast.36, bf16[256,160]{1,0:T(8,128)(2,1)S(1)} %get-tuple-element.122.refs_7_.refs_2_, ...), custom_call_target="tpu_custom_call" | custom-call | flops 1 | bytes 1 | tf_op jit(solution)/shard_map/last_backward/pallas_call | solution.py:189
  55.1 4.5 %collective-permute-start.17 = (bf16[32,640]{1,0:T(8,128)(2,1)S(1)}, bf16[32,640]{1,0:T(8,128)(2,1)S(1)}, u32[]{:S(2)}, u32[]{:S(2)}) collective-permute-start(bf16[32,640]{1,0:T(8,128)(2,1)S(1)} %get-tuple-element.137), channel_id=1, source_target_pairs={{0,30},{1,31},{2,0},{3,1},{4,2},{5,3},{6,4},{7,5},{8,6},{9,7},{10,... | collective-permute-start | bytes 122888 | tf_op jit(solution)/shard_map/ppermute | solution.py:671
  59.6 0.4 collective-permute-start.18
  60.1 2.2 %kernel_grads_last.1 = (f32[8,128]{1,0:T(8,128)S(1)}, f32[18,160,320]{2,1,0:T(8,128)}) custom-call(f32[9,160,320]{2,1,0:T(8,128)S(1)} %kernel_grads_add_0.2.refs_12_.refs_0_, f32[9,160,320]{2,1,0:T(8,128)S(1)} %kernel_grads_add_0.3.refs_2_.refs_1_, bf16[256,160]{1,0:T(8,128)(2,1)S(1)} %get-tuple-element.139.refs_2_, ...), custom_call_target="tpu_custom_call" | custom-call | flops 1 | bytes 1 | tf_op jit(solution)/shard_map/kernel_grads_last/pallas_call | solution.py:189
  62.2 0.8 %collective-permute-done.18.refs_13_ = bf16[32,640]{1,0:T(8,128)(2,1)S(1)} collective-permute-done((bf16[32,640]{1,0:T(8,128)(2,1)S(1)}, bf16[32,640]{1,0:T(8,128)(2,1)S(1)}, u32[]{:S(2)}, u32[]{:S(2)}) %collective-permute-start.18) | collective-permute-done | bytes 40992 | tf_op jit(solution)/shard_map/ppermute | solution.py:671
  63.0 1.5 %finish.1 = (bf16[3,128,320]{2,1,0:T(8,128)(2,1)}, bf16[3,128,320]{2,1,0:T(8,128)(2,1)}, bf16[3,128,320]{2,1,0:T(8,128)(2,1)}, bf16[6,128,320]{2,1,0:T(8,128)(2,1)}, bf16[2,128,320]{2,1,0:T(8,128)(2,1)}) custom-call(s32[2,16]{1,0:T(2,128)S(1)} %bitcast.31, ...), custom_call_target="tpu_custom_call", output_to_operand_aliasing={{0}: (2, {}), {1}: (3, {}), {2}: (4, {}), {3}: (5, {})} | custom-call | flops 1 | bytes 1 | tf_op jit(solution)/shard_map/finish/pallas_call | solution.py:189
  (16 shorter events, 0.0 us)
Async XLA Ops:
  0.6 8.8 %copy-start = (bf16[1,2,3,3,160,320]{5,4,3,2,1,0:T(8,128)(2,1)S(1)}, bf16[1,2,3,3,160,320]{5,4,3,2,1,0:T(8,128)(2,1)}, u32[]{:S(2)}) copy-start(bf16[1,2,3,3,160,320]{5,4,3,2,1,0:T(8,128)(2,1)} %param.12) | copy-start | bytes 5529604
  2.4 5.0 %collective-permute-start = (bf16[32,640]{1,0:T(8,128)(2,1)S(1)}, bf16[32,640]{1,0:T(8,128)(2,1)S(1)}, u32[]{:S(2)}, u32[]{:S(2)}) collective-permute-start(bf16[32,640]{1,0:T(8,128)(2,1)S(1)} %get-tuple-element.84), channel_id=1, source_target_pairs={{0,1},{1,0},{2,3},{3,2},{4,5},{5,4},{6,7},{7,6},{8,9},{9,8},{10,11... | collective-permute-start | bytes 122888 | tf_op jit(solution)/shard_map/ppermute | solution.py:671
  7.4 6.1 %collective-permute-start.1 = (bf16[128,640]{1,0:T(8,128)(2,1)S(1)}, bf16[128,640]{1,0:T(8,128)(2,1)S(1)}, u32[]{:S(2)}, u32[]{:S(2)}) collective-permute-start(bf16[128,640]{1,0:T(8,128)(2,1)S(1)} %get-tuple-element.86), channel_id=1, source_target_pairs={{0,1},{1,0},{2,3},{3,2},{4,5},{5,4},{6,7},{7,6},{8,9},{9,8},{10,11... | collective-permute-start | bytes 491528 | tf_op jit(solution)/shard_map/ppermute | solution.py:671
  9.4 8.2 %copy-start.1 = (f32[1,2,3,3,160,320]{5,4,3,2,1,0:T(8,128)S(1)}, f32[1,2,3,3,160,320]{5,4,3,2,1,0:T(8,128)}, u32[]{:S(2)}) copy-start(f32[1,2,3,3,160,320]{5,4,3,2,1,0:T(8,128)} %param.13) | copy-start | bytes 11059204
  10.8 7.4 %collective-permute-start.3 = (bf16[128,640]{1,0:T(8,128)(2,1)S(1)}, bf16[128,640]{1,0:T(8,128)(2,1)S(1)}, u32[]{:S(2)}, u32[]{:S(2)}) collective-permute-start(bf16[128,640]{1,0:T(8,128)(2,1)S(1)} %get-tuple-element.95), channel_id=1, source_target_pairs={{0,1},{1,0},{2,3},{3,2},{4,5},{5,4},{6,7},{7,6},{8,9},{9,8},{10,11... | collective-permute-start | bytes 491528 | tf_op jit(solution)/shard_map/ppermute | solution.py:671
  14.9 9.8 %collective-permute-start.2 = (bf16[128,640]{1,0:T(8,128)(2,1)S(1)}, bf16[128,640]{1,0:T(8,128)(2,1)S(1)}, u32[]{:S(2)}, u32[]{:S(2)}) collective-permute-start(bf16[128,640]{1,0:T(8,128)(2,1)S(1)} %get-tuple-element.93), channel_id=1, source_target_pairs={{0,1},{1,0},{2,3},{3,2},{4,5},{5,4},{6,7},{7,6},{8,9},{9,8},{10,11... | collective-permute-start | bytes 491528 | tf_op jit(solution)/shard_map/ppermute | solution.py:671
  17.4 7.3 %collective-permute-start.4 = (bf16[64,640]{1,0:T(8,128)(2,1)S(1)}, bf16[64,640]{1,0:T(8,128)(2,1)S(1)}, u32[]{:S(2)}, u32[]{:S(2)}) collective-permute-start(bf16[64,640]{1,0:T(8,128)(2,1)S(1)} %get-tuple-element.96), channel_id=1, source_target_pairs={{0,30},{1,31},{2,28},{3,29},{4,26},{5,27},{6,24},{7,25},{8,22},{9,... | collective-permute-start | bytes 245768 | tf_op jit(solution)/shard_map/ppermute | solution.py:671
  19.9 12.2 %copy-start.2 = (s32[16,2]{0,1:T(2,128)S(1)}, s32[16,2]{0,1:T(2,128)}, u32[]{:S(2)}) copy-start(s32[16,2]{0,1:T(2,128)} %param.14) | copy-start | bytes 388
  19.9 12.2 %collective-permute-start.8 = (bf16[64,640]{1,0:T(8,128)(2,1)S(1)}, bf16[64,640]{1,0:T(8,128)(2,1)S(1)}, u32[]{:S(2)}, u32[]{:S(2)}) collective-permute-start(bf16[64,640]{1,0:T(8,128)(2,1)S(1)} %get-tuple-element.104), channel_id=1, source_target_pairs={{0,2},{1,3},{2,4},{3,5},{4,6},{5,7},{6,8},{7,9},{8,10},{9,11},{10,... | collective-permute-start | bytes 245768 | tf_op jit(solution)/shard_map/ppermute | solution.py:671
  24.4 7.7 %collective-permute-start.9 = (bf16[64,640]{1,0:T(8,128)(2,1)S(1)}, bf16[64,640]{1,0:T(8,128)(2,1)S(1)}, u32[]{:S(2)}, u32[]{:S(2)}) collective-permute-start(bf16[64,640]{1,0:T(8,128)(2,1)S(1)} %get-tuple-element.105), channel_id=1, source_target_pairs={{0,3},{1,2},{2,5},{3,4},{4,7},{5,6},{6,9},{7,8},{8,11},{9,10},{10,... | collective-permute-start | bytes 245768 | tf_op jit(solution)/shard_map/ppermute | solution.py:671
  26.3 10.5 %collective-permute-start.7 = (bf16[128,640]{1,0:T(8,128)(2,1)S(1)}, bf16[128,640]{1,0:T(8,128)(2,1)S(1)}, u32[]{:S(2)}, u32[]{:S(2)}) collective-permute-start(bf16[128,640]{1,0:T(8,128)(2,1)S(1)} %get-tuple-element.103), channel_id=1, source_target_pairs={{0,1},{1,0},{2,3},{3,2},{4,5},{5,4},{6,7},{7,6},{8,9},{9,8},{10,11... | collective-permute-start | bytes 491528 | tf_op jit(solution)/shard_map/ppermute | solution.py:671
  27.8 9.0 %collective-permute-start.6 = (bf16[64,640]{1,0:T(8,128)(2,1)S(1)}, bf16[64,640]{1,0:T(8,128)(2,1)S(1)}, u32[]{:S(2)}, u32[]{:S(2)}) collective-permute-start(bf16[64,640]{1,0:T(8,128)(2,1)S(1)} %get-tuple-element.102.refs_8_), channel_id=1, source_target_pairs={{0,31},{1,30},{2,1},{3,0},{4,3},{5,2},{6,5},{7,4},{8,7},{9,6},{10,... | collective-permute-start | bytes 245768 | tf_op jit(solution)/shard_map/ppermute | solution.py:671
  31.8 5.0 %collective-permute-start.5 = (bf16[64,640]{1,0:T(8,128)(2,1)S(1)}, bf16[64,640]{1,0:T(8,128)(2,1)S(1)}, u32[]{:S(2)}, u32[]{:S(2)}) collective-permute-start(bf16[64,640]{1,0:T(8,128)(2,1)S(1)} %get-tuple-element.102.refs_8_), channel_id=1, source_target_pairs={{0,30},{1,31},{2,0},{3,1},{4,2},{5,3},{6,4},{7,5},{8,6},{9,7},{10,... | collective-permute-start | bytes 245768 | tf_op jit(solution)/shard_map/ppermute | solution.py:671
  34.2 6.0 %collective-permute-start.12 = (bf16[96,640]{1,0:T(8,128)(2,1)S(1)}, bf16[96,640]{1,0:T(8,128)(2,1)S(1)}, u32[]{:S(2)}, u32[]{:S(2)}) collective-permute-start(bf16[96,640]{1,0:T(8,128)(2,1)S(1)} %get-tuple-element.120), channel_id=1, source_target_pairs={{0,1},{1,0},{2,3},{3,2},{4,5},{5,4},{6,7},{7,6},{8,9},{9,8},{10,11... | collective-permute-start | bytes 368648 | tf_op jit(solution)/shard_map/ppermute | solution.py:671
  35.3 4.8 %collective-permute-start.11 = (bf16[64,640]{1,0:T(8,128)(2,1)S(1)}, bf16[64,640]{1,0:T(8,128)(2,1)S(1)}, u32[]{:S(2)}, u32[]{:S(2)}) collective-permute-start(bf16[64,640]{1,0:T(8,128)(2,1)S(1)} %get-tuple-element.117), channel_id=1, source_target_pairs={{0,0},{1,1},{2,30},{3,31},{4,28},{5,29},{6,26},{7,27},{8,24},{9,25... | collective-permute-start | bytes 245768 | tf_op jit(solution)/shard_map/ppermute | solution.py:671
  36.2 0.7 %copy-start.3 = (s32[16,2]{0,1:T(2,128)S(1)}, s32[16,2]{0,1:T(2,128)}, u32[]{:S(2)}) copy-start(s32[16,2]{0,1:T(2,128)} %param.15) | copy-start | bytes 388
  39.2 6.7 %collective-permute-start.10 = (bf16[128,640]{1,0:T(8,128)(2,1)S(1)}, bf16[128,640]{1,0:T(8,128)(2,1)S(1)}, u32[]{:S(2)}, u32[]{:S(2)}) collective-permute-start(bf16[128,640]{1,0:T(8,128)(2,1)S(1)} %get-tuple-element.115), channel_id=1, source_target_pairs={{0,1},{1,0},{2,3},{3,2},{4,5},{5,4},{6,7},{7,6},{8,9},{9,8},{10,11... | collective-permute-start | bytes 491528 | tf_op jit(solution)/shard_map/ppermute | solution.py:671
  42.2 5.5 %collective-permute-start.13 = (bf16[128,480]{1,0:T(8,128)(2,1)S(1)}, bf16[128,480]{1,0:T(8,128)(2,1)S(1)}, u32[]{:S(2)}, u32[]{:S(2)}) collective-permute-start(bf16[128,480]{1,0:T(8,128)(2,1)S(1)} %get-tuple-element.129), channel_id=1, source_target_pairs={{0,1},{1,0},{2,3},{3,2},{4,5},{5,4},{6,7},{7,6},{8,9},{9,8},{10,11... | collective-permute-start | bytes 368648 | tf_op jit(solution)/shard_map/ppermute | solution.py:671
  47.8 15.3 %collective-permute-start.16 = (bf16[128,480]{1,0:T(8,128)(2,1)S(1)}, bf16[128,480]{1,0:T(8,128)(2,1)S(1)}, u32[]{:S(2)}, u32[]{:S(2)}) collective-permute-start(bf16[128,480]{1,0:T(8,128)(2,1)S(1)} %get-tuple-element.136), channel_id=1, source_target_pairs={{0,1},{1,0},{2,3},{3,2},{4,5},{5,4},{6,7},{7,6},{8,9},{9,8},{10,11... | collective-permute-start | bytes 368648 | tf_op jit(solution)/shard_map/ppermute | solution.py:671
  49.2 13.9 %collective-permute-start.15 = (bf16[128,320]{1,0:T(8,128)(2,1)S(1)}, bf16[128,320]{1,0:T(8,128)(2,1)S(1)}, u32[]{:S(2)}, u32[]{:S(2)}) collective-permute-start(bf16[128,320]{1,0:T(8,128)(2,1)S(1)} %get-tuple-element.133), channel_id=1, source_target_pairs={{0,30},{1,31},{2,28},{3,29},{4,26},{5,27},{6,24},{7,25},{8,22},{9,... | collective-permute-start | bytes 245768 | tf_op jit(solution)/shard_map/ppermute | solution.py:671
  52.8 10.2 %collective-permute-start.14 = (bf16[128,320]{1,0:T(8,128)(2,1)S(1)}, bf16[128,320]{1,0:T(8,128)(2,1)S(1)}, u32[]{:S(2)}, u32[]{:S(2)}) collective-permute-start(bf16[128,320]{1,0:T(8,128)(2,1)S(1)} %get-tuple-element.131.refs_9_.refs_6_), channel_id=1, source_target_pairs={{0,2},{1,3},{2,4},{3,5},{4,6},{5,7},{6,8},{7,9},{8,10},{9,11},{10,... | collective-permute-start | bytes 245768 | tf_op jit(solution)/shard_map/ppermute | solution.py:671
  55.1 7.1 %collective-permute-start.17 = (bf16[32,640]{1,0:T(8,128)(2,1)S(1)}, bf16[32,640]{1,0:T(8,128)(2,1)S(1)}, u32[]{:S(2)}, u32[]{:S(2)}) collective-permute-start(bf16[32,640]{1,0:T(8,128)(2,1)S(1)} %get-tuple-element.137), channel_id=1, source_target_pairs={{0,30},{1,31},{2,0},{3,1},{4,2},{5,3},{6,4},{7,5},{8,6},{9,7},{10,... | collective-permute-start | bytes 122888 | tf_op jit(solution)/shard_map/ppermute | solution.py:671
  59.6 3.4 %collective-permute-start.18 = (bf16[32,640]{1,0:T(8,128)(2,1)S(1)}, bf16[32,640]{1,0:T(8,128)(2,1)S(1)}, u32[]{:S(2)}, u32[]{:S(2)}) collective-permute-start(bf16[32,640]{1,0:T(8,128)(2,1)S(1)} %get-tuple-element.138), channel_id=1, source_target_pairs={{0,31},{1,30},{2,1},{3,0},{4,3},{5,2},{6,5},{7,4},{8,7},{9,6},{10,... | collective-permute-start | bytes 122888 | tf_op jit(solution)/shard_map/ppermute | solution.py:671
where the time goes:
time: 64.9 us; the launch traced here: 64.7 us
  starting transfers between devices  32.4 us (50%)
  Pallas kernels  25.5 us (39%)
  waiting for transfers between devices  5.78 us (9%)
  between operations  1.01 us (2%)
    ppermute x19, starting transfers between devices, move(): return lax.ppermute(x, ('section', 'row'), route)  32.4 us
    pallas_call x18, Pallas kernels, call(): pl.pallas_call(inner, name=name, out_shape=[jax.ShapeDtypeStruct(shape, d...  25.5 us
    ppermute x19, waiting for transfers between devices, move(): return lax.ppermute(x, ('section', 'row'), route)  5.78 us
  transfers between devices with their start and end apart: 19, of which 4 were waited for; matrix products, arithmetic and copies ran while one was open for 0% of the time, Pallas kernels for 34%

commit v1 on v0

--- a/solution.py
+++ b/solution.py
@@ -140,37 +140,55 @@
     pad_ref[2, cols : cols + cells, :] = right.astype(BF)
 
 
+def spread_wide(z, x, line_ref, pad_ref):
+    cells, cols = z.cells, z.cols
+    line_ref[8 : 8 + cells, :] = x
+    column = lax.rem(lax.broadcasted_iota(jnp.int32, (cells, 1), 0), cols)
+    edge = jnp.zeros((cols, 3 * z.share), BF)
+    pad_ref[:cols, :] = edge
+    pad_ref[cols + cells :, :] = edge
+    left = jnp.where(column > 0, line_ref[7 : 7 + cells, :], 0.0)
+    right = jnp.where(column < cols - 1, line_ref[9 : 9 + cells, :], 0.0)
+    pad_ref[cols : cols + cells, :] = side_by_side([left, x, right]).astype(BF)
+
+
 def convolve(z, pad_ref, kernel_ref, which):
     total = None
     for a in range(3):
-        for b in range(3):
-            term = jnp.dot(
-                pad_ref[b, a * z.cols : a * z.cols + z.cells, :],
-                kernel_ref[9 * which + 3 * a + b],
-                preferred_element_type=F32,
-            )
-            total = term if total is None else total + term
+        first = (9 * which + 3 * a) * z.share
+        term = jnp.dot(
+            pad_ref[a * z.cols : a * z.cols + z.cells, :],
+            kernel_ref[first : first + 3 * z.share, :],
+            preferred_element_type=F32,
+        )
+        total = term if total is None else total + term
     return total
 
 
-def convolve_back(z, pad_ref, kernel_ref, which):
+def convolve_back(z, pad_ref, kernel_ref, which, line_ref):
+    cells, cols, w = z.cells, z.cols, z.share
     total = None
     for a in range(3):
-        for b in range(3):
-            term = lax.dot_general(
-                pad_ref[b, a * z.cols : a * z.cols + z.cells, :],
-                kernel_ref[9 * which + 3 * (2 - a) + 2 - b],
-                (((1,), (1,)), ((), ())),
-                preferred_element_type=F32,
-            )
-            total = term if total is None else total + term
-    return total
+        first = (9 * which + 3 * (2 - a)) * w
+        term = lax.dot_general(
+            pad_ref[1, a * cols : a * cols + cells, :],
+            kernel_ref[first : first + 3 * w, :],
+            (((1,), (1,)), ((), ())),
+            preferred_element_type=F32,
+        )
+        total = term if total is None else total + term
+    column = lax.rem(lax.broadcasted_iota(jnp.int32, (cells, 1), 0), cols)
+    line_ref[8 : 8 + cells, :w] = total[:, :w]
+    out = total[:, w : 2 * w]
+    out = out + jnp.where(column < cols - 1, line_ref[9 : 9 + cells, :w], 0.0)
+    line_ref[8 : 8 + cells, :w] = total[:, 2 * w :]
+    return out + jnp.where(column > 0, line_ref[7 : 7 + cells, :w], 0.0)
 
 
 def pad_shapes(z, width):
     return [
         pltpu.VMEM((z.cells + 16, width), F32),
-        pltpu.VMEM((3, z.cells + 2 * z.cols, width), BF),
+        pltpu.VMEM((z.cells + 2 * z.cols, 3 * width), BF),
     ]
 
 
@@ -289,7 +307,7 @@
     _, row = where_am_i()
     assemble(z, h_out, [unfold(z, piece) for piece in pieces], row, 0, z.share)
     y, _ = normalize(z, h_out[...].astype(F32))
-    spread(z, y * sigmoid(y), line, pad)
+    spread_wide(z, y * sigmoid(y), line, pad)
     send_partials(z, row, convolve(z, pad, kernel, 0), own, sends, extra)
 
 
@@ -319,7 +337,7 @@
     h = jnp.where(taken, total, h_out[...].astype(F32))
     h_out[...] = h.astype(BF)
     y, _ = normalize(z, h)
-    spread(z, y * sigmoid(y), line, pad)
+    spread_wide(z, y * sigmoid(y), line, pad)
     send_partials(z, row, convolve(z, pad, kernel, 0), own, sends, lasts)
 
 
@@ -328,7 +346,7 @@
     logistic = sigmoid(y)
     act_out[...] = (y * logistic).astype(BF)
     spread(z, g, line, pad)
-    q = norm_back(z, y, factor, logistic, convolve_back(z, pad, kernel, 1)).astype(BF)
+    q = norm_back(z, y, factor, logistic, convolve_back(z, pad, kernel, 1, line)).astype(BF)
     q_out[...] = q
     fold(z, q_send, q.astype(F32))
 
@@ -390,7 +408,7 @@
     i = jnp.where(encoder, c0, skip.astype(F32)).astype(BF)
     i_out[...] = i
     y, _ = normalize(z, i.astype(F32))
-    spread(z, y * sigmoid(y), line, pad)
+    spread_wide(z, y * sigmoid(y), line, pad)
     total = convolve(z, pad, kernel, 1)
     base = h[...].astype(F32) + jnp.where(encoder, 0.0, c0)
     full[...] = total + side_by_side([jnp.where(row == j, base, 0.0) for j in range(z.parts)])
@@ -449,7 +467,7 @@
     logistic = sigmoid(y)
     act_out[...] = (y * logistic).astype(BF)
     spread(z, now, line, pad)
-    back = norm_back(z, y, factor, logistic, convolve_back(z, pad, kernel, 0))
+    back = norm_back(z, y, factor, logistic, convolve_back(z, pad, kernel, 0, line))
     return share_of(z, g, row) + back, whole
 
 
@@ -653,7 +671,7 @@
     c, w, local, cells = z.channels, z.share, z.local, z.cells
     fwd, bwd, mir = (x.reshape(slots, local, c) for x in (fwd_queue, bwd_queue, mirror_queue))
     kept = stash.reshape(2 * slots, local, c)
-    kernels = weights.reshape(18, w, c)
+    kernels = weights.reshape(18 * w, c)
     acc = grad_acc.reshape(18, w, c)
     fs, bs = fwd_slot.T, bwd_slot.T
     fold_shape, wide = (cells // FOLD, FOLD * w), (cells, c)

time: 64.9 us -> 65.5 us (level)
  transfers between devices with their start and end apart: 19 -> 19, of which waited for: 4 -> 5; matrix products, arithmetic and copies ran while one was open for 0% -> 0% of each run, Pallas kernels for 34% -> 35%
where the time goes in v1:
time: 65.5 us; the launch traced here: 65.3 us
  starting transfers between devices  32.1 us (49%)
  Pallas kernels  26 us (40%)
  waiting for transfers between devices  6.14 us (9%)
  between operations  1 us (2%)
    ppermute x19, starting transfers between devices, move(): return lax.ppermute(x, ('section', 'row'), route)  32.1 us
    pallas_call x18, Pallas kernels, call(): pl.pallas_call(inner, name=name, out_shape=[jax.ShapeDtypeStruct(shape, d...  26 us
    ppermute x19, waiting for transfers between devices, move(): return lax.ppermute(x, ('section', 'row'), route)  6.14 us
  transfers between devices with their start and end apart: 19, of which 5 were waited for; matrix products, arithmetic and copies ran while one was open for 0% of the time, Pallas kernels for 35%

profile of v1, /device:TPU:0, one launch (start us, length us, event | category | flops | bytes accessed | tf_op | source)
XLA Modules:
  0.0 65.3 jit_solution(16069681476912378672)
XLA Ops:
  0.6 1.7 %pack_first.1 = (bf16[32,640]{1,0:T(8,128)(2,1)S(1)}, bf16[32,640]{1,0:T(8,128)(2,1)S(1)}, bf16[3,128,320]{2,1,0:T(8,128)(2,1)S(1)}, bf16[3,128,320]{2,1,0:T(8,1...) custom-call(s32[2,16]{1,0:T(2,128)} %bitcast.24, s32[2,16]{1,0:T(2,128)} %bitcast.32, ...), custom_call_target="tpu_custom_call" | custom-call | flops 1 | bytes 1 | tf_op jit(solution)/shard_map/pack_first/pallas_call | solution.py:207
  2.4 3.0 %collective-permute-start = (bf16[32,640]{1,0:T(8,128)(2,1)S(1)}, bf16[32,640]{1,0:T(8,128)(2,1)S(1)}, u32[]{:S(2)}, u32[]{:S(2)}) collective-permute-start(bf16[32,640]{1,0:T(8,128)(2,1)S(1)} %get-tuple-element.84), channel_id=1, source_target_pairs={{0,1},{1,0},{2,3},{3,2},{4,5},{5,4},{6,7},{7,6},{8,9},{9,8},{10,11... | collective-permute-start | bytes 122888 | tf_op jit(solution)/shard_map/ppermute | solution.py:689
  5.4 1.2 %pack_later.1 = (bf16[128,640]{1,0:T(8,128)(2,1)S(1)}, bf16[128,640]{1,0:T(8,128)(2,1)S(1)}, bf16[64,640]{1,0:T(8,128)(2,1)S(1)}, bf16[64,640]{1,0:T(8,128)(2,1)...) custom-call(s32[2,16]{1,0:T(2,128)} %bitcast.25, ...), custom_call_target="tpu_custom_call" | custom-call | flops 1 | bytes 1 | tf_op jit(solution)/shard_map/pack_later/pallas_call | solution.py:207
  6.6 0.7 %collective-permute-done.refs_1_ = bf16[32,640]{1,0:T(8,128)(2,1)S(1)} collective-permute-done((bf16[32,640]{1,0:T(8,128)(2,1)S(1)}, bf16[32,640]{1,0:T(8,128)(2,1)S(1)}, u32[]{:S(2)}, u32[]{:S(2)}) %collective-permute-start) | collective-permute-done | bytes 40992 | tf_op jit(solution)/shard_map/ppermute | solution.py:689
  7.4 2.0 %collective-permute-start.1 = (bf16[128,640]{1,0:T(8,128)(2,1)S(1)}, bf16[128,640]{1,0:T(8,128)(2,1)S(1)}, u32[]{:S(2)}, u32[]{:S(2)}) collective-permute-start(bf16[128,640]{1,0:T(8,128)(2,1)S(1)} %get-tuple-element.86), channel_id=1, source_target_pairs={{0,1},{1,0},{2,3},{3,2},{4,5},{5,4},{6,7},{7,6},{8,9},{9,8},{10,11... | collective-permute-start | bytes 491528 | tf_op jit(solution)/shard_map/ppermute | solution.py:689
  9.4 1.3 %first_forward.1 = (f32[256,160]{1,0:T(8,128)S(1)}, bf16[256,160]{1,0:T(8,128)(2,1)S(1)}, bf16[128,640]{1,0:T(8,128)(2,1)S(1)}) custom-call(bf16[32,640]{1,0:T(8,128)(2,1)S(1)} %get-tuple-element.81.refs_6_.refs_0_, bf16[32,640]{1,0:T(8,128)(2,1)S(1)} %collective-permute-done.refs_1_, bf16[64,640]{1,0:T(8,128)(2,1)S(1)} %get-tuple-element.89.refs_2_.refs_3_.refs_5_, ...), custom_call_target="tpu_custom_call" | custom-call | flops 1 | bytes 1 | tf_op jit(solution)/shard_map/first_forward/pallas_call | solution.py:207
  10.7 0.1 collective-permute-start.3
  10.8 2.9 %collective-permute-done.1.refs_1_.refs_4_ = bf16[128,640]{1,0:T(8,128)(2,1)S(1)} collective-permute-done((bf16[128,640]{1,0:T(8,128)(2,1)S(1)}, bf16[128,640]{1,0:T(8,128)(2,1)S(1)}, u32[]{:S(2)}, u32[]{:S(2)}) %collective-permute-start.1) | collective-permute-done | bytes 163872 | tf_op jit(solution)/shard_map/ppermute | solution.py:689
  13.7 1.8 %first_backward.1 = (bf16[256,160]{1,0:T(8,128)(2,1)S(1)}, bf16[64,640]{1,0:T(8,128)(2,1)S(1)}, bf16[3,320,320]{2,1,0:T(8,128)(2,1)S(1)}, bf16[256,160]{1,0:T(8,128)(2,1)S(1)}, bf16[128,640]{1,0:T(8,128)(2,1)S(1)}) custom-call(bf16[128,640]{1,0:T(8,128)(2,1)S(1)} %get-tuple-element.85.refs_0_.refs_3_, ...), custom_call_target="tpu_custom_call" | custom-call | flops 1 | bytes 1 | tf_op jit(solution)/shard_map/first_backward/pallas_call | solution.py:207
  15.4 2.3 %collective-permute-start.2 = (bf16[128,640]{1,0:T(8,128)(2,1)S(1)}, bf16[128,640]{1,0:T(8,128)(2,1)S(1)}, u32[]{:S(2)}, u32[]{:S(2)}) collective-permute-start(bf16[128,640]{1,0:T(8,128)(2,1)S(1)} %get-tuple-element.93), channel_id=1, source_target_pairs={{0,1},{1,0},{2,3},{3,2},{4,5},{5,4},{6,7},{7,6},{8,9},{9,8},{10,11... | collective-permute-start | bytes 491528 | tf_op jit(solution)/shard_map/ppermute | solution.py:689
  17.8 0.2 collective-permute-start.4
  17.9 0.6 kernel_grads_add_9.1.refs_6_.refs_0_
  18.6 0.0 collective-permute-done.3.refs_1_.refs_4_.refs_6_
  18.6 1.4 %second_forward.1 = (bf16[256,160]{1,0:T(8,128)(2,1)S(1)}, bf16[256,320]{1,0:T(8,128)(2,1)S(1)}, bf16[64,640]{1,0:T(8,128)(2,1)S(1)}, bf16[64,640]{1,0:T(8,128)(2,1)S(1)}) custom-call(f32[256,160]{1,0:T(8,128)S(1)} %get-tuple-element.91.refs_5_.refs_0_, bf16[128,640]{1,0:T(8,128)(2,1)S(1)} %collective-permute-done.3.refs_1_.refs_4_.refs_6_, ...), custom_call_target="tpu_custom_call" | custom-call | flops 1 | bytes 1 | tf_op jit(solution)/shard_map/second_forward/pallas_call | solution.py:207
  20.0 0.0 copy-start.2
  20.0 4.5 %collective-permute-start.8 = (bf16[64,640]{1,0:T(8,128)(2,1)S(1)}, bf16[64,640]{1,0:T(8,128)(2,1)S(1)}, u32[]{:S(2)}, u32[]{:S(2)}) collective-permute-start(bf16[64,640]{1,0:T(8,128)(2,1)S(1)} %get-tuple-element.104), channel_id=1, source_target_pairs={{0,2},{1,3},{2,4},{3,5},{4,6},{5,7},{6,8},{7,9},{8,10},{9,11},{10,... | collective-permute-start | bytes 245768 | tf_op jit(solution)/shard_map/ppermute | solution.py:689
  24.5 0.4 collective-permute-start.9
  24.9 0.1 collective-permute-done.4.refs_5_.refs_4_
  25.0 0.0 collective-permute-done.2.refs_1_.refs_4_.refs_8_
  25.0 1.9 %second_backward.1 = (bf16[64,640]{1,0:T(8,128)(2,1)S(1)}, bf16[3,320,320]{2,1,0:T(8,128)(2,1)S(1)}, bf16[256,160]{1,0:T(8,128)(2,1)S(1)}, bf16[128,640]{1,0:T(8,128)(2,1)S(1)}) custom-call(bf16[256,160]{1,0:T(8,128)(2,1)S(1)} %get-tuple-element.92.refs_3_.refs_0_, bf16[128,640]{1,0:T(8,128)(2,1)S(1)} %collective-permute-done.2.refs_1_.refs_4_.refs_8_, ...), custom_call_target="tpu_custom_call" | custom-call | flops 1 | bytes 1 | tf_op jit(solution)/shard_map/second_backward/pallas_call | solution.py:207
  26.9 1.3 %collective-permute-start.7 = (bf16[128,640]{1,0:T(8,128)(2,1)S(1)}, bf16[128,640]{1,0:T(8,128)(2,1)S(1)}, u32[]{:S(2)}, u32[]{:S(2)}) collective-permute-start(bf16[128,640]{1,0:T(8,128)(2,1)S(1)} %get-tuple-element.103), channel_id=1, source_target_pairs={{0,1},{1,0},{2,3},{3,2},{4,5},{5,4},{6,7},{7,6},{8,9},{9,8},{10,11... | collective-permute-start | bytes 491528 | tf_op jit(solution)/shard_map/ppermute | solution.py:689
  28.2 4.1 %collective-permute-start.6 = (bf16[64,640]{1,0:T(8,128)(2,1)S(1)}, bf16[64,640]{1,0:T(8,128)(2,1)S(1)}, u32[]{:S(2)}, u32[]{:S(2)}) collective-permute-start(bf16[64,640]{1,0:T(8,128)(2,1)S(1)} %get-tuple-element.102.refs_8_), channel_id=1, source_target_pairs={{0,31},{1,30},{2,1},{3,0},{4,3},{5,2},{6,5},{7,4},{8,7},{9,6},{10,... | collective-permute-start | bytes 245768 | tf_op jit(solution)/shard_map/ppermute | solution.py:689
  32.3 0.4 collective-permute-start.5
  32.7 0.0 collective-permute-done.8.refs_1_
  32.7 1.9 %later_forward.1 = (f32[256,160]{1,0:T(8,128)S(1)}, bf16[256,160]{1,0:T(8,128)(2,1)S(1)}, bf16[256,160]{1,0:T(8,128)(2,1)S(1)}, bf16[64,640]{1,0:T(8,128)(2,1)S(1)}, bf16[96,640]{1,0:T(8,128)(2,1)S(1)}) custom-call(s32[2,16]{1,0:T(2,128)S(1)} %bitcast.26, bf16[64,640]{1,0:T(8,128)(2,1)S(1)} %collective-permute-done.8.refs_1_, ...), custom_call_target="tpu_custom_call" | custom-call | flops 1 | bytes 1 | tf_op jit(solution)/shard_map/later_forward/pallas_call | solution.py:207
  34.6 1.0 %collective-permute-start.12 = (bf16[96,640]{1,0:T(8,128)(2,1)S(1)}, bf16[96,640]{1,0:T(8,128)(2,1)S(1)}, u32[]{:S(2)}, u32[]{:S(2)}) collective-permute-start(bf16[96,640]{1,0:T(8,128)(2,1)S(1)} %get-tuple-element.120), channel_id=1, source_target_pairs={{0,1},{1,0},{2,3},{3,2},{4,5},{5,4},{6,7},{7,6},{8,9},{9,8},{10,11... | collective-permute-start | bytes 368648 | tf_op jit(solution)/shard_map/ppermute | solution.py:689
  35.6 0.8 %collective-permute-start.11 = (bf16[64,640]{1,0:T(8,128)(2,1)S(1)}, bf16[64,640]{1,0:T(8,128)(2,1)S(1)}, u32[]{:S(2)}, u32[]{:S(2)}) collective-permute-start(bf16[64,640]{1,0:T(8,128)(2,1)S(1)} %get-tuple-element.117), channel_id=1, source_target_pairs={{0,0},{1,1},{2,30},{3,31},{4,28},{5,29},{6,26},{7,27},{8,24},{9,25... | collective-permute-start | bytes 245768 | tf_op jit(solution)/shard_map/ppermute | solution.py:689
  36.4 0.0 copy-start.3
  36.4 0.6 kernel_grads_add_0.2.refs_12_.refs_0_
  37.1 0.0 copy-done.3
  37.1 2.6 %later_backward.1 = (bf16[256,160]{1,0:T(8,128)(2,1)S(1)}, bf16[3,320,320]{2,1,0:T(8,128)(2,1)S(1)}, bf16[256,160]{1,0:T(8,128)(2,1)S(1)}, bf16[256,320]{1,0:T(8...) custom-call(s32[2,16]{1,0:T(2,128)S(1)} %bitcast.27, ...), custom_call_target="tpu_custom_call" | custom-call | flops 1 | bytes 1 | tf_op jit(solution)/shard_map/later_backward/pallas_call | solution.py:207
  39.8 1.2 %collective-permute-start.10 = (bf16[128,640]{1,0:T(8,128)(2,1)S(1)}, bf16[128,640]{1,0:T(8,128)(2,1)S(1)}, u32[]{:S(2)}, u32[]{:S(2)}) collective-permute-start(bf16[128,640]{1,0:T(8,128)(2,1)S(1)} %get-tuple-element.115), channel_id=1, source_target_pairs={{0,1},{1,0},{2,3},{3,2},{4,5},{5,4},{6,7},{7,6},{8,9},{9,8},{10,11... | collective-permute-start | bytes 491528 | tf_op jit(solution)/shard_map/ppermute | solution.py:689
  41.0 1.8 %last_forward.1 = (bf16[128,480]{1,0:T(8,128)(2,1)S(1)}, bf16[128,480]{1,0:T(8,128)(2,1)S(1)}) custom-call(s32[2,16]{1,0:T(2,128)S(1)} %bitcast.28, f32[256,160]{1,0:T(8,128)S(1)} %get-tuple-element.111.refs_3_.refs_1_, bf16[96,640]{1,0:T(8,128)(2,1)S(1)} %collective-permute-done.12.refs_2_, bf16[256,160]{1,0:T(8,128)(2,1)S(1)} %get-tuple-element.121.refs_3_, ...), custom_call_target="tpu_custom_call" | custom-call | flops 1 | bytes 1 | tf_op jit(solution)/shard_map/last_forward/pallas_call | solution.py:207
  42.8 1.0 %collective-permute-start.13 = (bf16[128,480]{1,0:T(8,128)(2,1)S(1)}, bf16[128,480]{1,0:T(8,128)(2,1)S(1)}, u32[]{:S(2)}, u32[]{:S(2)}) collective-permute-start(bf16[128,480]{1,0:T(8,128)(2,1)S(1)} %get-tuple-element.129), channel_id=1, source_target_pairs={{0,1},{1,0},{2,3},{3,2},{4,5},{5,4},{6,7},{7,6},{8,9},{9,8},{10,11... | collective-permute-start | bytes 368648 | tf_op jit(solution)/shard_map/ppermute | solution.py:689
  43.8 0.6 kernel_grads_add_0.3.refs_2_.refs_1_
  44.4 0.2 pack_rows.1
  44.6 1.8 %collective-permute-done.10.refs_9_.refs_3_ = bf16[128,640]{1,0:T(8,128)(2,1)S(1)} collective-permute-done((bf16[128,640]{1,0:T(8,128)(2,1)S(1)}, bf16[128,640]{1,0:T(8,128)(2,1)S(1)}, u32[]{:S(2)}, u32[]{:S(2)}) %collective-permute-start.10) | collective-permute-done | bytes 163872 | tf_op jit(solution)/shard_map/ppermute | solution.py:689
  46.5 1.8 %write_queues.1 = (f32[8,128]{1,0:T(8,128)S(1)}, bf16[3,128,320]{2,1,0:T(8,128)(2,1)}, bf16[3,128,320]{2,1,0:T(8,128)(2,1)}, bf16[3,128,320]{2,1,0:T(8,128)(2,1)}, bf16[6,128,320]{2,1,0:T(8,128)(2,1)}) custom-call(s32[2,16]{1,0:T(2,128)S(1)} %bitcast.29, s32[2,16]{1,0:T(2,128)S(1)} %bitcast.35, bf16[3,128,320]{2,1,0:T(8,128)(2,1)S(1)} %get-tuple-element.77.refs_2_, ...), custom_call_target="tpu_custom_call" | custom-call | flops 1 | bytes 1 | tf_op jit(solution)/shard_map/write_queues/pallas_call | solution.py:207
  48.3 0.0 collective-permute-done.13.refs_1_
  48.3 1.5 %collective-permute-start.16 = (bf16[128,480]{1,0:T(8,128)(2,1)S(1)}, bf16[128,480]{1,0:T(8,128)(2,1)S(1)}, u32[]{:S(2)}, u32[]{:S(2)}) collective-permute-start(bf16[128,480]{1,0:T(8,128)(2,1)S(1)} %get-tuple-element.136), channel_id=1, source_target_pairs={{0,1},{1,0},{2,3},{3,2},{4,5},{5,4},{6,7},{7,6},{8,9},{9,8},{10,11... | collective-permute-start | bytes 368648 | tf_op jit(solution)/shard_map/ppermute | solution.py:689
  49.9 0.2 add_rows.1
  50.1 3.0 %collective-permute-start.15 = (bf16[128,320]{1,0:T(8,128)(2,1)S(1)}, bf16[128,320]{1,0:T(8,128)(2,1)S(1)}, u32[]{:S(2)}, u32[]{:S(2)}) collective-permute-start(bf16[128,320]{1,0:T(8,128)(2,1)S(1)} %get-tuple-element.133), channel_id=1, source_target_pairs={{0,30},{1,31},{2,28},{3,29},{4,26},{5,27},{6,24},{7,25},{8,22},{9,... | collective-permute-start | bytes 245768 | tf_op jit(solution)/shard_map/ppermute | solution.py:689
  53.1 2.6 %last_backward.1 = (bf16[32,640]{1,0:T(8,128)(2,1)S(1)}, bf16[32,640]{1,0:T(8,128)(2,1)S(1)}, bf16[3,320,320]{2,1,0:T(8,128)(2,1)S(1)}, bf16[256,160]{1,0:T(8,128)(2,1)S(1)}) custom-call(s32[2,16]{1,0:T(2,128)S(1)} %bitcast.30, s32[2,16]{1,0:T(2,128)S(1)} %bitcast.36, bf16[256,160]{1,0:T(8,128)(2,1)S(1)} %get-tuple-element.122.refs_7_.refs_2_, ...), custom_call_target="tpu_custom_call" | custom-call | flops 1 | bytes 1 | tf_op jit(solution)/shard_map/last_backward/pallas_call | solution.py:207
  55.7 4.5 %collective-permute-start.17 = (bf16[32,640]{1,0:T(8,128)(2,1)S(1)}, bf16[32,640]{1,0:T(8,128)(2,1)S(1)}, u32[]{:S(2)}, u32[]{:S(2)}) collective-permute-start(bf16[32,640]{1,0:T(8,128)(2,1)S(1)} %get-tuple-element.137), channel_id=1, source_target_pairs={{0,30},{1,31},{2,0},{3,1},{4,2},{5,3},{6,4},{7,5},{8,6},{9,7},{10,... | collective-permute-start | bytes 122888 | tf_op jit(solution)/shard_map/ppermute | solution.py:689
  60.2 0.8 %collective-permute-start.18 = (bf16[32,640]{1,0:T(8,128)(2,1)S(1)}, bf16[32,640]{1,0:T(8,128)(2,1)S(1)}, u32[]{:S(2)}, u32[]{:S(2)}) collective-permute-start(bf16[32,640]{1,0:T(8,128)(2,1)S(1)} %get-tuple-element.138), channel_id=1, source_target_pairs={{0,31},{1,30},{2,1},{3,0},{4,3},{5,2},{6,5},{7,4},{8,7},{9,6},{10,... | collective-permute-start | bytes 122888 | tf_op jit(solution)/shard_map/ppermute | solution.py:689
  61.0 2.2 %kernel_grads_last.1 = (f32[8,128]{1,0:T(8,128)S(1)}, f32[18,160,320]{2,1,0:T(8,128)}) custom-call(f32[9,160,320]{2,1,0:T(8,128)S(1)} %kernel_grads_add_0.2.refs_12_.refs_0_, f32[9,160,320]{2,1,0:T(8,128)S(1)} %kernel_grads_add_0.3.refs_2_.refs_1_, bf16[256,160]{1,0:T(8,128)(2,1)S(1)} %get-tuple-element.139.refs_2_, ...), custom_call_target="tpu_custom_call" | custom-call | flops 1 | bytes 1 | tf_op jit(solution)/shard_map/kernel_grads_last/pallas_call | solution.py:207
  63.1 0.5 collective-permute-done.18.refs_13_
  63.6 1.5 %finish.1 = (bf16[3,128,320]{2,1,0:T(8,128)(2,1)}, bf16[3,128,320]{2,1,0:T(8,128)(2,1)}, bf16[3,128,320]{2,1,0:T(8,128)(2,1)}, bf16[6,128,320]{2,1,0:T(8,128)(2,1)}, bf16[2,128,320]{2,1,0:T(8,128)(2,1)}) custom-call(s32[2,16]{1,0:T(2,128)S(1)} %bitcast.31, ...), custom_call_target="tpu_custom_call", output_to_operand_aliasing={{0}: (2, {}), {1}: (3, {}), {2}: (4, {}), {3}: (5, {})} | custom-call | flops 1 | bytes 1 | tf_op jit(solution)/shard_map/finish/pallas_call | solution.py:207
  (16 shorter events, 0.0 us)
Async XLA Ops:
  0.6 8.8 %copy-start = (bf16[1,2,3,3,160,320]{5,4,3,2,1,0:T(8,128)(2,1)S(1)}, bf16[1,2,3,3,160,320]{5,4,3,2,1,0:T(8,128)(2,1)}, u32[]{:S(2)}) copy-start(bf16[1,2,3,3,160,320]{5,4,3,2,1,0:T(8,128)(2,1)} %param.12) | copy-start | bytes 5529604
  2.4 5.0 %collective-permute-start = (bf16[32,640]{1,0:T(8,128)(2,1)S(1)}, bf16[32,640]{1,0:T(8,128)(2,1)S(1)}, u32[]{:S(2)}, u32[]{:S(2)}) collective-permute-start(bf16[32,640]{1,0:T(8,128)(2,1)S(1)} %get-tuple-element.84), channel_id=1, source_target_pairs={{0,1},{1,0},{2,3},{3,2},{4,5},{5,4},{6,7},{7,6},{8,9},{9,8},{10,11... | collective-permute-start | bytes 122888 | tf_op jit(solution)/shard_map/ppermute | solution.py:689
  7.4 6.3 %collective-permute-start.1 = (bf16[128,640]{1,0:T(8,128)(2,1)S(1)}, bf16[128,640]{1,0:T(8,128)(2,1)S(1)}, u32[]{:S(2)}, u32[]{:S(2)}) collective-permute-start(bf16[128,640]{1,0:T(8,128)(2,1)S(1)} %get-tuple-element.86), channel_id=1, source_target_pairs={{0,1},{1,0},{2,3},{3,2},{4,5},{5,4},{6,7},{7,6},{8,9},{9,8},{10,11... | collective-permute-start | bytes 491528 | tf_op jit(solution)/shard_map/ppermute | solution.py:689
  9.4 8.5 %copy-start.1 = (f32[1,2,3,3,160,320]{5,4,3,2,1,0:T(8,128)S(1)}, f32[1,2,3,3,160,320]{5,4,3,2,1,0:T(8,128)}, u32[]{:S(2)}) copy-start(f32[1,2,3,3,160,320]{5,4,3,2,1,0:T(8,128)} %param.13) | copy-start | bytes 11059204
  10.7 7.9 %collective-permute-start.3 = (bf16[128,640]{1,0:T(8,128)(2,1)S(1)}, bf16[128,640]{1,0:T(8,128)(2,1)S(1)}, u32[]{:S(2)}, u32[]{:S(2)}) collective-permute-start(bf16[128,640]{1,0:T(8,128)(2,1)S(1)} %get-tuple-element.95), channel_id=1, source_target_pairs={{0,1},{1,0},{2,3},{3,2},{4,5},{5,4},{6,7},{7,6},{8,9},{9,8},{10,11... | collective-permute-start | bytes 491528 | tf_op jit(solution)/shard_map/ppermute | solution.py:689
  15.4 9.6 %collective-permute-start.2 = (bf16[128,640]{1,0:T(8,128)(2,1)S(1)}, bf16[128,640]{1,0:T(8,128)(2,1)S(1)}, u32[]{:S(2)}, u32[]{:S(2)}) collective-permute-start(bf16[128,640]{1,0:T(8,128)(2,1)S(1)} %get-tuple-element.93), channel_id=1, source_target_pairs={{0,1},{1,0},{2,3},{3,2},{4,5},{5,4},{6,7},{7,6},{8,9},{9,8},{10,11... | collective-permute-start | bytes 491528 | tf_op jit(solution)/shard_map/ppermute | solution.py:689
  17.8 7.2 %collective-permute-start.4 = (bf16[64,640]{1,0:T(8,128)(2,1)S(1)}, bf16[64,640]{1,0:T(8,128)(2,1)S(1)}, u32[]{:S(2)}, u32[]{:S(2)}) collective-permute-start(bf16[64,640]{1,0:T(8,128)(2,1)S(1)} %get-tuple-element.96), channel_id=1, source_target_pairs={{0,30},{1,31},{2,28},{3,29},{4,26},{5,27},{6,24},{7,25},{8,22},{9,... | collective-permute-start | bytes 245768 | tf_op jit(solution)/shard_map/ppermute | solution.py:689
  20.0 12.7 %copy-start.2 = (s32[16,2]{0,1:T(2,128)S(1)}, s32[16,2]{0,1:T(2,128)}, u32[]{:S(2)}) copy-start(s32[16,2]{0,1:T(2,128)} %param.14) | copy-start | bytes 388
  20.0 12.7 %collective-permute-start.8 = (bf16[64,640]{1,0:T(8,128)(2,1)S(1)}, bf16[64,640]{1,0:T(8,128)(2,1)S(1)}, u32[]{:S(2)}, u32[]{:S(2)}) collective-permute-start(bf16[64,640]{1,0:T(8,128)(2,1)S(1)} %get-tuple-element.104), channel_id=1, source_target_pairs={{0,2},{1,3},{2,4},{3,5},{4,6},{5,7},{6,8},{7,9},{8,10},{9,11},{10,... | collective-permute-start | bytes 245768 | tf_op jit(solution)/shard_map/ppermute | solution.py:689
  24.5 8.2 %collective-permute-start.9 = (bf16[64,640]{1,0:T(8,128)(2,1)S(1)}, bf16[64,640]{1,0:T(8,128)(2,1)S(1)}, u32[]{:S(2)}, u32[]{:S(2)}) collective-permute-start(bf16[64,640]{1,0:T(8,128)(2,1)S(1)} %get-tuple-element.105), channel_id=1, source_target_pairs={{0,3},{1,2},{2,5},{3,4},{4,7},{5,6},{6,9},{7,8},{8,11},{9,10},{10,... | collective-permute-start | bytes 245768 | tf_op jit(solution)/shard_map/ppermute | solution.py:689
  26.9 10.1 %collective-permute-start.7 = (bf16[128,640]{1,0:T(8,128)(2,1)S(1)}, bf16[128,640]{1,0:T(8,128)(2,1)S(1)}, u32[]{:S(2)}, u32[]{:S(2)}) collective-permute-start(bf16[128,640]{1,0:T(8,128)(2,1)S(1)} %get-tuple-element.103), channel_id=1, source_target_pairs={{0,1},{1,0},{2,3},{3,2},{4,5},{5,4},{6,7},{7,6},{8,9},{9,8},{10,11... | collective-permute-start | bytes 491528 | tf_op jit(solution)/shard_map/ppermute | solution.py:689
  28.2 8.8 %collective-permute-start.6 = (bf16[64,640]{1,0:T(8,128)(2,1)S(1)}, bf16[64,640]{1,0:T(8,128)(2,1)S(1)}, u32[]{:S(2)}, u32[]{:S(2)}) collective-permute-start(bf16[64,640]{1,0:T(8,128)(2,1)S(1)} %get-tuple-element.102.refs_8_), channel_id=1, source_target_pairs={{0,31},{1,30},{2,1},{3,0},{4,3},{5,2},{6,5},{7,4},{8,7},{9,6},{10,... | collective-permute-start | bytes 245768 | tf_op jit(solution)/shard_map/ppermute | solution.py:689
  32.3 4.8 %collective-permute-start.5 = (bf16[64,640]{1,0:T(8,128)(2,1)S(1)}, bf16[64,640]{1,0:T(8,128)(2,1)S(1)}, u32[]{:S(2)}, u32[]{:S(2)}) collective-permute-start(bf16[64,640]{1,0:T(8,128)(2,1)S(1)} %get-tuple-element.102.refs_8_), channel_id=1, source_target_pairs={{0,30},{1,31},{2,0},{3,1},{4,2},{5,3},{6,4},{7,5},{8,6},{9,7},{10,... | collective-permute-start | bytes 245768 | tf_op jit(solution)/shard_map/ppermute | solution.py:689
  34.6 6.3 %collective-permute-start.12 = (bf16[96,640]{1,0:T(8,128)(2,1)S(1)}, bf16[96,640]{1,0:T(8,128)(2,1)S(1)}, u32[]{:S(2)}, u32[]{:S(2)}) collective-permute-start(bf16[96,640]{1,0:T(8,128)(2,1)S(1)} %get-tuple-element.120), channel_id=1, source_target_pairs={{0,1},{1,0},{2,3},{3,2},{4,5},{5,4},{6,7},{7,6},{8,9},{9,8},{10,11... | collective-permute-start | bytes 368648 | tf_op jit(solution)/shard_map/ppermute | solution.py:689
  35.6 5.4 %collective-permute-start.11 = (bf16[64,640]{1,0:T(8,128)(2,1)S(1)}, bf16[64,640]{1,0:T(8,128)(2,1)S(1)}, u32[]{:S(2)}, u32[]{:S(2)}) collective-permute-start(bf16[64,640]{1,0:T(8,128)(2,1)S(1)} %get-tuple-element.117), channel_id=1, source_target_pairs={{0,0},{1,1},{2,30},{3,31},{4,28},{5,29},{6,26},{7,27},{8,24},{9,25... | collective-permute-start | bytes 245768 | tf_op jit(solution)/shard_map/ppermute | solution.py:689
  36.4 0.7 %copy-start.3 = (s32[16,2]{0,1:T(2,128)S(1)}, s32[16,2]{0,1:T(2,128)}, u32[]{:S(2)}) copy-start(s32[16,2]{0,1:T(2,128)} %param.15) | copy-start | bytes 388
  39.8 6.7 %collective-permute-start.10 = (bf16[128,640]{1,0:T(8,128)(2,1)S(1)}, bf16[128,640]{1,0:T(8,128)(2,1)S(1)}, u32[]{:S(2)}, u32[]{:S(2)}) collective-permute-start(bf16[128,640]{1,0:T(8,128)(2,1)S(1)} %get-tuple-element.115), channel_id=1, source_target_pairs={{0,1},{1,0},{2,3},{3,2},{4,5},{5,4},{6,7},{7,6},{8,9},{9,8},{10,11... | collective-permute-start | bytes 491528 | tf_op jit(solution)/shard_map/ppermute | solution.py:689
  42.8 5.5 %collective-permute-start.13 = (bf16[128,480]{1,0:T(8,128)(2,1)S(1)}, bf16[128,480]{1,0:T(8,128)(2,1)S(1)}, u32[]{:S(2)}, u32[]{:S(2)}) collective-permute-start(bf16[128,480]{1,0:T(8,128)(2,1)S(1)} %get-tuple-element.129), channel_id=1, source_target_pairs={{0,1},{1,0},{2,3},{3,2},{4,5},{5,4},{6,7},{7,6},{8,9},{9,8},{10,11... | collective-permute-start | bytes 368648 | tf_op jit(solution)/shard_map/ppermute | solution.py:689
  48.3 15.3 %collective-permute-start.16 = (bf16[128,480]{1,0:T(8,128)(2,1)S(1)}, bf16[128,480]{1,0:T(8,128)(2,1)S(1)}, u32[]{:S(2)}, u32[]{:S(2)}) collective-permute-start(bf16[128,480]{1,0:T(8,128)(2,1)S(1)} %get-tuple-element.136), channel_id=1, source_target_pairs={{0,1},{1,0},{2,3},{3,2},{4,5},{5,4},{6,7},{7,6},{8,9},{9,8},{10,11... | collective-permute-start | bytes 368648 | tf_op jit(solution)/shard_map/ppermute | solution.py:689
  50.1 13.5 %collective-permute-start.15 = (bf16[128,320]{1,0:T(8,128)(2,1)S(1)}, bf16[128,320]{1,0:T(8,128)(2,1)S(1)}, u32[]{:S(2)}, u32[]{:S(2)}) collective-permute-start(bf16[128,320]{1,0:T(8,128)(2,1)S(1)} %get-tuple-element.133), channel_id=1, source_target_pairs={{0,30},{1,31},{2,28},{3,29},{4,26},{5,27},{6,24},{7,25},{8,22},{9,... | collective-permute-start | bytes 245768 | tf_op jit(solution)/shard_map/ppermute | solution.py:689
  53.1 10.5 %collective-permute-start.14 = (bf16[128,320]{1,0:T(8,128)(2,1)S(1)}, bf16[128,320]{1,0:T(8,128)(2,1)S(1)}, u32[]{:S(2)}, u32[]{:S(2)}) collective-permute-start(bf16[128,320]{1,0:T(8,128)(2,1)S(1)} %get-tuple-element.131.refs_9_.refs_6_), channel_id=1, source_target_pairs={{0,2},{1,3},{2,4},{3,5},{4,6},{5,7},{6,8},{7,9},{8,10},{9,11},{10,... | collective-permute-start | bytes 245768 | tf_op jit(solution)/shard_map/ppermute | solution.py:689
  55.7 7.4 %collective-permute-start.17 = (bf16[32,640]{1,0:T(8,128)(2,1)S(1)}, bf16[32,640]{1,0:T(8,128)(2,1)S(1)}, u32[]{:S(2)}, u32[]{:S(2)}) collective-permute-start(bf16[32,640]{1,0:T(8,128)(2,1)S(1)} %get-tuple-element.137), channel_id=1, source_target_pairs={{0,30},{1,31},{2,0},{3,1},{4,2},{5,3},{6,4},{7,5},{8,6},{9,7},{10,... | collective-permute-start | bytes 122888 | tf_op jit(solution)/shard_map/ppermute | solution.py:689
  60.2 3.4 %collective-permute-start.18 = (bf16[32,640]{1,0:T(8,128)(2,1)S(1)}, bf16[32,640]{1,0:T(8,128)(2,1)S(1)}, u32[]{:S(2)}, u32[]{:S(2)}) collective-permute-start(bf16[32,640]{1,0:T(8,128)(2,1)S(1)} %get-tuple-element.138), channel_id=1, source_target_pairs={{0,31},{1,30},{2,1},{3,0},{4,3},{5,2},{6,5},{7,4},{8,7},{9,6},{10,... | collective-permute-start | bytes 122888 | tf_op jit(solution)/shard_map/ppermute | solution.py:689

commit v2 on v1

--- a/solution.py
+++ b/solution.py
@@ -165,24 +165,19 @@
     return total
 
 
-def convolve_back(z, pad_ref, kernel_ref, which, line_ref):
-    cells, cols, w = z.cells, z.cols, z.share
+def convolve_back(z, pad_ref, kernel_ref, which):
     total = None
     for a in range(3):
-        first = (9 * which + 3 * (2 - a)) * w
-        term = lax.dot_general(
-            pad_ref[1, a * cols : a * cols + cells, :],
-            kernel_ref[first : first + 3 * w, :],
-            (((1,), (1,)), ((), ())),
-            preferred_element_type=F32,
-        )
-        total = term if total is None else total + term
-    column = lax.rem(lax.broadcasted_iota(jnp.int32, (cells, 1), 0), cols)
-    line_ref[8 : 8 + cells, :w] = total[:, :w]
-    out = total[:, w : 2 * w]
-    out = out + jnp.where(column < cols - 1, line_ref[9 : 9 + cells, :w], 0.0)
-    line_ref[8 : 8 + cells, :w] = total[:, 2 * w :]
-    return out + jnp.where(column > 0, line_ref[7 : 7 + cells, :w], 0.0)
+        for b in range(3):
+            first = (9 * which + 3 * (2 - a) + 2 - b) * z.share
+            term = lax.dot_general(
+                pad_ref[b, a * z.cols : a * z.cols + z.cells, :],
+                kernel_ref[first : first + z.share, :],
+                (((1,), (1,)), ((), ())),
+                preferred_element_type=F32,
+            )
+            total = term if total is None else total + term
+    return total
 
 
 def pad_shapes(z, width):
@@ -346,7 +341,7 @@
     logistic = sigmoid(y)
     act_out[...] = (y * logistic).astype(BF)
     spread(z, g, line, pad)
-    q = norm_back(z, y, factor, logistic, convolve_back(z, pad, kernel, 1, line)).astype(BF)
+    q = norm_back(z, y, factor, logistic, convolve_back(z, pad, kernel, 1)).astype(BF)
     q_out[...] = q
     fold(z, q_send, q.astype(F32))
 
@@ -467,7 +462,7 @@
     logistic = sigmoid(y)
     act_out[...] = (y * logistic).astype(BF)
     spread(z, now, line, pad)
-    back = norm_back(z, y, factor, logistic, convolve_back(z, pad, kernel, 0, line))
+    back = norm_back(z, y, factor, logistic, convolve_back(z, pad, kernel, 0))
     return share_of(z, g, row) + back, whole
 
 

time: 65.5 us -> 64.5 us (0.985)
  Pallas kernels: 26 us -> 24.7 us
    pallas_call x18, Pallas kernels: 26 us -> 24.7 us  [call(): pl.pallas_call(inner, name=name, out_shape=[jax.ShapeDtypeStruct(shape, d...]
  transfers between devices with their start and end apart: 19 -> 19, of which waited for: 5 -> 5; matrix products, arithmetic and copies ran while one was open for 0% -> 0% of each run, Pallas kernels for 35% -> 33%
where the time goes in v2:
time: 64.5 us; the launch traced here: 64.3 us
  starting transfers between devices  32.1 us (50%)
  Pallas kernels  24.7 us (38%)
  waiting for transfers between devices  6.43 us (10%)
  between operations  1.01 us (2%)
    ppermute x19, starting transfers between devices, move(): return lax.ppermute(x, ('section', 'row'), route)  32.1 us
    pallas_call x18, Pallas kernels, call(): pl.pallas_call(inner, name=name, out_shape=[jax.ShapeDtypeStruct(shape, d...  24.7 us
    ppermute x19, waiting for transfers between devices, move(): return lax.ppermute(x, ('section', 'row'), route)  6.43 us
  transfers between devices with their start and end apart: 19, of which 5 were waited for; matrix products, arithmetic and copies ran while one was open for 0% of the time, Pallas kernels for 33%

profile of v2, /device:TPU:0, one launch (start us, length us, event | category | flops | bytes accessed | tf_op | source)
XLA Modules:
  0.0 64.3 jit_solution(7105116024258386335)
XLA Ops:
  0.6 1.7 %pack_first.1 = (bf16[32,640]{1,0:T(8,128)(2,1)S(1)}, bf16[32,640]{1,0:T(8,128)(2,1)S(1)}, bf16[3,128,320]{2,1,0:T(8,128)(2,1)S(1)}, bf16[3,128,320]{2,1,0:T(8,1...) custom-call(s32[2,16]{1,0:T(2,128)} %bitcast.24, s32[2,16]{1,0:T(2,128)} %bitcast.32, ...), custom_call_target="tpu_custom_call" | custom-call | flops 1 | bytes 1 | tf_op jit(solution)/shard_map/pack_first/pallas_call | solution.py:202
  2.4 3.0 %collective-permute-start = (bf16[32,640]{1,0:T(8,128)(2,1)S(1)}, bf16[32,640]{1,0:T(8,128)(2,1)S(1)}, u32[]{:S(2)}, u32[]{:S(2)}) collective-permute-start(bf16[32,640]{1,0:T(8,128)(2,1)S(1)} %get-tuple-element.84), channel_id=1, source_target_pairs={{0,1},{1,0},{2,3},{3,2},{4,5},{5,4},{6,7},{7,6},{8,9},{9,8},{10,11... | collective-permute-start | bytes 122888 | tf_op jit(solution)/shard_map/ppermute | solution.py:684
  5.4 1.2 %pack_later.1 = (bf16[128,640]{1,0:T(8,128)(2,1)S(1)}, bf16[128,640]{1,0:T(8,128)(2,1)S(1)}, bf16[64,640]{1,0:T(8,128)(2,1)S(1)}, bf16[64,640]{1,0:T(8,128)(2,1)...) custom-call(s32[2,16]{1,0:T(2,128)} %bitcast.25, ...), custom_call_target="tpu_custom_call" | custom-call | flops 1 | bytes 1 | tf_op jit(solution)/shard_map/pack_later/pallas_call | solution.py:202
  6.6 0.7 %collective-permute-done.refs_1_ = bf16[32,640]{1,0:T(8,128)(2,1)S(1)} collective-permute-done((bf16[32,640]{1,0:T(8,128)(2,1)S(1)}, bf16[32,640]{1,0:T(8,128)(2,1)S(1)}, u32[]{:S(2)}, u32[]{:S(2)}) %collective-permute-start) | collective-permute-done | bytes 40992 | tf_op jit(solution)/shard_map/ppermute | solution.py:684
  7.4 2.0 %collective-permute-start.1 = (bf16[128,640]{1,0:T(8,128)(2,1)S(1)}, bf16[128,640]{1,0:T(8,128)(2,1)S(1)}, u32[]{:S(2)}, u32[]{:S(2)}) collective-permute-start(bf16[128,640]{1,0:T(8,128)(2,1)S(1)} %get-tuple-element.86), channel_id=1, source_target_pairs={{0,1},{1,0},{2,3},{3,2},{4,5},{5,4},{6,7},{7,6},{8,9},{9,8},{10,11... | collective-permute-start | bytes 491528 | tf_op jit(solution)/shard_map/ppermute | solution.py:684
  9.4 1.3 %first_forward.1 = (f32[256,160]{1,0:T(8,128)S(1)}, bf16[256,160]{1,0:T(8,128)(2,1)S(1)}, bf16[128,640]{1,0:T(8,128)(2,1)S(1)}) custom-call(bf16[32,640]{1,0:T(8,128)(2,1)S(1)} %get-tuple-element.81.refs_6_.refs_0_, bf16[32,640]{1,0:T(8,128)(2,1)S(1)} %collective-permute-done.refs_1_, bf16[64,640]{1,0:T(8,128)(2,1)S(1)} %get-tuple-element.89.refs_2_.refs_3_.refs_5_, ...), custom_call_target="tpu_custom_call" | custom-call | flops 1 | bytes 1 | tf_op jit(solution)/shard_map/first_forward/pallas_call | solution.py:202
  10.7 0.1 collective-permute-start.3
  10.8 2.9 %collective-permute-done.1.refs_1_.refs_4_ = bf16[128,640]{1,0:T(8,128)(2,1)S(1)} collective-permute-done((bf16[128,640]{1,0:T(8,128)(2,1)S(1)}, bf16[128,640]{1,0:T(8,128)(2,1)S(1)}, u32[]{:S(2)}, u32[]{:S(2)}) %collective-permute-start.1) | collective-permute-done | bytes 163872 | tf_op jit(solution)/shard_map/ppermute | solution.py:684
  13.7 1.4 %first_backward.1 = (bf16[256,160]{1,0:T(8,128)(2,1)S(1)}, bf16[64,640]{1,0:T(8,128)(2,1)S(1)}, bf16[3,320,320]{2,1,0:T(8,128)(2,1)S(1)}, bf16[256,160]{1,0:T(8,128)(2,1)S(1)}, bf16[128,640]{1,0:T(8,128)(2,1)S(1)}) custom-call(bf16[128,640]{1,0:T(8,128)(2,1)S(1)} %get-tuple-element.85.refs_0_.refs_3_, ...), custom_call_target="tpu_custom_call" | custom-call | flops 1 | bytes 1 | tf_op jit(solution)/shard_map/first_backward/pallas_call | solution.py:202
  15.1 2.3 %collective-permute-start.2 = (bf16[128,640]{1,0:T(8,128)(2,1)S(1)}, bf16[128,640]{1,0:T(8,128)(2,1)S(1)}, u32[]{:S(2)}, u32[]{:S(2)}) collective-permute-start(bf16[128,640]{1,0:T(8,128)(2,1)S(1)} %get-tuple-element.93), channel_id=1, source_target_pairs={{0,1},{1,0},{2,3},{3,2},{4,5},{5,4},{6,7},{7,6},{8,9},{9,8},{10,11... | collective-permute-start | bytes 491528 | tf_op jit(solution)/shard_map/ppermute | solution.py:684
  17.4 0.2 collective-permute-start.4
  17.6 0.6 kernel_grads_add_9.1.refs_6_.refs_0_
  18.2 1.4 %second_forward.1 = (bf16[256,160]{1,0:T(8,128)(2,1)S(1)}, bf16[256,320]{1,0:T(8,128)(2,1)S(1)}, bf16[64,640]{1,0:T(8,128)(2,1)S(1)}, bf16[64,640]{1,0:T(8,128)(2,1)S(1)}) custom-call(f32[256,160]{1,0:T(8,128)S(1)} %get-tuple-element.91.refs_5_.refs_0_, bf16[128,640]{1,0:T(8,128)(2,1)S(1)} %collective-permute-done.3.refs_1_.refs_4_.refs_6_, ...), custom_call_target="tpu_custom_call" | custom-call | flops 1 | bytes 1 | tf_op jit(solution)/shard_map/second_forward/pallas_call | solution.py:202
  19.7 0.0 copy-start.2
  19.7 4.5 %collective-permute-start.8 = (bf16[64,640]{1,0:T(8,128)(2,1)S(1)}, bf16[64,640]{1,0:T(8,128)(2,1)S(1)}, u32[]{:S(2)}, u32[]{:S(2)}) collective-permute-start(bf16[64,640]{1,0:T(8,128)(2,1)S(1)} %get-tuple-element.104), channel_id=1, source_target_pairs={{0,2},{1,3},{2,4},{3,5},{4,6},{5,7},{6,8},{7,9},{8,10},{9,11},{10,... | collective-permute-start | bytes 245768 | tf_op jit(solution)/shard_map/ppermute | solution.py:684
  24.2 0.4 collective-permute-start.9
  24.6 0.1 collective-permute-done.4.refs_5_.refs_4_
  24.7 0.0 collective-permute-done.2.refs_1_.refs_4_.refs_8_
  24.7 1.6 %second_backward.1 = (bf16[64,640]{1,0:T(8,128)(2,1)S(1)}, bf16[3,320,320]{2,1,0:T(8,128)(2,1)S(1)}, bf16[256,160]{1,0:T(8,128)(2,1)S(1)}, bf16[128,640]{1,0:T(8,128)(2,1)S(1)}) custom-call(bf16[256,160]{1,0:T(8,128)(2,1)S(1)} %get-tuple-element.92.refs_3_.refs_0_, bf16[128,640]{1,0:T(8,128)(2,1)S(1)} %collective-permute-done.2.refs_1_.refs_4_.refs_8_, ...), custom_call_target="tpu_custom_call" | custom-call | flops 1 | bytes 1 | tf_op jit(solution)/shard_map/second_backward/pallas_call | solution.py:202
  26.3 1.3 %collective-permute-start.7 = (bf16[128,640]{1,0:T(8,128)(2,1)S(1)}, bf16[128,640]{1,0:T(8,128)(2,1)S(1)}, u32[]{:S(2)}, u32[]{:S(2)}) collective-permute-start(bf16[128,640]{1,0:T(8,128)(2,1)S(1)} %get-tuple-element.103), channel_id=1, source_target_pairs={{0,1},{1,0},{2,3},{3,2},{4,5},{5,4},{6,7},{7,6},{8,9},{9,8},{10,11... | collective-permute-start | bytes 491528 | tf_op jit(solution)/shard_map/ppermute | solution.py:684
  27.6 4.1 %collective-permute-start.6 = (bf16[64,640]{1,0:T(8,128)(2,1)S(1)}, bf16[64,640]{1,0:T(8,128)(2,1)S(1)}, u32[]{:S(2)}, u32[]{:S(2)}) collective-permute-start(bf16[64,640]{1,0:T(8,128)(2,1)S(1)} %get-tuple-element.102.refs_8_), channel_id=1, source_target_pairs={{0,31},{1,30},{2,1},{3,0},{4,3},{5,2},{6,5},{7,4},{8,7},{9,6},{10,... | collective-permute-start | bytes 245768 | tf_op jit(solution)/shard_map/ppermute | solution.py:684
  31.7 0.4 collective-permute-start.5
  32.1 1.9 %later_forward.1 = (f32[256,160]{1,0:T(8,128)S(1)}, bf16[256,160]{1,0:T(8,128)(2,1)S(1)}, bf16[256,160]{1,0:T(8,128)(2,1)S(1)}, bf16[64,640]{1,0:T(8,128)(2,1)S(1)}, bf16[96,640]{1,0:T(8,128)(2,1)S(1)}) custom-call(s32[2,16]{1,0:T(2,128)S(1)} %bitcast.26, bf16[64,640]{1,0:T(8,128)(2,1)S(1)} %collective-permute-done.8.refs_1_, ...), custom_call_target="tpu_custom_call" | custom-call | flops 1 | bytes 1 | tf_op jit(solution)/shard_map/later_forward/pallas_call | solution.py:202
  34.0 1.0 %collective-permute-start.12 = (bf16[96,640]{1,0:T(8,128)(2,1)S(1)}, bf16[96,640]{1,0:T(8,128)(2,1)S(1)}, u32[]{:S(2)}, u32[]{:S(2)}) collective-permute-start(bf16[96,640]{1,0:T(8,128)(2,1)S(1)} %get-tuple-element.120), channel_id=1, source_target_pairs={{0,1},{1,0},{2,3},{3,2},{4,5},{5,4},{6,7},{7,6},{8,9},{9,8},{10,11... | collective-permute-start | bytes 368648 | tf_op jit(solution)/shard_map/ppermute | solution.py:684
  35.0 0.8 %collective-permute-start.11 = (bf16[64,640]{1,0:T(8,128)(2,1)S(1)}, bf16[64,640]{1,0:T(8,128)(2,1)S(1)}, u32[]{:S(2)}, u32[]{:S(2)}) collective-permute-start(bf16[64,640]{1,0:T(8,128)(2,1)S(1)} %get-tuple-element.117), channel_id=1, source_target_pairs={{0,0},{1,1},{2,30},{3,31},{4,28},{5,29},{6,26},{7,27},{8,24},{9,25... | collective-permute-start | bytes 245768 | tf_op jit(solution)/shard_map/ppermute | solution.py:684
  35.8 0.0 copy-start.3
  35.8 0.6 kernel_grads_add_0.2.refs_12_.refs_0_
  36.4 0.0 collective-permute-done.5.refs_2_
  36.4 0.0 collective-permute-done.7.refs_5_
  36.5 0.0 copy-done.3
  36.5 2.3 %later_backward.1 = (bf16[256,160]{1,0:T(8,128)(2,1)S(1)}, bf16[3,320,320]{2,1,0:T(8,128)(2,1)S(1)}, bf16[256,160]{1,0:T(8,128)(2,1)S(1)}, bf16[256,320]{1,0:T(8...) custom-call(s32[2,16]{1,0:T(2,128)S(1)} %bitcast.27, ...), custom_call_target="tpu_custom_call" | custom-call | flops 1 | bytes 1 | tf_op jit(solution)/shard_map/later_backward/pallas_call | solution.py:202
  38.8 1.2 %collective-permute-start.10 = (bf16[128,640]{1,0:T(8,128)(2,1)S(1)}, bf16[128,640]{1,0:T(8,128)(2,1)S(1)}, u32[]{:S(2)}, u32[]{:S(2)}) collective-permute-start(bf16[128,640]{1,0:T(8,128)(2,1)S(1)} %get-tuple-element.115), channel_id=1, source_target_pairs={{0,1},{1,0},{2,3},{3,2},{4,5},{5,4},{6,7},{7,6},{8,9},{9,8},{10,11... | collective-permute-start | bytes 491528 | tf_op jit(solution)/shard_map/ppermute | solution.py:684
  40.0 1.8 %last_forward.1 = (bf16[128,480]{1,0:T(8,128)(2,1)S(1)}, bf16[128,480]{1,0:T(8,128)(2,1)S(1)}) custom-call(s32[2,16]{1,0:T(2,128)S(1)} %bitcast.28, f32[256,160]{1,0:T(8,128)S(1)} %get-tuple-element.111.refs_3_.refs_1_, bf16[96,640]{1,0:T(8,128)(2,1)S(1)} %collective-permute-done.12.refs_2_, bf16[256,160]{1,0:T(8,128)(2,1)S(1)} %get-tuple-element.121.refs_3_, ...), custom_call_target="tpu_custom_call" | custom-call | flops 1 | bytes 1 | tf_op jit(solution)/shard_map/last_forward/pallas_call | solution.py:202
  41.8 1.0 %collective-permute-start.13 = (bf16[128,480]{1,0:T(8,128)(2,1)S(1)}, bf16[128,480]{1,0:T(8,128)(2,1)S(1)}, u32[]{:S(2)}, u32[]{:S(2)}) collective-permute-start(bf16[128,480]{1,0:T(8,128)(2,1)S(1)} %get-tuple-element.129), channel_id=1, source_target_pairs={{0,1},{1,0},{2,3},{3,2},{4,5},{5,4},{6,7},{7,6},{8,9},{9,8},{10,11... | collective-permute-start | bytes 368648 | tf_op jit(solution)/shard_map/ppermute | solution.py:684
  42.8 0.6 kernel_grads_add_0.3.refs_2_.refs_1_
  43.4 0.2 pack_rows.1
  43.7 1.8 %collective-permute-done.10.refs_9_.refs_3_ = bf16[128,640]{1,0:T(8,128)(2,1)S(1)} collective-permute-done((bf16[128,640]{1,0:T(8,128)(2,1)S(1)}, bf16[128,640]{1,0:T(8,128)(2,1)S(1)}, u32[]{:S(2)}, u32[]{:S(2)}) %collective-permute-start.10) | collective-permute-done | bytes 163872 | tf_op jit(solution)/shard_map/ppermute | solution.py:684
  45.5 1.8 %write_queues.1 = (f32[8,128]{1,0:T(8,128)S(1)}, bf16[3,128,320]{2,1,0:T(8,128)(2,1)}, bf16[3,128,320]{2,1,0:T(8,128)(2,1)}, bf16[3,128,320]{2,1,0:T(8,128)(2,1)}, bf16[6,128,320]{2,1,0:T(8,128)(2,1)}) custom-call(s32[2,16]{1,0:T(2,128)S(1)} %bitcast.29, s32[2,16]{1,0:T(2,128)S(1)} %bitcast.35, bf16[3,128,320]{2,1,0:T(8,128)(2,1)S(1)} %get-tuple-element.77.refs_2_, ...), custom_call_target="tpu_custom_call" | custom-call | flops 1 | bytes 1 | tf_op jit(solution)/shard_map/write_queues/pallas_call | solution.py:202
  47.4 1.5 %collective-permute-start.16 = (bf16[128,480]{1,0:T(8,128)(2,1)S(1)}, bf16[128,480]{1,0:T(8,128)(2,1)S(1)}, u32[]{:S(2)}, u32[]{:S(2)}) collective-permute-start(bf16[128,480]{1,0:T(8,128)(2,1)S(1)} %get-tuple-element.136), channel_id=1, source_target_pairs={{0,1},{1,0},{2,3},{3,2},{4,5},{5,4},{6,7},{7,6},{8,9},{9,8},{10,11... | collective-permute-start | bytes 368648 | tf_op jit(solution)/shard_map/ppermute | solution.py:684
  48.9 0.2 add_rows.1
  49.1 3.4 %collective-permute-start.15 = (bf16[128,320]{1,0:T(8,128)(2,1)S(1)}, bf16[128,320]{1,0:T(8,128)(2,1)S(1)}, u32[]{:S(2)}, u32[]{:S(2)}) collective-permute-start(bf16[128,320]{1,0:T(8,128)(2,1)S(1)} %get-tuple-element.133), channel_id=1, source_target_pairs={{0,30},{1,31},{2,28},{3,29},{4,26},{5,27},{6,24},{7,25},{8,22},{9,... | collective-permute-start | bytes 245768 | tf_op jit(solution)/shard_map/ppermute | solution.py:684
  52.5 0.2 collective-permute-start.14
  52.7 2.3 %last_backward.1 = (bf16[32,640]{1,0:T(8,128)(2,1)S(1)}, bf16[32,640]{1,0:T(8,128)(2,1)S(1)}, bf16[3,320,320]{2,1,0:T(8,128)(2,1)S(1)}, bf16[256,160]{1,0:T(8,128)(2,1)S(1)}) custom-call(s32[2,16]{1,0:T(2,128)S(1)} %bitcast.30, s32[2,16]{1,0:T(2,128)S(1)} %bitcast.36, bf16[256,160]{1,0:T(8,128)(2,1)S(1)} %get-tuple-element.122.refs_7_.refs_2_, ...), custom_call_target="tpu_custom_call" | custom-call | flops 1 | bytes 1 | tf_op jit(solution)/shard_map/last_backward/pallas_call | solution.py:202
  54.9 4.3 %collective-permute-start.17 = (bf16[32,640]{1,0:T(8,128)(2,1)S(1)}, bf16[32,640]{1,0:T(8,128)(2,1)S(1)}, u32[]{:S(2)}, u32[]{:S(2)}) collective-permute-start(bf16[32,640]{1,0:T(8,128)(2,1)S(1)} %get-tuple-element.137), channel_id=1, source_target_pairs={{0,30},{1,31},{2,0},{3,1},{4,2},{5,3},{6,4},{7,5},{8,6},{9,7},{10,... | collective-permute-start | bytes 122888 | tf_op jit(solution)/shard_map/ppermute | solution.py:684
  59.2 0.5 collective-permute-start.18
  59.7 2.2 %kernel_grads_last.1 = (f32[8,128]{1,0:T(8,128)S(1)}, f32[18,160,320]{2,1,0:T(8,128)}) custom-call(f32[9,160,320]{2,1,0:T(8,128)S(1)} %kernel_grads_add_0.2.refs_12_.refs_0_, f32[9,160,320]{2,1,0:T(8,128)S(1)} %kernel_grads_add_0.3.refs_2_.refs_1_, bf16[256,160]{1,0:T(8,128)(2,1)S(1)} %get-tuple-element.139.refs_2_, ...), custom_call_target="tpu_custom_call" | custom-call | flops 1 | bytes 1 | tf_op jit(solution)/shard_map/kernel_grads_last/pallas_call | solution.py:202
  61.9 0.8 %collective-permute-done.18.refs_13_ = bf16[32,640]{1,0:T(8,128)(2,1)S(1)} collective-permute-done((bf16[32,640]{1,0:T(8,128)(2,1)S(1)}, bf16[32,640]{1,0:T(8,128)(2,1)S(1)}, u32[]{:S(2)}, u32[]{:S(2)}) %collective-permute-start.18) | collective-permute-done | bytes 40992 | tf_op jit(solution)/shard_map/ppermute | solution.py:684
  62.7 1.5 %finish.1 = (bf16[3,128,320]{2,1,0:T(8,128)(2,1)}, bf16[3,128,320]{2,1,0:T(8,128)(2,1)}, bf16[3,128,320]{2,1,0:T(8,128)(2,1)}, bf16[6,128,320]{2,1,0:T(8,128)(2,1)}, bf16[2,128,320]{2,1,0:T(8,128)(2,1)}) custom-call(s32[2,16]{1,0:T(2,128)S(1)} %bitcast.31, ...), custom_call_target="tpu_custom_call", output_to_operand_aliasing={{0}: (2, {}), {1}: (3, {}), {2}: (4, {}), {3}: (5, {})} | custom-call | flops 1 | bytes 1 | tf_op jit(solution)/shard_map/finish/pallas_call | solution.py:202
  (16 shorter events, 0.0 us)
Async XLA Ops:
  0.6 8.8 %copy-start = (bf16[1,2,3,3,160,320]{5,4,3,2,1,0:T(8,128)(2,1)S(1)}, bf16[1,2,3,3,160,320]{5,4,3,2,1,0:T(8,128)(2,1)}, u32[]{:S(2)}) copy-start(bf16[1,2,3,3,160,320]{5,4,3,2,1,0:T(8,128)(2,1)} %param.12) | copy-start | bytes 5529604
  2.4 5.0 %collective-permute-start = (bf16[32,640]{1,0:T(8,128)(2,1)S(1)}, bf16[32,640]{1,0:T(8,128)(2,1)S(1)}, u32[]{:S(2)}, u32[]{:S(2)}) collective-permute-start(bf16[32,640]{1,0:T(8,128)(2,1)S(1)} %get-tuple-element.84), channel_id=1, source_target_pairs={{0,1},{1,0},{2,3},{3,2},{4,5},{5,4},{6,7},{7,6},{8,9},{9,8},{10,11... | collective-permute-start | bytes 122888 | tf_op jit(solution)/shard_map/ppermute | solution.py:684
  7.4 6.3 %collective-permute-start.1 = (bf16[128,640]{1,0:T(8,128)(2,1)S(1)}, bf16[128,640]{1,0:T(8,128)(2,1)S(1)}, u32[]{:S(2)}, u32[]{:S(2)}) collective-permute-start(bf16[128,640]{1,0:T(8,128)(2,1)S(1)} %get-tuple-element.86), channel_id=1, source_target_pairs={{0,1},{1,0},{2,3},{3,2},{4,5},{5,4},{6,7},{7,6},{8,9},{9,8},{10,11... | collective-permute-start | bytes 491528 | tf_op jit(solution)/shard_map/ppermute | solution.py:684
  9.4 8.2 %copy-start.1 = (f32[1,2,3,3,160,320]{5,4,3,2,1,0:T(8,128)S(1)}, f32[1,2,3,3,160,320]{5,4,3,2,1,0:T(8,128)}, u32[]{:S(2)}) copy-start(f32[1,2,3,3,160,320]{5,4,3,2,1,0:T(8,128)} %param.13) | copy-start | bytes 11059204
  10.7 7.5 %collective-permute-start.3 = (bf16[128,640]{1,0:T(8,128)(2,1)S(1)}, bf16[128,640]{1,0:T(8,128)(2,1)S(1)}, u32[]{:S(2)}, u32[]{:S(2)}) collective-permute-start(bf16[128,640]{1,0:T(8,128)(2,1)S(1)} %get-tuple-element.95), channel_id=1, source_target_pairs={{0,1},{1,0},{2,3},{3,2},{4,5},{5,4},{6,7},{7,6},{8,9},{9,8},{10,11... | collective-permute-start | bytes 491528 | tf_op jit(solution)/shard_map/ppermute | solution.py:684
  15.1 9.6 %collective-permute-start.2 = (bf16[128,640]{1,0:T(8,128)(2,1)S(1)}, bf16[128,640]{1,0:T(8,128)(2,1)S(1)}, u32[]{:S(2)}, u32[]{:S(2)}) collective-permute-start(bf16[128,640]{1,0:T(8,128)(2,1)S(1)} %get-tuple-element.93), channel_id=1, source_target_pairs={{0,1},{1,0},{2,3},{3,2},{4,5},{5,4},{6,7},{7,6},{8,9},{9,8},{10,11... | collective-permute-start | bytes 491528 | tf_op jit(solution)/shard_map/ppermute | solution.py:684
  17.4 7.2 %collective-permute-start.4 = (bf16[64,640]{1,0:T(8,128)(2,1)S(1)}, bf16[64,640]{1,0:T(8,128)(2,1)S(1)}, u32[]{:S(2)}, u32[]{:S(2)}) collective-permute-start(bf16[64,640]{1,0:T(8,128)(2,1)S(1)} %get-tuple-element.96), channel_id=1, source_target_pairs={{0,30},{1,31},{2,28},{3,29},{4,26},{5,27},{6,24},{7,25},{8,22},{9,... | collective-permute-start | bytes 245768 | tf_op jit(solution)/shard_map/ppermute | solution.py:684
  19.7 12.4 %copy-start.2 = (s32[16,2]{0,1:T(2,128)S(1)}, s32[16,2]{0,1:T(2,128)}, u32[]{:S(2)}) copy-start(s32[16,2]{0,1:T(2,128)} %param.14) | copy-start | bytes 388
  19.7 12.4 %collective-permute-start.8 = (bf16[64,640]{1,0:T(8,128)(2,1)S(1)}, bf16[64,640]{1,0:T(8,128)(2,1)S(1)}, u32[]{:S(2)}, u32[]{:S(2)}) collective-permute-start(bf16[64,640]{1,0:T(8,128)(2,1)S(1)} %get-tuple-element.104), channel_id=1, source_target_pairs={{0,2},{1,3},{2,4},{3,5},{4,6},{5,7},{6,8},{7,9},{8,10},{9,11},{10,... | collective-permute-start | bytes 245768 | tf_op jit(solution)/shard_map/ppermute | solution.py:684
  24.2 7.9 %collective-permute-start.9 = (bf16[64,640]{1,0:T(8,128)(2,1)S(1)}, bf16[64,640]{1,0:T(8,128)(2,1)S(1)}, u32[]{:S(2)}, u32[]{:S(2)}) collective-permute-start(bf16[64,640]{1,0:T(8,128)(2,1)S(1)} %get-tuple-element.105), channel_id=1, source_target_pairs={{0,3},{1,2},{2,5},{3,4},{4,7},{5,6},{6,9},{7,8},{8,11},{9,10},{10,... | collective-permute-start | bytes 245768 | tf_op jit(solution)/shard_map/ppermute | solution.py:684
  26.3 10.1 %collective-permute-start.7 = (bf16[128,640]{1,0:T(8,128)(2,1)S(1)}, bf16[128,640]{1,0:T(8,128)(2,1)S(1)}, u32[]{:S(2)}, u32[]{:S(2)}) collective-permute-start(bf16[128,640]{1,0:T(8,128)(2,1)S(1)} %get-tuple-element.103), channel_id=1, source_target_pairs={{0,1},{1,0},{2,3},{3,2},{4,5},{5,4},{6,7},{7,6},{8,9},{9,8},{10,11... | collective-permute-start | bytes 491528 | tf_op jit(solution)/shard_map/ppermute | solution.py:684
  27.6 8.8 %collective-permute-start.6 = (bf16[64,640]{1,0:T(8,128)(2,1)S(1)}, bf16[64,640]{1,0:T(8,128)(2,1)S(1)}, u32[]{:S(2)}, u32[]{:S(2)}) collective-permute-start(bf16[64,640]{1,0:T(8,128)(2,1)S(1)} %get-tuple-element.102.refs_8_), channel_id=1, source_target_pairs={{0,31},{1,30},{2,1},{3,0},{4,3},{5,2},{6,5},{7,4},{8,7},{9,6},{10,... | collective-permute-start | bytes 245768 | tf_op jit(solution)/shard_map/ppermute | solution.py:684
  31.7 4.8 %collective-permute-start.5 = (bf16[64,640]{1,0:T(8,128)(2,1)S(1)}, bf16[64,640]{1,0:T(8,128)(2,1)S(1)}, u32[]{:S(2)}, u32[]{:S(2)}) collective-permute-start(bf16[64,640]{1,0:T(8,128)(2,1)S(1)} %get-tuple-element.102.refs_8_), channel_id=1, source_target_pairs={{0,30},{1,31},{2,0},{3,1},{4,2},{5,3},{6,4},{7,5},{8,6},{9,7},{10,... | collective-permute-start | bytes 245768 | tf_op jit(solution)/shard_map/ppermute | solution.py:684
  34.0 6.0 %collective-permute-start.12 = (bf16[96,640]{1,0:T(8,128)(2,1)S(1)}, bf16[96,640]{1,0:T(8,128)(2,1)S(1)}, u32[]{:S(2)}, u32[]{:S(2)}) collective-permute-start(bf16[96,640]{1,0:T(8,128)(2,1)S(1)} %get-tuple-element.120), channel_id=1, source_target_pairs={{0,1},{1,0},{2,3},{3,2},{4,5},{5,4},{6,7},{7,6},{8,9},{9,8},{10,11... | collective-permute-start | bytes 368648 | tf_op jit(solution)/shard_map/ppermute | solution.py:684
  35.0 5.0 %collective-permute-start.11 = (bf16[64,640]{1,0:T(8,128)(2,1)S(1)}, bf16[64,640]{1,0:T(8,128)(2,1)S(1)}, u32[]{:S(2)}, u32[]{:S(2)}) collective-permute-start(bf16[64,640]{1,0:T(8,128)(2,1)S(1)} %get-tuple-element.117), channel_id=1, source_target_pairs={{0,0},{1,1},{2,30},{3,31},{4,28},{5,29},{6,26},{7,27},{8,24},{9,25... | collective-permute-start | bytes 245768 | tf_op jit(solution)/shard_map/ppermute | solution.py:684
  35.8 0.7 %copy-start.3 = (s32[16,2]{0,1:T(2,128)S(1)}, s32[16,2]{0,1:T(2,128)}, u32[]{:S(2)}) copy-start(s32[16,2]{0,1:T(2,128)} %param.15) | copy-start | bytes 388
  38.8 6.7 %collective-permute-start.10 = (bf16[128,640]{1,0:T(8,128)(2,1)S(1)}, bf16[128,640]{1,0:T(8,128)(2,1)S(1)}, u32[]{:S(2)}, u32[]{:S(2)}) collective-permute-start(bf16[128,640]{1,0:T(8,128)(2,1)S(1)} %get-tuple-element.115), channel_id=1, source_target_pairs={{0,1},{1,0},{2,3},{3,2},{4,5},{5,4},{6,7},{7,6},{8,9},{9,8},{10,11... | collective-permute-start | bytes 491528 | tf_op jit(solution)/shard_map/ppermute | solution.py:684
  41.8 5.5 %collective-permute-start.13 = (bf16[128,480]{1,0:T(8,128)(2,1)S(1)}, bf16[128,480]{1,0:T(8,128)(2,1)S(1)}, u32[]{:S(2)}, u32[]{:S(2)}) collective-permute-start(bf16[128,480]{1,0:T(8,128)(2,1)S(1)} %get-tuple-element.129), channel_id=1, source_target_pairs={{0,1},{1,0},{2,3},{3,2},{4,5},{5,4},{6,7},{7,6},{8,9},{9,8},{10,11... | collective-permute-start | bytes 368648 | tf_op jit(solution)/shard_map/ppermute | solution.py:684
  47.4 15.3 %collective-permute-start.16 = (bf16[128,480]{1,0:T(8,128)(2,1)S(1)}, bf16[128,480]{1,0:T(8,128)(2,1)S(1)}, u32[]{:S(2)}, u32[]{:S(2)}) collective-permute-start(bf16[128,480]{1,0:T(8,128)(2,1)S(1)} %get-tuple-element.136), channel_id=1, source_target_pairs={{0,1},{1,0},{2,3},{3,2},{4,5},{5,4},{6,7},{7,6},{8,9},{9,8},{10,11... | collective-permute-start | bytes 368648 | tf_op jit(solution)/shard_map/ppermute | solution.py:684
  49.1 13.6 %collective-permute-start.15 = (bf16[128,320]{1,0:T(8,128)(2,1)S(1)}, bf16[128,320]{1,0:T(8,128)(2,1)S(1)}, u32[]{:S(2)}, u32[]{:S(2)}) collective-permute-start(bf16[128,320]{1,0:T(8,128)(2,1)S(1)} %get-tuple-element.133), channel_id=1, source_target_pairs={{0,30},{1,31},{2,28},{3,29},{4,26},{5,27},{6,24},{7,25},{8,22},{9,... | collective-permute-start | bytes 245768 | tf_op jit(solution)/shard_map/ppermute | solution.py:684
  52.5 10.2 %collective-permute-start.14 = (bf16[128,320]{1,0:T(8,128)(2,1)S(1)}, bf16[128,320]{1,0:T(8,128)(2,1)S(1)}, u32[]{:S(2)}, u32[]{:S(2)}) collective-permute-start(bf16[128,320]{1,0:T(8,128)(2,1)S(1)} %get-tuple-element.131.refs_9_.refs_6_), channel_id=1, source_target_pairs={{0,2},{1,3},{2,4},{3,5},{4,6},{5,7},{6,8},{7,9},{8,10},{9,11},{10,... | collective-permute-start | bytes 245768 | tf_op jit(solution)/shard_map/ppermute | solution.py:684
  54.9 6.9 %collective-permute-start.17 = (bf16[32,640]{1,0:T(8,128)(2,1)S(1)}, bf16[32,640]{1,0:T(8,128)(2,1)S(1)}, u32[]{:S(2)}, u32[]{:S(2)}) collective-permute-start(bf16[32,640]{1,0:T(8,128)(2,1)S(1)} %get-tuple-element.137), channel_id=1, source_target_pairs={{0,30},{1,31},{2,0},{3,1},{4,2},{5,3},{6,4},{7,5},{8,6},{9,7},{10,... | collective-permute-start | bytes 122888 | tf_op jit(solution)/shard_map/ppermute | solution.py:684
  59.2 3.4 %collective-permute-start.18 = (bf16[32,640]{1,0:T(8,128)(2,1)S(1)}, bf16[32,640]{1,0:T(8,128)(2,1)S(1)}, u32[]{:S(2)}, u32[]{:S(2)}) collective-permute-start(bf16[32,640]{1,0:T(8,128)(2,1)S(1)} %get-tuple-element.138), channel_id=1, source_target_pairs={{0,31},{1,30},{2,1},{3,0},{4,3},{5,2},{6,5},{7,4},{8,7},{9,6},{10,... | collective-permute-start | bytes 122888 | tf_op jit(solution)/shard_map/ppermute | solution.py:684

commit v3 on v2

--- a/solution.py
+++ b/solution.py
@@ -810,13 +810,22 @@
     )
     rows1 = exchange(sends)
     part_i = add_grads(0, sum_i, act_i1, g_pad1, (sends[0],))
+    *dh_sends, f_pad1, act_h1 = run(
+        last_backward,
+        (fs, bs),
+        (q1, *q_received, g_pad1, heads[0], *sums, h0, kernels),
+        [((local // FOLD, FOLD * w), BF)] * n + [(padded, BF), (half, BF)],
+        [pltpu.VMEM(half, BF), pltpu.VMEM(half, BF), wide_line],
+        after=(part_i,),
+    )
+    dh1_in = [backward(x, d) for d, x in enumerate(dh_sends)]
     packed = run(
         pack_rows,
         (),
         (full0, mir_in),
         [((local, c + w), BF)] * n,
         [pltpu.VMEM(half, BF)],
-        after=(part_i,),
+        after=(act_h1,),
     )
     token, *written = run(
         write_queues,
@@ -831,21 +840,12 @@
     out1, mirror1, i1 = run(
         add_rows,
         (),
-        (*rows1, q1, *q_received),
+        (*rows1, *held_until([q1], dh1_in), *q_received),
         [(rows, BF)] * 3,
         [pltpu.VMEM(wide, F32)],
         after=(token,),
     )
     fwd1, mir1 = onward(out1, 0), mirrored(mirror1, 0)
-    *dh_sends, f_pad1, act_h1 = run(
-        last_backward,
-        (fs, bs),
-        (q1, *q_received, g_pad1, heads[0], *sums, h0, kernels),
-        [((local // FOLD, FOLD * w), BF)] * n + [(padded, BF), (half, BF)],
-        [pltpu.VMEM(half, BF), pltpu.VMEM(half, BF), wide_line],
-        after=(out1,),
-    )
-    dh1_in = [backward(x, d) for d, x in enumerate(dh_sends)]
     token, grad_total = run(
         kernel_grads_last,
         (),
@@ -853,6 +853,7 @@
         [((8, 128), F32), ((18, w, c), F32)],
         [pltpu.VMEM((9, w, c), F32), sems((10,))],
         far_outs=1,
+        after=(out1,),
     )
     fwd_out, bwd_out, mir_out, stash_out, emitted = run(
         finish,

time: 64.5 us -> 70.7 us (1.096)
  waiting for transfers between devices: 6.43 us -> 17.1 us
  starting transfers between devices: 32.1 us -> 27.6 us
    ppermute x19, waiting for transfers between devices: 6.43 us -> 17.1 us  [move(): return lax.ppermute(x, ('section', 'row'), route)]
    ppermute x19, starting transfers between devices: 32.1 us -> 27.6 us  [move(): return lax.ppermute(x, ('section', 'row'), route)]
  transfers between devices with their start and end apart: 19 -> 19, of which waited for: 5 -> 9; matrix products, arithmetic and copies ran while one was open for 0% -> 0% of each run, Pallas kernels for 33% -> 28%
where the time goes in v3:
time: 70.7 us; the launch traced here: 70.5 us
  starting transfers between devices  27.6 us (39%)
  Pallas kernels  24.7 us (35%)
  waiting for transfers between devices  17.1 us (24%)
  between operations  1.01 us (1%)
    ppermute x19, starting transfers between devices, move(): return lax.ppermute(x, ('section', 'row'), route)  27.6 us
    pallas_call x18, Pallas kernels, call(): pl.pallas_call(inner, name=name, out_shape=[jax.ShapeDtypeStruct(shape, d...  24.7 us
    ppermute x19, waiting for transfers between devices, move(): return lax.ppermute(x, ('section', 'row'), route)  17.1 us
  transfers between devices with their start and end apart: 19, of which 9 were waited for; matrix products, arithmetic and copies ran while one was open for 0% of the time, Pallas kernels for 28%

profile of v3, /device:TPU:0, one launch (start us, length us, event | category | flops | bytes accessed | tf_op | source)
XLA Modules:
  0.0 70.5 jit_solution(7393023359350455173)
XLA Ops:
  0.6 1.7 %pack_first.1 = (bf16[32,640]{1,0:T(8,128)(2,1)S(1)}, bf16[32,640]{1,0:T(8,128)(2,1)S(1)}, bf16[3,128,320]{2,1,0:T(8,128)(2,1)S(1)}, bf16[3,128,320]{2,1,0:T(8,1...) custom-call(s32[2,16]{1,0:T(2,128)} %bitcast.24, s32[2,16]{1,0:T(2,128)} %bitcast.32, ...), custom_call_target="tpu_custom_call" | custom-call | flops 1 | bytes 1 | tf_op jit(solution)/shard_map/pack_first/pallas_call | solution.py:202
  2.4 3.0 %collective-permute-start = (bf16[32,640]{1,0:T(8,128)(2,1)S(1)}, bf16[32,640]{1,0:T(8,128)(2,1)S(1)}, u32[]{:S(2)}, u32[]{:S(2)}) collective-permute-start(bf16[32,640]{1,0:T(8,128)(2,1)S(1)} %get-tuple-element.85), channel_id=1, source_target_pairs={{0,1},{1,0},{2,3},{3,2},{4,5},{5,4},{6,7},{7,6},{8,9},{9,8},{10,11... | collective-permute-start | bytes 122888 | tf_op jit(solution)/shard_map/ppermute | solution.py:684
  5.4 1.2 %pack_later.1 = (bf16[128,640]{1,0:T(8,128)(2,1)S(1)}, bf16[128,640]{1,0:T(8,128)(2,1)S(1)}, bf16[64,640]{1,0:T(8,128)(2,1)S(1)}, bf16[64,640]{1,0:T(8,128)(2,1)...) custom-call(s32[2,16]{1,0:T(2,128)} %bitcast.25, ...), custom_call_target="tpu_custom_call" | custom-call | flops 1 | bytes 1 | tf_op jit(solution)/shard_map/pack_later/pallas_call | solution.py:202
  6.6 0.7 %collective-permute-done.refs_1_ = bf16[32,640]{1,0:T(8,128)(2,1)S(1)} collective-permute-done((bf16[32,640]{1,0:T(8,128)(2,1)S(1)}, bf16[32,640]{1,0:T(8,128)(2,1)S(1)}, u32[]{:S(2)}, u32[]{:S(2)}) %collective-permute-start) | collective-permute-done | bytes 40992 | tf_op jit(solution)/shard_map/ppermute | solution.py:684
  7.4 2.0 %collective-permute-start.1 = (bf16[128,640]{1,0:T(8,128)(2,1)S(1)}, bf16[128,640]{1,0:T(8,128)(2,1)S(1)}, u32[]{:S(2)}, u32[]{:S(2)}) collective-permute-start(bf16[128,640]{1,0:T(8,128)(2,1)S(1)} %get-tuple-element.87), channel_id=1, source_target_pairs={{0,1},{1,0},{2,3},{3,2},{4,5},{5,4},{6,7},{7,6},{8,9},{9,8},{10,11... | collective-permute-start | bytes 491528 | tf_op jit(solution)/shard_map/ppermute | solution.py:684
  9.4 1.3 %first_forward.1 = (f32[256,160]{1,0:T(8,128)S(1)}, bf16[256,160]{1,0:T(8,128)(2,1)S(1)}, bf16[128,640]{1,0:T(8,128)(2,1)S(1)}) custom-call(bf16[32,640]{1,0:T(8,128)(2,1)S(1)} %get-tuple-element.82.refs_6_.refs_0_, bf16[32,640]{1,0:T(8,128)(2,1)S(1)} %collective-permute-done.refs_1_, bf16[64,640]{1,0:T(8,128)(2,1)S(1)} %get-tuple-element.90.refs_2_.refs_3_.refs_5_, ...), custom_call_target="tpu_custom_call" | custom-call | flops 1 | bytes 1 | tf_op jit(solution)/shard_map/first_forward/pallas_call | solution.py:202
  10.7 0.1 collective-permute-start.3
  10.8 2.9 %collective-permute-done.1.refs_1_.refs_4_ = bf16[128,640]{1,0:T(8,128)(2,1)S(1)} collective-permute-done((bf16[128,640]{1,0:T(8,128)(2,1)S(1)}, bf16[128,640]{1,0:T(8,128)(2,1)S(1)}, u32[]{:S(2)}, u32[]{:S(2)}) %collective-permute-start.1) | collective-permute-done | bytes 163872 | tf_op jit(solution)/shard_map/ppermute | solution.py:684
  13.7 1.4 %first_backward.1 = (bf16[256,160]{1,0:T(8,128)(2,1)S(1)}, bf16[64,640]{1,0:T(8,128)(2,1)S(1)}, bf16[3,320,320]{2,1,0:T(8,128)(2,1)S(1)}, bf16[256,160]{1,0:T(8,128)(2,1)S(1)}, bf16[128,640]{1,0:T(8,128)(2,1)S(1)}) custom-call(bf16[128,640]{1,0:T(8,128)(2,1)S(1)} %get-tuple-element.86.refs_0_.refs_3_, ...), custom_call_target="tpu_custom_call" | custom-call | flops 1 | bytes 1 | tf_op jit(solution)/shard_map/first_backward/pallas_call | solution.py:202
  15.1 2.3 %collective-permute-start.2 = (bf16[128,640]{1,0:T(8,128)(2,1)S(1)}, bf16[128,640]{1,0:T(8,128)(2,1)S(1)}, u32[]{:S(2)}, u32[]{:S(2)}) collective-permute-start(bf16[128,640]{1,0:T(8,128)(2,1)S(1)} %get-tuple-element.94), channel_id=1, source_target_pairs={{0,1},{1,0},{2,3},{3,2},{4,5},{5,4},{6,7},{7,6},{8,9},{9,8},{10,11... | collective-permute-start | bytes 491528 | tf_op jit(solution)/shard_map/ppermute | solution.py:684
  17.4 0.2 collective-permute-start.4
  17.6 0.6 kernel_grads_add_9.1.refs_6_.refs_0_
  18.2 1.4 %second_forward.1 = (bf16[256,160]{1,0:T(8,128)(2,1)S(1)}, bf16[256,320]{1,0:T(8,128)(2,1)S(1)}, bf16[64,640]{1,0:T(8,128)(2,1)S(1)}, bf16[64,640]{1,0:T(8,128)(2,1)S(1)}) custom-call(f32[256,160]{1,0:T(8,128)S(1)} %get-tuple-element.92.refs_5_.refs_0_, bf16[128,640]{1,0:T(8,128)(2,1)S(1)} %collective-permute-done.3.refs_1_.refs_4_.refs_6_, ...), custom_call_target="tpu_custom_call" | custom-call | flops 1 | bytes 1 | tf_op jit(solution)/shard_map/second_forward/pallas_call | solution.py:202
  19.7 0.0 copy-start.2
  19.7 5.0 %collective-permute-done.4.refs_5_.refs_4_ = bf16[64,640]{1,0:T(8,128)(2,1)S(1)} collective-permute-done((bf16[64,640]{1,0:T(8,128)(2,1)S(1)}, bf16[64,640]{1,0:T(8,128)(2,1)S(1)}, u32[]{:S(2)}, u32[]{:S(2)}) %collective-permute-start.4) | collective-permute-done | bytes 81952 | tf_op jit(solution)/shard_map/ppermute | solution.py:684
  24.7 1.6 %second_backward.1 = (bf16[64,640]{1,0:T(8,128)(2,1)S(1)}, bf16[3,320,320]{2,1,0:T(8,128)(2,1)S(1)}, bf16[256,160]{1,0:T(8,128)(2,1)S(1)}, bf16[128,640]{1,0:T(8,128)(2,1)S(1)}) custom-call(bf16[256,160]{1,0:T(8,128)(2,1)S(1)} %get-tuple-element.93.refs_3_.refs_0_, bf16[128,640]{1,0:T(8,128)(2,1)S(1)} %collective-permute-done.2.refs_1_.refs_4_.refs_8_, ...), custom_call_target="tpu_custom_call" | custom-call | flops 1 | bytes 1 | tf_op jit(solution)/shard_map/second_backward/pallas_call | solution.py:202
  26.3 0.1 collective-permute-start.7
  26.4 0.2 collective-permute-start.8
  26.6 2.8 %collective-permute-start.9 = (bf16[64,640]{1,0:T(8,128)(2,1)S(1)}, bf16[64,640]{1,0:T(8,128)(2,1)S(1)}, u32[]{:S(2)}, u32[]{:S(2)}) collective-permute-start(bf16[64,640]{1,0:T(8,128)(2,1)S(1)} %get-tuple-element.106), channel_id=1, source_target_pairs={{0,3},{1,2},{2,5},{3,4},{4,7},{5,6},{6,9},{7,8},{8,11},{9,10},{10,... | collective-permute-start | bytes 245768 | tf_op jit(solution)/shard_map/ppermute | solution.py:684
  29.3 3.0 %collective-permute-start.6 = (bf16[64,640]{1,0:T(8,128)(2,1)S(1)}, bf16[64,640]{1,0:T(8,128)(2,1)S(1)}, u32[]{:S(2)}, u32[]{:S(2)}) collective-permute-start(bf16[64,640]{1,0:T(8,128)(2,1)S(1)} %get-tuple-element.103.refs_8_), channel_id=1, source_target_pairs={{0,31},{1,30},{2,1},{3,0},{4,3},{5,2},{6,5},{7,4},{8,7},{9,6},{10,... | collective-permute-start | bytes 245768 | tf_op jit(solution)/shard_map/ppermute | solution.py:684
  32.3 0.3 collective-permute-start.5
  32.6 0.4 collective-permute-done.8.refs_1_
  33.0 2.4 %collective-permute-done.9.refs_2_ = bf16[64,640]{1,0:T(8,128)(2,1)S(1)} collective-permute-done((bf16[64,640]{1,0:T(8,128)(2,1)S(1)}, bf16[64,640]{1,0:T(8,128)(2,1)S(1)}, u32[]{:S(2)}, u32[]{:S(2)}) %collective-permute-start.9) | collective-permute-done | bytes 81952 | tf_op jit(solution)/shard_map/ppermute | solution.py:684
  35.5 1.9 %later_forward.1 = (f32[256,160]{1,0:T(8,128)S(1)}, bf16[256,160]{1,0:T(8,128)(2,1)S(1)}, bf16[256,160]{1,0:T(8,128)(2,1)S(1)}, bf16[64,640]{1,0:T(8,128)(2,1)S(1)}, bf16[96,640]{1,0:T(8,128)(2,1)S(1)}) custom-call(s32[2,16]{1,0:T(2,128)S(1)} %bitcast.26, bf16[64,640]{1,0:T(8,128)(2,1)S(1)} %collective-permute-done.8.refs_1_, ...), custom_call_target="tpu_custom_call" | custom-call | flops 1 | bytes 1 | tf_op jit(solution)/shard_map/later_forward/pallas_call | solution.py:202
  37.4 0.7 collective-permute-start.12
  38.0 0.8 %collective-permute-start.11 = (bf16[64,640]{1,0:T(8,128)(2,1)S(1)}, bf16[64,640]{1,0:T(8,128)(2,1)S(1)}, u32[]{:S(2)}, u32[]{:S(2)}) collective-permute-start(bf16[64,640]{1,0:T(8,128)(2,1)S(1)} %get-tuple-element.118), channel_id=1, source_target_pairs={{0,0},{1,1},{2,30},{3,31},{4,28},{5,29},{6,26},{7,27},{8,24},{9,25... | collective-permute-start | bytes 245768 | tf_op jit(solution)/shard_map/ppermute | solution.py:684
  38.9 0.0 copy-start.3
  38.9 0.6 kernel_grads_add_0.2.refs_12_.refs_0_
  39.5 0.0 copy-done.3
  39.6 2.3 %later_backward.1 = (bf16[256,160]{1,0:T(8,128)(2,1)S(1)}, bf16[3,320,320]{2,1,0:T(8,128)(2,1)S(1)}, bf16[256,160]{1,0:T(8,128)(2,1)S(1)}, bf16[256,320]{1,0:T(8...) custom-call(s32[2,16]{1,0:T(2,128)S(1)} %bitcast.27, ...), custom_call_target="tpu_custom_call" | custom-call | flops 1 | bytes 1 | tf_op jit(solution)/shard_map/later_backward/pallas_call | solution.py:202
  41.9 1.5 %collective-permute-start.10 = (bf16[128,640]{1,0:T(8,128)(2,1)S(1)}, bf16[128,640]{1,0:T(8,128)(2,1)S(1)}, u32[]{:S(2)}, u32[]{:S(2)}) collective-permute-start(bf16[128,640]{1,0:T(8,128)(2,1)S(1)} %get-tuple-element.116), channel_id=1, source_target_pairs={{0,1},{1,0},{2,3},{3,2},{4,5},{5,4},{6,7},{7,6},{8,9},{9,8},{10,11... | collective-permute-start | bytes 491528 | tf_op jit(solution)/shard_map/ppermute | solution.py:684
  43.4 1.8 %last_forward.1 = (bf16[128,480]{1,0:T(8,128)(2,1)S(1)}, bf16[128,480]{1,0:T(8,128)(2,1)S(1)}) custom-call(s32[2,16]{1,0:T(2,128)S(1)} %bitcast.28, f32[256,160]{1,0:T(8,128)S(1)} %get-tuple-element.112.refs_3_.refs_1_, bf16[96,640]{1,0:T(8,128)(2,1)S(1)} %collective-permute-done.12.refs_2_, bf16[256,160]{1,0:T(8,128)(2,1)S(1)} %get-tuple-element.123.refs_3_, ...), custom_call_target="tpu_custom_call" | custom-call | flops 1 | bytes 1 | tf_op jit(solution)/shard_map/last_forward/pallas_call | solution.py:202
  45.2 0.7 collective-permute-start.13
  45.9 0.6 kernel_grads_add_0.3.refs_9_.refs_1_
  46.5 0.7 %collective-permute-done.10.refs_3_.refs_9_ = bf16[128,640]{1,0:T(8,128)(2,1)S(1)} collective-permute-done((bf16[128,640]{1,0:T(8,128)(2,1)S(1)}, bf16[128,640]{1,0:T(8,128)(2,1)S(1)}, u32[]{:S(2)}, u32[]{:S(2)}) %collective-permute-start.10) | collective-permute-done | bytes 163872 | tf_op jit(solution)/shard_map/ppermute | solution.py:684
  47.3 2.3 %last_backward.1 = (bf16[32,640]{1,0:T(8,128)(2,1)S(1)}, bf16[32,640]{1,0:T(8,128)(2,1)S(1)}, bf16[3,320,320]{2,1,0:T(8,128)(2,1)S(1)}, bf16[256,160]{1,0:T(8,128)(2,1)S(1)}) custom-call(s32[2,16]{1,0:T(2,128)S(1)} %bitcast.29, s32[2,16]{1,0:T(2,128)S(1)} %bitcast.35, bf16[256,160]{1,0:T(8,128)(2,1)S(1)} %get-tuple-element.134.refs_7_.refs_2_, ...), custom_call_target="tpu_custom_call" | custom-call | flops 1 | bytes 1 | tf_op jit(solution)/shard_map/last_backward/pallas_call | solution.py:202
  49.6 5.0 %collective-permute-start.14 = (bf16[32,640]{1,0:T(8,128)(2,1)S(1)}, bf16[32,640]{1,0:T(8,128)(2,1)S(1)}, u32[]{:S(2)}, u32[]{:S(2)}) collective-permute-start(bf16[32,640]{1,0:T(8,128)(2,1)S(1)} %get-tuple-element.132), channel_id=1, source_target_pairs={{0,30},{1,31},{2,0},{3,1},{4,2},{5,3},{6,4},{7,5},{8,6},{9,7},{10,... | collective-permute-start | bytes 122888 | tf_op jit(solution)/shard_map/ppermute | solution.py:684
  54.5 0.3 collective-permute-start.15
  54.9 0.2 pack_rows.1
  55.1 1.8 %write_queues.1 = (f32[8,128]{1,0:T(8,128)S(1)}, bf16[3,128,320]{2,1,0:T(8,128)(2,1)}, bf16[3,128,320]{2,1,0:T(8,128)(2,1)}, bf16[3,128,320]{2,1,0:T(8,128)(2,1)}, bf16[6,128,320]{2,1,0:T(8,128)(2,1)}) custom-call(s32[2,16]{1,0:T(2,128)S(1)} %bitcast.30, s32[2,16]{1,0:T(2,128)S(1)} %bitcast.36, bf16[3,128,320]{2,1,0:T(8,128)(2,1)S(1)} %get-tuple-element.78.refs_2_, ...), custom_call_target="tpu_custom_call" | custom-call | flops 1 | bytes 1 | tf_op jit(solution)/shard_map/write_queues/pallas_call | solution.py:202
  56.9 1.3 %collective-permute-start.18 = (bf16[128,480]{1,0:T(8,128)(2,1)S(1)}, bf16[128,480]{1,0:T(8,128)(2,1)S(1)}, u32[]{:S(2)}, u32[]{:S(2)}) collective-permute-start(bf16[128,480]{1,0:T(8,128)(2,1)S(1)} %get-tuple-element.141), channel_id=1, source_target_pairs={{0,1},{1,0},{2,3},{3,2},{4,5},{5,4},{6,7},{7,6},{8,9},{9,8},{10,11... | collective-permute-start | bytes 368648 | tf_op jit(solution)/shard_map/ppermute | solution.py:684
  58.2 0.2 collective-permute-done.15.refs_13_
  58.4 0.2 add_rows.1
  58.6 3.4 %collective-permute-start.17 = (bf16[128,320]{1,0:T(8,128)(2,1)S(1)}, bf16[128,320]{1,0:T(8,128)(2,1)S(1)}, u32[]{:S(2)}, u32[]{:S(2)}) collective-permute-start(bf16[128,320]{1,0:T(8,128)(2,1)S(1)} %get-tuple-element.138), channel_id=1, source_target_pairs={{0,30},{1,31},{2,28},{3,29},{4,26},{5,27},{6,24},{7,25},{8,22},{9,... | collective-permute-start | bytes 245768 | tf_op jit(solution)/shard_map/ppermute | solution.py:684
  62.0 2.2 %kernel_grads_last.1 = (f32[8,128]{1,0:T(8,128)S(1)}, f32[18,160,320]{2,1,0:T(8,128)}) custom-call(f32[9,160,320]{2,1,0:T(8,128)S(1)} %kernel_grads_add_0.2.refs_12_.refs_0_, f32[9,160,320]{2,1,0:T(8,128)S(1)} %kernel_grads_add_0.3.refs_9_.refs_1_, bf16[256,160]{1,0:T(8,128)(2,1)S(1)} %get-tuple-element.125.refs_2_, ...), custom_call_target="tpu_custom_call" | custom-call | flops 1 | bytes 1 | tf_op jit(solution)/shard_map/kernel_grads_last/pallas_call | solution.py:202
  64.2 2.0 %collective-permute-done.17.refs_9_ = bf16[128,320]{1,0:T(8,128)(2,1)S(1)} collective-permute-done((bf16[128,320]{1,0:T(8,128)(2,1)S(1)}, bf16[128,320]{1,0:T(8,128)(2,1)S(1)}, u32[]{:S(2)}, u32[]{:S(2)}) %collective-permute-start.17) | collective-permute-done | bytes 81952 | tf_op jit(solution)/shard_map/ppermute | solution.py:684
  66.2 2.6 %collective-permute-done.16.refs_8_ = bf16[128,320]{1,0:T(8,128)(2,1)S(1)} collective-permute-done((bf16[128,320]{1,0:T(8,128)(2,1)S(1)}, bf16[128,320]{1,0:T(8,128)(2,1)S(1)}, u32[]{:S(2)}, u32[]{:S(2)}) %collective-permute-start.16) | collective-permute-done | bytes 81952 | tf_op jit(solution)/shard_map/ppermute | solution.py:684
  68.9 1.5 %finish.1 = (bf16[3,128,320]{2,1,0:T(8,128)(2,1)}, bf16[3,128,320]{2,1,0:T(8,128)(2,1)}, bf16[3,128,320]{2,1,0:T(8,128)(2,1)}, bf16[6,128,320]{2,1,0:T(8,128)(2,1)}, bf16[2,128,320]{2,1,0:T(8,128)(2,1)}) custom-call(s32[2,16]{1,0:T(2,128)S(1)} %bitcast.31, ...), custom_call_target="tpu_custom_call", output_to_operand_aliasing={{0}: (2, {}), {1}: (3, {}), {2}: (4, {}), {3}: (5, {})} | custom-call | flops 1 | bytes 1 | tf_op jit(solution)/shard_map/finish/pallas_call | solution.py:202
  (16 shorter events, 0.0 us)
Async XLA Ops:
  0.6 8.8 %copy-start = (bf16[1,2,3,3,160,320]{5,4,3,2,1,0:T(8,128)(2,1)S(1)}, bf16[1,2,3,3,160,320]{5,4,3,2,1,0:T(8,128)(2,1)}, u32[]{:S(2)}) copy-start(bf16[1,2,3,3,160,320]{5,4,3,2,1,0:T(8,128)(2,1)} %param.12) | copy-start | bytes 5529604
  2.4 5.0 %collective-permute-start = (bf16[32,640]{1,0:T(8,128)(2,1)S(1)}, bf16[32,640]{1,0:T(8,128)(2,1)S(1)}, u32[]{:S(2)}, u32[]{:S(2)}) collective-permute-start(bf16[32,640]{1,0:T(8,128)(2,1)S(1)} %get-tuple-element.85), channel_id=1, source_target_pairs={{0,1},{1,0},{2,3},{3,2},{4,5},{5,4},{6,7},{7,6},{8,9},{9,8},{10,11... | collective-permute-start | bytes 122888 | tf_op jit(solution)/shard_map/ppermute | solution.py:684
  7.4 6.3 %collective-permute-start.1 = (bf16[128,640]{1,0:T(8,128)(2,1)S(1)}, bf16[128,640]{1,0:T(8,128)(2,1)S(1)}, u32[]{:S(2)}, u32[]{:S(2)}) collective-permute-start(bf16[128,640]{1,0:T(8,128)(2,1)S(1)} %get-tuple-element.87), channel_id=1, source_target_pairs={{0,1},{1,0},{2,3},{3,2},{4,5},{5,4},{6,7},{7,6},{8,9},{9,8},{10,11... | collective-permute-start | bytes 491528 | tf_op jit(solution)/shard_map/ppermute | solution.py:684
  9.4 8.2 %copy-start.1 = (f32[1,2,3,3,160,320]{5,4,3,2,1,0:T(8,128)S(1)}, f32[1,2,3,3,160,320]{5,4,3,2,1,0:T(8,128)}, u32[]{:S(2)}) copy-start(f32[1,2,3,3,160,320]{5,4,3,2,1,0:T(8,128)} %param.13) | copy-start | bytes 11059204
  10.7 7.5 %collective-permute-start.3 = (bf16[128,640]{1,0:T(8,128)(2,1)S(1)}, bf16[128,640]{1,0:T(8,128)(2,1)S(1)}, u32[]{:S(2)}, u32[]{:S(2)}) collective-permute-start(bf16[128,640]{1,0:T(8,128)(2,1)S(1)} %get-tuple-element.96), channel_id=1, source_target_pairs={{0,1},{1,0},{2,3},{3,2},{4,5},{5,4},{6,7},{7,6},{8,9},{9,8},{10,11... | collective-permute-start | bytes 491528 | tf_op jit(solution)/shard_map/ppermute | solution.py:684
  15.1 9.6 %collective-permute-start.2 = (bf16[128,640]{1,0:T(8,128)(2,1)S(1)}, bf16[128,640]{1,0:T(8,128)(2,1)S(1)}, u32[]{:S(2)}, u32[]{:S(2)}) collective-permute-start(bf16[128,640]{1,0:T(8,128)(2,1)S(1)} %get-tuple-element.94), channel_id=1, source_target_pairs={{0,1},{1,0},{2,3},{3,2},{4,5},{5,4},{6,7},{7,6},{8,9},{9,8},{10,11... | collective-permute-start | bytes 491528 | tf_op jit(solution)/shard_map/ppermute | solution.py:684
  17.4 7.2 %collective-permute-start.4 = (bf16[64,640]{1,0:T(8,128)(2,1)S(1)}, bf16[64,640]{1,0:T(8,128)(2,1)S(1)}, u32[]{:S(2)}, u32[]{:S(2)}) collective-permute-start(bf16[64,640]{1,0:T(8,128)(2,1)S(1)} %get-tuple-element.97), channel_id=1, source_target_pairs={{0,30},{1,31},{2,28},{3,29},{4,26},{5,27},{6,24},{7,25},{8,22},{9,... | collective-permute-start | bytes 245768 | tf_op jit(solution)/shard_map/ppermute | solution.py:684
  19.7 15.8 %copy-start.2 = (s32[16,2]{0,1:T(2,128)S(1)}, s32[16,2]{0,1:T(2,128)}, u32[]{:S(2)}) copy-start(s32[16,2]{0,1:T(2,128)} %param.14) | copy-start | bytes 388
  26.3 13.2 %collective-permute-start.7 = (bf16[128,640]{1,0:T(8,128)(2,1)S(1)}, bf16[128,640]{1,0:T(8,128)(2,1)S(1)}, u32[]{:S(2)}, u32[]{:S(2)}) collective-permute-start(bf16[128,640]{1,0:T(8,128)(2,1)S(1)} %get-tuple-element.104), channel_id=1, source_target_pairs={{0,1},{1,0},{2,3},{3,2},{4,5},{5,4},{6,7},{7,6},{8,9},{9,8},{10,11... | collective-permute-start | bytes 491528 | tf_op jit(solution)/shard_map/ppermute | solution.py:684
  26.4 6.6 %collective-permute-start.8 = (bf16[64,640]{1,0:T(8,128)(2,1)S(1)}, bf16[64,640]{1,0:T(8,128)(2,1)S(1)}, u32[]{:S(2)}, u32[]{:S(2)}) collective-permute-start(bf16[64,640]{1,0:T(8,128)(2,1)S(1)} %get-tuple-element.105), channel_id=1, source_target_pairs={{0,2},{1,3},{2,4},{3,5},{4,6},{5,7},{6,8},{7,9},{8,10},{9,11},{10,... | collective-permute-start | bytes 245768 | tf_op jit(solution)/shard_map/ppermute | solution.py:684
  26.6 8.9 %collective-permute-start.9 = (bf16[64,640]{1,0:T(8,128)(2,1)S(1)}, bf16[64,640]{1,0:T(8,128)(2,1)S(1)}, u32[]{:S(2)}, u32[]{:S(2)}) collective-permute-start(bf16[64,640]{1,0:T(8,128)(2,1)S(1)} %get-tuple-element.106), channel_id=1, source_target_pairs={{0,3},{1,2},{2,5},{3,4},{4,7},{5,6},{6,9},{7,8},{8,11},{9,10},{10,... | collective-permute-start | bytes 245768 | tf_op jit(solution)/shard_map/ppermute | solution.py:684
  29.3 10.2 %collective-permute-start.6 = (bf16[64,640]{1,0:T(8,128)(2,1)S(1)}, bf16[64,640]{1,0:T(8,128)(2,1)S(1)}, u32[]{:S(2)}, u32[]{:S(2)}) collective-permute-start(bf16[64,640]{1,0:T(8,128)(2,1)S(1)} %get-tuple-element.103.refs_8_), channel_id=1, source_target_pairs={{0,31},{1,30},{2,1},{3,0},{4,3},{5,2},{6,5},{7,4},{8,7},{9,6},{10,... | collective-permute-start | bytes 245768 | tf_op jit(solution)/shard_map/ppermute | solution.py:684
  32.3 7.2 %collective-permute-start.5 = (bf16[64,640]{1,0:T(8,128)(2,1)S(1)}, bf16[64,640]{1,0:T(8,128)(2,1)S(1)}, u32[]{:S(2)}, u32[]{:S(2)}) collective-permute-start(bf16[64,640]{1,0:T(8,128)(2,1)S(1)} %get-tuple-element.103.refs_8_), channel_id=1, source_target_pairs={{0,30},{1,31},{2,0},{3,1},{4,2},{5,3},{6,4},{7,5},{8,6},{9,7},{10,... | collective-permute-start | bytes 245768 | tf_op jit(solution)/shard_map/ppermute | solution.py:684
  37.4 6.0 %collective-permute-start.12 = (bf16[96,640]{1,0:T(8,128)(2,1)S(1)}, bf16[96,640]{1,0:T(8,128)(2,1)S(1)}, u32[]{:S(2)}, u32[]{:S(2)}) collective-permute-start(bf16[96,640]{1,0:T(8,128)(2,1)S(1)} %get-tuple-element.122), channel_id=1, source_target_pairs={{0,1},{1,0},{2,3},{3,2},{4,5},{5,4},{6,7},{7,6},{8,9},{9,8},{10,11... | collective-permute-start | bytes 368648 | tf_op jit(solution)/shard_map/ppermute | solution.py:684
  38.0 5.4 %collective-permute-start.11 = (bf16[64,640]{1,0:T(8,128)(2,1)S(1)}, bf16[64,640]{1,0:T(8,128)(2,1)S(1)}, u32[]{:S(2)}, u32[]{:S(2)}) collective-permute-start(bf16[64,640]{1,0:T(8,128)(2,1)S(1)} %get-tuple-element.118), channel_id=1, source_target_pairs={{0,0},{1,1},{2,30},{3,31},{4,28},{5,29},{6,26},{7,27},{8,24},{9,25... | collective-permute-start | bytes 245768 | tf_op jit(solution)/shard_map/ppermute | solution.py:684
  38.9 0.7 copy-start.3
  41.9 5.4 %collective-permute-start.10 = (bf16[128,640]{1,0:T(8,128)(2,1)S(1)}, bf16[128,640]{1,0:T(8,128)(2,1)S(1)}, u32[]{:S(2)}, u32[]{:S(2)}) collective-permute-start(bf16[128,640]{1,0:T(8,128)(2,1)S(1)} %get-tuple-element.116), channel_id=1, source_target_pairs={{0,1},{1,0},{2,3},{3,2},{4,5},{5,4},{6,7},{7,6},{8,9},{9,8},{10,11... | collective-permute-start | bytes 491528 | tf_op jit(solution)/shard_map/ppermute | solution.py:684
  45.2 11.7 %collective-permute-start.13 = (bf16[128,480]{1,0:T(8,128)(2,1)S(1)}, bf16[128,480]{1,0:T(8,128)(2,1)S(1)}, u32[]{:S(2)}, u32[]{:S(2)}) collective-permute-start(bf16[128,480]{1,0:T(8,128)(2,1)S(1)} %get-tuple-element.131), channel_id=1, source_target_pairs={{0,1},{1,0},{2,3},{3,2},{4,5},{5,4},{6,7},{7,6},{8,9},{9,8},{10,11... | collective-permute-start | bytes 368648 | tf_op jit(solution)/shard_map/ppermute | solution.py:684
  49.6 8.7 %collective-permute-start.14 = (bf16[32,640]{1,0:T(8,128)(2,1)S(1)}, bf16[32,640]{1,0:T(8,128)(2,1)S(1)}, u32[]{:S(2)}, u32[]{:S(2)}) collective-permute-start(bf16[32,640]{1,0:T(8,128)(2,1)S(1)} %get-tuple-element.132), channel_id=1, source_target_pairs={{0,30},{1,31},{2,0},{3,1},{4,2},{5,3},{6,4},{7,5},{8,6},{9,7},{10,... | collective-permute-start | bytes 122888 | tf_op jit(solution)/shard_map/ppermute | solution.py:684
  54.5 3.9 %collective-permute-start.15 = (bf16[32,640]{1,0:T(8,128)(2,1)S(1)}, bf16[32,640]{1,0:T(8,128)(2,1)S(1)}, u32[]{:S(2)}, u32[]{:S(2)}) collective-permute-start(bf16[32,640]{1,0:T(8,128)(2,1)S(1)} %get-tuple-element.133), channel_id=1, source_target_pairs={{0,31},{1,30},{2,1},{3,0},{4,3},{5,2},{6,5},{7,4},{8,7},{9,6},{10,... | collective-permute-start | bytes 122888 | tf_op jit(solution)/shard_map/ppermute | solution.py:684
  56.9 7.2 %collective-permute-start.18 = (bf16[128,480]{1,0:T(8,128)(2,1)S(1)}, bf16[128,480]{1,0:T(8,128)(2,1)S(1)}, u32[]{:S(2)}, u32[]{:S(2)}) collective-permute-start(bf16[128,480]{1,0:T(8,128)(2,1)S(1)} %get-tuple-element.141), channel_id=1, source_target_pairs={{0,1},{1,0},{2,3},{3,2},{4,5},{5,4},{6,7},{7,6},{8,9},{9,8},{10,11... | collective-permute-start | bytes 368648 | tf_op jit(solution)/shard_map/ppermute | solution.py:684
  58.6 7.6 %collective-permute-start.17 = (bf16[128,320]{1,0:T(8,128)(2,1)S(1)}, bf16[128,320]{1,0:T(8,128)(2,1)S(1)}, u32[]{:S(2)}, u32[]{:S(2)}) collective-permute-start(bf16[128,320]{1,0:T(8,128)(2,1)S(1)} %get-tuple-element.138), channel_id=1, source_target_pairs={{0,30},{1,31},{2,28},{3,29},{4,26},{5,27},{6,24},{7,25},{8,22},{9,... | collective-permute-start | bytes 245768 | tf_op jit(solution)/shard_map/ppermute | solution.py:684
  62.0 6.8 %collective-permute-start.16 = (bf16[128,320]{1,0:T(8,128)(2,1)S(1)}, bf16[128,320]{1,0:T(8,128)(2,1)S(1)}, u32[]{:S(2)}, u32[]{:S(2)}) collective-permute-start(bf16[128,320]{1,0:T(8,128)(2,1)S(1)} %get-tuple-element.136.refs_4_.refs_6_), channel_id=1, source_target_pairs={{0,2},{1,3},{2,4},{3,5},{4,6},{5,7},{6,8},{7,9},{8,10},{9,11},{10,... | collective-permute-start | bytes 245768 | tf_op jit(solution)/shard_map/ppermute | solution.py:684

commit v4 on v2

--- a/solution.py
+++ b/solution.py
@@ -92,15 +92,19 @@
 
 def group_sums(z, first, second):
     width = first.shape[1]
-    line = lax.broadcasted_iota(jnp.int32, (8, width), 0)
-    both = jnp.where(line == 0, first, jnp.where(line == 1, second, 0.0))
+    line = lax.broadcasted_iota(jnp.int32, (16, width), 0)
+    rows = jnp.zeros((16, width), F32)
+    for start, rest in ((0, first), (3, second)):
+        for j in range(3):
+            piece = rest.astype(BF).astype(F32)
+            rows = jnp.where(line == start + j, piece, rows)
+            rest = rest - piece
     across = lax.broadcasted_iota(jnp.int32, (width, width), 1).astype(F32)
     down = lax.broadcasted_iota(jnp.int32, (width, width), 0).astype(F32)
     same = jnp.floor((across + 0.5) * (1.0 / z.group)) == jnp.floor((down + 0.5) * (1.0 / z.group))
-    sums = jnp.dot(
-        both, same.astype(F32), precision=lax.Precision.HIGHEST, preferred_element_type=F32
-    )
-    return sums[0:1], sums[1:2]
+    ones = jnp.where(same, 1.0, 0.0).astype(BF)
+    sums = jnp.dot(rows.astype(BF), ones, preferred_element_type=F32)
+    return sums[0:1] + sums[1:2] + sums[2:3], sums[3:4] + sums[4:5] + sums[5:6]
 
 
 def normalize(z, x):

time: 64.5 us -> 63.6 us (0.986)
  Pallas kernels: 24.7 us -> 23.4 us
    pallas_call x18, Pallas kernels: 24.7 us -> 23.4 us  [call(): pl.pallas_call(inner, name=name, out_shape=[jax.ShapeDtypeStruct(shape, d...]
  transfers between devices with their start and end apart: 19 -> 19, of which waited for: 5 -> 5; matrix products, arithmetic and copies ran while one was open for 0% -> 0% of each run, Pallas kernels for 33% -> 32%
where the time goes in v4:
time: 63.6 us; the launch traced here: 63.4 us
  starting transfers between devices  32.3 us (51%)
  Pallas kernels  23.4 us (37%)
  waiting for transfers between devices  6.85 us (11%)
  between operations  0.85 us (1%)
    ppermute x19, starting transfers between devices, move(): return lax.ppermute(x, ('section', 'row'), route)  32.3 us
    pallas_call x18, Pallas kernels, call(): pl.pallas_call(inner, name=name, out_shape=[jax.ShapeDtypeStruct(shape, d...  23.4 us
    ppermute x19, waiting for transfers between devices, move(): return lax.ppermute(x, ('section', 'row'), route)  6.85 us
  transfers between devices with their start and end apart: 19, of which 5 were waited for; matrix products, arithmetic and copies ran while one was open for 0% of the time, Pallas kernels for 32%

profile of v4, /device:TPU:0, one launch (start us, length us, event | category | flops | bytes accessed | tf_op | source)
XLA Modules:
  0.0 63.4 jit_solution(16956382111733083605)
XLA Ops:
  0.6 1.7 %pack_first.1 = (bf16[32,640]{1,0:T(8,128)(2,1)S(1)}, bf16[32,640]{1,0:T(8,128)(2,1)S(1)}, bf16[3,128,320]{2,1,0:T(8,128)(2,1)S(1)}, bf16[3,128,320]{2,1,0:T(8,1...) custom-call(s32[2,16]{1,0:T(2,128)} %bitcast.24, s32[2,16]{1,0:T(2,128)} %bitcast.32, ...), custom_call_target="tpu_custom_call" | custom-call | flops 1 | bytes 1 | tf_op jit(solution)/shard_map/pack_first/pallas_call | solution.py:206
  2.4 3.0 %collective-permute-start = (bf16[32,640]{1,0:T(8,128)(2,1)S(1)}, bf16[32,640]{1,0:T(8,128)(2,1)S(1)}, u32[]{:S(2)}, u32[]{:S(2)}) collective-permute-start(bf16[32,640]{1,0:T(8,128)(2,1)S(1)} %get-tuple-element.84), channel_id=1, source_target_pairs={{0,1},{1,0},{2,3},{3,2},{4,5},{5,4},{6,7},{7,6},{8,9},{9,8},{10,11... | collective-permute-start | bytes 122888 | tf_op jit(solution)/shard_map/ppermute | solution.py:688
  5.4 1.2 %pack_later.1 = (bf16[128,640]{1,0:T(8,128)(2,1)S(1)}, bf16[128,640]{1,0:T(8,128)(2,1)S(1)}, bf16[64,640]{1,0:T(8,128)(2,1)S(1)}, bf16[64,640]{1,0:T(8,128)(2,1)...) custom-call(s32[2,16]{1,0:T(2,128)} %bitcast.25, ...), custom_call_target="tpu_custom_call" | custom-call | flops 1 | bytes 1 | tf_op jit(solution)/shard_map/pack_later/pallas_call | solution.py:206
  6.6 0.7 %collective-permute-done.refs_1_ = bf16[32,640]{1,0:T(8,128)(2,1)S(1)} collective-permute-done((bf16[32,640]{1,0:T(8,128)(2,1)S(1)}, bf16[32,640]{1,0:T(8,128)(2,1)S(1)}, u32[]{:S(2)}, u32[]{:S(2)}) %collective-permute-start) | collective-permute-done | bytes 40992 | tf_op jit(solution)/shard_map/ppermute | solution.py:688
  7.4 2.0 %collective-permute-start.1 = (bf16[128,640]{1,0:T(8,128)(2,1)S(1)}, bf16[128,640]{1,0:T(8,128)(2,1)S(1)}, u32[]{:S(2)}, u32[]{:S(2)}) collective-permute-start(bf16[128,640]{1,0:T(8,128)(2,1)S(1)} %get-tuple-element.86), channel_id=1, source_target_pairs={{0,1},{1,0},{2,3},{3,2},{4,5},{5,4},{6,7},{7,6},{8,9},{9,8},{10,11... | collective-permute-start | bytes 491528 | tf_op jit(solution)/shard_map/ppermute | solution.py:688
  9.4 1.2 %first_forward.1 = (f32[256,160]{1,0:T(8,128)S(1)}, bf16[256,160]{1,0:T(8,128)(2,1)S(1)}, bf16[128,640]{1,0:T(8,128)(2,1)S(1)}) custom-call(bf16[32,640]{1,0:T(8,128)(2,1)S(1)} %get-tuple-element.81.refs_6_.refs_0_, bf16[32,640]{1,0:T(8,128)(2,1)S(1)} %collective-permute-done.refs_1_, bf16[64,640]{1,0:T(8,128)(2,1)S(1)} %get-tuple-element.89.refs_2_.refs_3_.refs_5_, ...), custom_call_target="tpu_custom_call" | custom-call | flops 1 | bytes 1 | tf_op jit(solution)/shard_map/first_forward/pallas_call | solution.py:206
  10.6 0.1 collective-permute-start.3
  10.6 3.1 %collective-permute-done.1.refs_1_.refs_4_ = bf16[128,640]{1,0:T(8,128)(2,1)S(1)} collective-permute-done((bf16[128,640]{1,0:T(8,128)(2,1)S(1)}, bf16[128,640]{1,0:T(8,128)(2,1)S(1)}, u32[]{:S(2)}, u32[]{:S(2)}) %collective-permute-start.1) | collective-permute-done | bytes 163872 | tf_op jit(solution)/shard_map/ppermute | solution.py:688
  13.8 1.3 %first_backward.1 = (bf16[256,160]{1,0:T(8,128)(2,1)S(1)}, bf16[64,640]{1,0:T(8,128)(2,1)S(1)}, bf16[3,320,320]{2,1,0:T(8,128)(2,1)S(1)}, bf16[256,160]{1,0:T(8,128)(2,1)S(1)}, bf16[128,640]{1,0:T(8,128)(2,1)S(1)}) custom-call(bf16[128,640]{1,0:T(8,128)(2,1)S(1)} %get-tuple-element.85.refs_0_.refs_3_, ...), custom_call_target="tpu_custom_call" | custom-call | flops 1 | bytes 1 | tf_op jit(solution)/shard_map/first_backward/pallas_call | solution.py:206
  15.1 2.2 %collective-permute-start.2 = (bf16[128,640]{1,0:T(8,128)(2,1)S(1)}, bf16[128,640]{1,0:T(8,128)(2,1)S(1)}, u32[]{:S(2)}, u32[]{:S(2)}) collective-permute-start(bf16[128,640]{1,0:T(8,128)(2,1)S(1)} %get-tuple-element.93), channel_id=1, source_target_pairs={{0,1},{1,0},{2,3},{3,2},{4,5},{5,4},{6,7},{7,6},{8,9},{9,8},{10,11... | collective-permute-start | bytes 491528 | tf_op jit(solution)/shard_map/ppermute | solution.py:688
  17.3 0.2 collective-permute-start.4
  17.5 0.6 kernel_grads_add_9.1.refs_6_.refs_0_
  18.1 0.0 collective-permute-done.3.refs_1_.refs_4_.refs_6_
  18.1 1.3 %second_forward.1 = (bf16[256,160]{1,0:T(8,128)(2,1)S(1)}, bf16[256,320]{1,0:T(8,128)(2,1)S(1)}, bf16[64,640]{1,0:T(8,128)(2,1)S(1)}, bf16[64,640]{1,0:T(8,128)(2,1)S(1)}) custom-call(f32[256,160]{1,0:T(8,128)S(1)} %get-tuple-element.91.refs_5_.refs_0_, bf16[128,640]{1,0:T(8,128)(2,1)S(1)} %collective-permute-done.3.refs_1_.refs_4_.refs_6_, ...), custom_call_target="tpu_custom_call" | custom-call | flops 1 | bytes 1 | tf_op jit(solution)/shard_map/second_forward/pallas_call | solution.py:206
  19.3 0.0 copy-start.2
  19.3 4.5 %collective-permute-start.8 = (bf16[64,640]{1,0:T(8,128)(2,1)S(1)}, bf16[64,640]{1,0:T(8,128)(2,1)S(1)}, u32[]{:S(2)}, u32[]{:S(2)}) collective-permute-start(bf16[64,640]{1,0:T(8,128)(2,1)S(1)} %get-tuple-element.104), channel_id=1, source_target_pairs={{0,2},{1,3},{2,4},{3,5},{4,6},{5,7},{6,8},{7,9},{8,10},{9,11},{10,... | collective-permute-start | bytes 245768 | tf_op jit(solution)/shard_map/ppermute | solution.py:688
  23.9 0.5 collective-permute-start.9
  24.4 0.1 collective-permute-done.4.refs_5_.refs_4_
  24.5 0.0 collective-permute-done.2.refs_1_.refs_4_.refs_8_
  24.5 1.5 %second_backward.1 = (bf16[64,640]{1,0:T(8,128)(2,1)S(1)}, bf16[3,320,320]{2,1,0:T(8,128)(2,1)S(1)}, bf16[256,160]{1,0:T(8,128)(2,1)S(1)}, bf16[128,640]{1,0:T(8,128)(2,1)S(1)}) custom-call(bf16[256,160]{1,0:T(8,128)(2,1)S(1)} %get-tuple-element.92.refs_3_.refs_0_, bf16[128,640]{1,0:T(8,128)(2,1)S(1)} %collective-permute-done.2.refs_1_.refs_4_.refs_8_, ...), custom_call_target="tpu_custom_call" | custom-call | flops 1 | bytes 1 | tf_op jit(solution)/shard_map/second_backward/pallas_call | solution.py:206
  26.0 1.1 %collective-permute-start.7 = (bf16[128,640]{1,0:T(8,128)(2,1)S(1)}, bf16[128,640]{1,0:T(8,128)(2,1)S(1)}, u32[]{:S(2)}, u32[]{:S(2)}) collective-permute-start(bf16[128,640]{1,0:T(8,128)(2,1)S(1)} %get-tuple-element.103), channel_id=1, source_target_pairs={{0,1},{1,0},{2,3},{3,2},{4,5},{5,4},{6,7},{7,6},{8,9},{9,8},{10,11... | collective-permute-start | bytes 491528 | tf_op jit(solution)/shard_map/ppermute | solution.py:688
  27.1 4.2 %collective-permute-start.6 = (bf16[64,640]{1,0:T(8,128)(2,1)S(1)}, bf16[64,640]{1,0:T(8,128)(2,1)S(1)}, u32[]{:S(2)}, u32[]{:S(2)}) collective-permute-start(bf16[64,640]{1,0:T(8,128)(2,1)S(1)} %get-tuple-element.102.refs_8_), channel_id=1, source_target_pairs={{0,31},{1,30},{2,1},{3,0},{4,3},{5,2},{6,5},{7,4},{8,7},{9,6},{10,... | collective-permute-start | bytes 245768 | tf_op jit(solution)/shard_map/ppermute | solution.py:688
  31.3 0.4 collective-permute-start.5
  31.8 0.0 collective-permute-done.8.refs_1_
  31.8 1.7 %later_forward.1 = (f32[256,160]{1,0:T(8,128)S(1)}, bf16[256,160]{1,0:T(8,128)(2,1)S(1)}, bf16[256,160]{1,0:T(8,128)(2,1)S(1)}, bf16[64,640]{1,0:T(8,128)(2,1)S(1)}, bf16[96,640]{1,0:T(8,128)(2,1)S(1)}) custom-call(s32[2,16]{1,0:T(2,128)S(1)} %bitcast.26, bf16[64,640]{1,0:T(8,128)(2,1)S(1)} %collective-permute-done.8.refs_1_, ...), custom_call_target="tpu_custom_call" | custom-call | flops 1 | bytes 1 | tf_op jit(solution)/shard_map/later_forward/pallas_call | solution.py:206
  33.5 0.9 %collective-permute-start.12 = (bf16[96,640]{1,0:T(8,128)(2,1)S(1)}, bf16[96,640]{1,0:T(8,128)(2,1)S(1)}, u32[]{:S(2)}, u32[]{:S(2)}) collective-permute-start(bf16[96,640]{1,0:T(8,128)(2,1)S(1)} %get-tuple-element.120), channel_id=1, source_target_pairs={{0,1},{1,0},{2,3},{3,2},{4,5},{5,4},{6,7},{7,6},{8,9},{9,8},{10,11... | collective-permute-start | bytes 368648 | tf_op jit(solution)/shard_map/ppermute | solution.py:688
  34.4 0.7 %collective-permute-start.11 = (bf16[64,640]{1,0:T(8,128)(2,1)S(1)}, bf16[64,640]{1,0:T(8,128)(2,1)S(1)}, u32[]{:S(2)}, u32[]{:S(2)}) collective-permute-start(bf16[64,640]{1,0:T(8,128)(2,1)S(1)} %get-tuple-element.117), channel_id=1, source_target_pairs={{0,0},{1,1},{2,30},{3,31},{4,28},{5,29},{6,26},{7,27},{8,24},{9,25... | collective-permute-start | bytes 245768 | tf_op jit(solution)/shard_map/ppermute | solution.py:688
  35.1 0.0 copy-start.3
  35.1 0.6 kernel_grads_add_0.2.refs_12_.refs_0_
  35.8 0.0 copy-done.3
  35.8 2.0 %later_backward.1 = (bf16[256,160]{1,0:T(8,128)(2,1)S(1)}, bf16[3,320,320]{2,1,0:T(8,128)(2,1)S(1)}, bf16[256,160]{1,0:T(8,128)(2,1)S(1)}, bf16[256,320]{1,0:T(8...) custom-call(s32[2,16]{1,0:T(2,128)S(1)} %bitcast.27, ...), custom_call_target="tpu_custom_call" | custom-call | flops 1 | bytes 1 | tf_op jit(solution)/shard_map/later_backward/pallas_call | solution.py:206
  37.8 1.2 %collective-permute-start.10 = (bf16[128,640]{1,0:T(8,128)(2,1)S(1)}, bf16[128,640]{1,0:T(8,128)(2,1)S(1)}, u32[]{:S(2)}, u32[]{:S(2)}) collective-permute-start(bf16[128,640]{1,0:T(8,128)(2,1)S(1)} %get-tuple-element.115), channel_id=1, source_target_pairs={{0,1},{1,0},{2,3},{3,2},{4,5},{5,4},{6,7},{7,6},{8,9},{9,8},{10,11... | collective-permute-start | bytes 491528 | tf_op jit(solution)/shard_map/ppermute | solution.py:688
  39.1 1.7 %last_forward.1 = (bf16[128,480]{1,0:T(8,128)(2,1)S(1)}, bf16[128,480]{1,0:T(8,128)(2,1)S(1)}) custom-call(s32[2,16]{1,0:T(2,128)S(1)} %bitcast.28, f32[256,160]{1,0:T(8,128)S(1)} %get-tuple-element.111.refs_3_.refs_1_, bf16[96,640]{1,0:T(8,128)(2,1)S(1)} %collective-permute-done.12.refs_2_, bf16[256,160]{1,0:T(8,128)(2,1)S(1)} %get-tuple-element.121.refs_3_, ...), custom_call_target="tpu_custom_call" | custom-call | flops 1 | bytes 1 | tf_op jit(solution)/shard_map/last_forward/pallas_call | solution.py:206
  40.8 1.1 %collective-permute-start.13 = (bf16[128,480]{1,0:T(8,128)(2,1)S(1)}, bf16[128,480]{1,0:T(8,128)(2,1)S(1)}, u32[]{:S(2)}, u32[]{:S(2)}) collective-permute-start(bf16[128,480]{1,0:T(8,128)(2,1)S(1)} %get-tuple-element.129), channel_id=1, source_target_pairs={{0,1},{1,0},{2,3},{3,2},{4,5},{5,4},{6,7},{7,6},{8,9},{9,8},{10,11... | collective-permute-start | bytes 368648 | tf_op jit(solution)/shard_map/ppermute | solution.py:688
  41.9 0.6 kernel_grads_add_0.3.refs_2_.refs_1_
  42.5 0.2 pack_rows.1
  42.7 1.9 %collective-permute-done.10.refs_9_.refs_3_ = bf16[128,640]{1,0:T(8,128)(2,1)S(1)} collective-permute-done((bf16[128,640]{1,0:T(8,128)(2,1)S(1)}, bf16[128,640]{1,0:T(8,128)(2,1)S(1)}, u32[]{:S(2)}, u32[]{:S(2)}) %collective-permute-start.10) | collective-permute-done | bytes 163872 | tf_op jit(solution)/shard_map/ppermute | solution.py:688
  44.6 1.8 %write_queues.1 = (f32[8,128]{1,0:T(8,128)S(1)}, bf16[3,128,320]{2,1,0:T(8,128)(2,1)}, bf16[3,128,320]{2,1,0:T(8,128)(2,1)}, bf16[3,128,320]{2,1,0:T(8,128)(2,1)}, bf16[6,128,320]{2,1,0:T(8,128)(2,1)}) custom-call(s32[2,16]{1,0:T(2,128)S(1)} %bitcast.29, s32[2,16]{1,0:T(2,128)S(1)} %bitcast.35, bf16[3,128,320]{2,1,0:T(8,128)(2,1)S(1)} %get-tuple-element.77.refs_2_, ...), custom_call_target="tpu_custom_call" | custom-call | flops 1 | bytes 1 | tf_op jit(solution)/shard_map/write_queues/pallas_call | solution.py:206
  46.5 1.5 %collective-permute-start.16 = (bf16[128,480]{1,0:T(8,128)(2,1)S(1)}, bf16[128,480]{1,0:T(8,128)(2,1)S(1)}, u32[]{:S(2)}, u32[]{:S(2)}) collective-permute-start(bf16[128,480]{1,0:T(8,128)(2,1)S(1)} %get-tuple-element.136), channel_id=1, source_target_pairs={{0,1},{1,0},{2,3},{3,2},{4,5},{5,4},{6,7},{7,6},{8,9},{9,8},{10,11... | collective-permute-start | bytes 368648 | tf_op jit(solution)/shard_map/ppermute | solution.py:688
  47.9 0.2 add_rows.1
  48.2 3.8 %collective-permute-start.15 = (bf16[128,320]{1,0:T(8,128)(2,1)S(1)}, bf16[128,320]{1,0:T(8,128)(2,1)S(1)}, u32[]{:S(2)}, u32[]{:S(2)}) collective-permute-start(bf16[128,320]{1,0:T(8,128)(2,1)S(1)} %get-tuple-element.133), channel_id=1, source_target_pairs={{0,30},{1,31},{2,28},{3,29},{4,26},{5,27},{6,24},{7,25},{8,22},{9,... | collective-permute-start | bytes 245768 | tf_op jit(solution)/shard_map/ppermute | solution.py:688
  51.9 0.7 %collective-permute-start.14 = (bf16[128,320]{1,0:T(8,128)(2,1)S(1)}, bf16[128,320]{1,0:T(8,128)(2,1)S(1)}, u32[]{:S(2)}, u32[]{:S(2)}) collective-permute-start(bf16[128,320]{1,0:T(8,128)(2,1)S(1)} %get-tuple-element.131.refs_9_.refs_6_), channel_id=1, source_target_pairs={{0,2},{1,3},{2,4},{3,5},{4,6},{5,7},{6,8},{7,9},{8,10},{9,11},{10,... | collective-permute-start | bytes 245768 | tf_op jit(solution)/shard_map/ppermute | solution.py:688
  52.6 2.1 %last_backward.1 = (bf16[32,640]{1,0:T(8,128)(2,1)S(1)}, bf16[32,640]{1,0:T(8,128)(2,1)S(1)}, bf16[3,320,320]{2,1,0:T(8,128)(2,1)S(1)}, bf16[256,160]{1,0:T(8,128)(2,1)S(1)}) custom-call(s32[2,16]{1,0:T(2,128)S(1)} %bitcast.30, s32[2,16]{1,0:T(2,128)S(1)} %bitcast.36, bf16[256,160]{1,0:T(8,128)(2,1)S(1)} %get-tuple-element.122.refs_7_.refs_2_, ...), custom_call_target="tpu_custom_call" | custom-call | flops 1 | bytes 1 | tf_op jit(solution)/shard_map/last_backward/pallas_call | solution.py:206
  54.7 3.8 %collective-permute-start.17 = (bf16[32,640]{1,0:T(8,128)(2,1)S(1)}, bf16[32,640]{1,0:T(8,128)(2,1)S(1)}, u32[]{:S(2)}, u32[]{:S(2)}) collective-permute-start(bf16[32,640]{1,0:T(8,128)(2,1)S(1)} %get-tuple-element.137), channel_id=1, source_target_pairs={{0,30},{1,31},{2,0},{3,1},{4,2},{5,3},{6,4},{7,5},{8,6},{9,7},{10,... | collective-permute-start | bytes 122888 | tf_op jit(solution)/shard_map/ppermute | solution.py:688
  58.5 0.4 collective-permute-start.18
  58.9 2.2 %kernel_grads_last.1 = (f32[8,128]{1,0:T(8,128)S(1)}, f32[18,160,320]{2,1,0:T(8,128)}) custom-call(f32[9,160,320]{2,1,0:T(8,128)S(1)} %kernel_grads_add_0.2.refs_12_.refs_0_, f32[9,160,320]{2,1,0:T(8,128)S(1)} %kernel_grads_add_0.3.refs_2_.refs_1_, bf16[256,160]{1,0:T(8,128)(2,1)S(1)} %get-tuple-element.139.refs_2_, ...), custom_call_target="tpu_custom_call" | custom-call | flops 1 | bytes 1 | tf_op jit(solution)/shard_map/kernel_grads_last/pallas_call | solution.py:206
  61.1 0.9 %collective-permute-done.18.refs_13_ = bf16[32,640]{1,0:T(8,128)(2,1)S(1)} collective-permute-done((bf16[32,640]{1,0:T(8,128)(2,1)S(1)}, bf16[32,640]{1,0:T(8,128)(2,1)S(1)}, u32[]{:S(2)}, u32[]{:S(2)}) %collective-permute-start.18) | collective-permute-done | bytes 40992 | tf_op jit(solution)/shard_map/ppermute | solution.py:688
  62.0 1.5 %finish.1 = (bf16[3,128,320]{2,1,0:T(8,128)(2,1)}, bf16[3,128,320]{2,1,0:T(8,128)(2,1)}, bf16[3,128,320]{2,1,0:T(8,128)(2,1)}, bf16[6,128,320]{2,1,0:T(8,128)(2,1)}, bf16[2,128,320]{2,1,0:T(8,128)(2,1)}) custom-call(s32[2,16]{1,0:T(2,128)S(1)} %bitcast.31, ...), custom_call_target="tpu_custom_call", output_to_operand_aliasing={{0}: (2, {}), {1}: (3, {}), {2}: (4, {}), {3}: (5, {})} | custom-call | flops 1 | bytes 1 | tf_op jit(solution)/shard_map/finish/pallas_call | solution.py:206
  (16 shorter events, 0.0 us)
Async XLA Ops:
  0.6 8.8 %copy-start = (bf16[1,2,3,3,160,320]{5,4,3,2,1,0:T(8,128)(2,1)S(1)}, bf16[1,2,3,3,160,320]{5,4,3,2,1,0:T(8,128)(2,1)}, u32[]{:S(2)}) copy-start(bf16[1,2,3,3,160,320]{5,4,3,2,1,0:T(8,128)(2,1)} %param.12) | copy-start | bytes 5529604
  2.4 5.0 %collective-permute-start = (bf16[32,640]{1,0:T(8,128)(2,1)S(1)}, bf16[32,640]{1,0:T(8,128)(2,1)S(1)}, u32[]{:S(2)}, u32[]{:S(2)}) collective-permute-start(bf16[32,640]{1,0:T(8,128)(2,1)S(1)} %get-tuple-element.84), channel_id=1, source_target_pairs={{0,1},{1,0},{2,3},{3,2},{4,5},{5,4},{6,7},{7,6},{8,9},{9,8},{10,11... | collective-permute-start | bytes 122888 | tf_op jit(solution)/shard_map/ppermute | solution.py:688
  7.4 6.4 %collective-permute-start.1 = (bf16[128,640]{1,0:T(8,128)(2,1)S(1)}, bf16[128,640]{1,0:T(8,128)(2,1)S(1)}, u32[]{:S(2)}, u32[]{:S(2)}) collective-permute-start(bf16[128,640]{1,0:T(8,128)(2,1)S(1)} %get-tuple-element.86), channel_id=1, source_target_pairs={{0,1},{1,0},{2,3},{3,2},{4,5},{5,4},{6,7},{7,6},{8,9},{9,8},{10,11... | collective-permute-start | bytes 491528 | tf_op jit(solution)/shard_map/ppermute | solution.py:688
  9.4 8.1 %copy-start.1 = (f32[1,2,3,3,160,320]{5,4,3,2,1,0:T(8,128)S(1)}, f32[1,2,3,3,160,320]{5,4,3,2,1,0:T(8,128)}, u32[]{:S(2)}) copy-start(f32[1,2,3,3,160,320]{5,4,3,2,1,0:T(8,128)} %param.13) | copy-start | bytes 11059204
  10.6 7.5 %collective-permute-start.3 = (bf16[128,640]{1,0:T(8,128)(2,1)S(1)}, bf16[128,640]{1,0:T(8,128)(2,1)S(1)}, u32[]{:S(2)}, u32[]{:S(2)}) collective-permute-start(bf16[128,640]{1,0:T(8,128)(2,1)S(1)} %get-tuple-element.95), channel_id=1, source_target_pairs={{0,1},{1,0},{2,3},{3,2},{4,5},{5,4},{6,7},{7,6},{8,9},{9,8},{10,11... | collective-permute-start | bytes 491528 | tf_op jit(solution)/shard_map/ppermute | solution.py:688
  15.1 9.5 %collective-permute-start.2 = (bf16[128,640]{1,0:T(8,128)(2,1)S(1)}, bf16[128,640]{1,0:T(8,128)(2,1)S(1)}, u32[]{:S(2)}, u32[]{:S(2)}) collective-permute-start(bf16[128,640]{1,0:T(8,128)(2,1)S(1)} %get-tuple-element.93), channel_id=1, source_target_pairs={{0,1},{1,0},{2,3},{3,2},{4,5},{5,4},{6,7},{7,6},{8,9},{9,8},{10,11... | collective-permute-start | bytes 491528 | tf_op jit(solution)/shard_map/ppermute | solution.py:688
  17.3 7.2 %collective-permute-start.4 = (bf16[64,640]{1,0:T(8,128)(2,1)S(1)}, bf16[64,640]{1,0:T(8,128)(2,1)S(1)}, u32[]{:S(2)}, u32[]{:S(2)}) collective-permute-start(bf16[64,640]{1,0:T(8,128)(2,1)S(1)} %get-tuple-element.96), channel_id=1, source_target_pairs={{0,30},{1,31},{2,28},{3,29},{4,26},{5,27},{6,24},{7,25},{8,22},{9,... | collective-permute-start | bytes 245768 | tf_op jit(solution)/shard_map/ppermute | solution.py:688
  19.3 12.4 %copy-start.2 = (s32[16,2]{0,1:T(2,128)S(1)}, s32[16,2]{0,1:T(2,128)}, u32[]{:S(2)}) copy-start(s32[16,2]{0,1:T(2,128)} %param.14) | copy-start | bytes 388
  19.3 12.4 %collective-permute-start.8 = (bf16[64,640]{1,0:T(8,128)(2,1)S(1)}, bf16[64,640]{1,0:T(8,128)(2,1)S(1)}, u32[]{:S(2)}, u32[]{:S(2)}) collective-permute-start(bf16[64,640]{1,0:T(8,128)(2,1)S(1)} %get-tuple-element.104), channel_id=1, source_target_pairs={{0,2},{1,3},{2,4},{3,5},{4,6},{5,7},{6,8},{7,9},{8,10},{9,11},{10,... | collective-permute-start | bytes 245768 | tf_op jit(solution)/shard_map/ppermute | solution.py:688
  23.9 7.9 %collective-permute-start.9 = (bf16[64,640]{1,0:T(8,128)(2,1)S(1)}, bf16[64,640]{1,0:T(8,128)(2,1)S(1)}, u32[]{:S(2)}, u32[]{:S(2)}) collective-permute-start(bf16[64,640]{1,0:T(8,128)(2,1)S(1)} %get-tuple-element.105), channel_id=1, source_target_pairs={{0,3},{1,2},{2,5},{3,4},{4,7},{5,6},{6,9},{7,8},{8,11},{9,10},{10,... | collective-permute-start | bytes 245768 | tf_op jit(solution)/shard_map/ppermute | solution.py:688
  26.0 9.7 %collective-permute-start.7 = (bf16[128,640]{1,0:T(8,128)(2,1)S(1)}, bf16[128,640]{1,0:T(8,128)(2,1)S(1)}, u32[]{:S(2)}, u32[]{:S(2)}) collective-permute-start(bf16[128,640]{1,0:T(8,128)(2,1)S(1)} %get-tuple-element.103), channel_id=1, source_target_pairs={{0,1},{1,0},{2,3},{3,2},{4,5},{5,4},{6,7},{7,6},{8,9},{9,8},{10,11... | collective-permute-start | bytes 491528 | tf_op jit(solution)/shard_map/ppermute | solution.py:688
  27.1 8.6 %collective-permute-start.6 = (bf16[64,640]{1,0:T(8,128)(2,1)S(1)}, bf16[64,640]{1,0:T(8,128)(2,1)S(1)}, u32[]{:S(2)}, u32[]{:S(2)}) collective-permute-start(bf16[64,640]{1,0:T(8,128)(2,1)S(1)} %get-tuple-element.102.refs_8_), channel_id=1, source_target_pairs={{0,31},{1,30},{2,1},{3,0},{4,3},{5,2},{6,5},{7,4},{8,7},{9,6},{10,... | collective-permute-start | bytes 245768 | tf_op jit(solution)/shard_map/ppermute | solution.py:688
  31.3 4.4 %collective-permute-start.5 = (bf16[64,640]{1,0:T(8,128)(2,1)S(1)}, bf16[64,640]{1,0:T(8,128)(2,1)S(1)}, u32[]{:S(2)}, u32[]{:S(2)}) collective-permute-start(bf16[64,640]{1,0:T(8,128)(2,1)S(1)} %get-tuple-element.102.refs_8_), channel_id=1, source_target_pairs={{0,30},{1,31},{2,0},{3,1},{4,2},{5,3},{6,4},{7,5},{8,6},{9,7},{10,... | collective-permute-start | bytes 245768 | tf_op jit(solution)/shard_map/ppermute | solution.py:688
  33.5 5.5 %collective-permute-start.12 = (bf16[96,640]{1,0:T(8,128)(2,1)S(1)}, bf16[96,640]{1,0:T(8,128)(2,1)S(1)}, u32[]{:S(2)}, u32[]{:S(2)}) collective-permute-start(bf16[96,640]{1,0:T(8,128)(2,1)S(1)} %get-tuple-element.120), channel_id=1, source_target_pairs={{0,1},{1,0},{2,3},{3,2},{4,5},{5,4},{6,7},{7,6},{8,9},{9,8},{10,11... | collective-permute-start | bytes 368648 | tf_op jit(solution)/shard_map/ppermute | solution.py:688
  34.4 4.6 %collective-permute-start.11 = (bf16[64,640]{1,0:T(8,128)(2,1)S(1)}, bf16[64,640]{1,0:T(8,128)(2,1)S(1)}, u32[]{:S(2)}, u32[]{:S(2)}) collective-permute-start(bf16[64,640]{1,0:T(8,128)(2,1)S(1)} %get-tuple-element.117), channel_id=1, source_target_pairs={{0,0},{1,1},{2,30},{3,31},{4,28},{5,29},{6,26},{7,27},{8,24},{9,25... | collective-permute-start | bytes 245768 | tf_op jit(solution)/shard_map/ppermute | solution.py:688
  35.1 0.7 %copy-start.3 = (s32[16,2]{0,1:T(2,128)S(1)}, s32[16,2]{0,1:T(2,128)}, u32[]{:S(2)}) copy-start(s32[16,2]{0,1:T(2,128)} %param.15) | copy-start | bytes 388
  37.8 6.8 %collective-permute-start.10 = (bf16[128,640]{1,0:T(8,128)(2,1)S(1)}, bf16[128,640]{1,0:T(8,128)(2,1)S(1)}, u32[]{:S(2)}, u32[]{:S(2)}) collective-permute-start(bf16[128,640]{1,0:T(8,128)(2,1)S(1)} %get-tuple-element.115), channel_id=1, source_target_pairs={{0,1},{1,0},{2,3},{3,2},{4,5},{5,4},{6,7},{7,6},{8,9},{9,8},{10,11... | collective-permute-start | bytes 491528 | tf_op jit(solution)/shard_map/ppermute | solution.py:688
  40.8 5.7 %collective-permute-start.13 = (bf16[128,480]{1,0:T(8,128)(2,1)S(1)}, bf16[128,480]{1,0:T(8,128)(2,1)S(1)}, u32[]{:S(2)}, u32[]{:S(2)}) collective-permute-start(bf16[128,480]{1,0:T(8,128)(2,1)S(1)} %get-tuple-element.129), channel_id=1, source_target_pairs={{0,1},{1,0},{2,3},{3,2},{4,5},{5,4},{6,7},{7,6},{8,9},{9,8},{10,11... | collective-permute-start | bytes 368648 | tf_op jit(solution)/shard_map/ppermute | solution.py:688
  46.5 15.5 %collective-permute-start.16 = (bf16[128,480]{1,0:T(8,128)(2,1)S(1)}, bf16[128,480]{1,0:T(8,128)(2,1)S(1)}, u32[]{:S(2)}, u32[]{:S(2)}) collective-permute-start(bf16[128,480]{1,0:T(8,128)(2,1)S(1)} %get-tuple-element.136), channel_id=1, source_target_pairs={{0,1},{1,0},{2,3},{3,2},{4,5},{5,4},{6,7},{7,6},{8,9},{9,8},{10,11... | collective-permute-start | bytes 368648 | tf_op jit(solution)/shard_map/ppermute | solution.py:688
  48.2 13.8 %collective-permute-start.15 = (bf16[128,320]{1,0:T(8,128)(2,1)S(1)}, bf16[128,320]{1,0:T(8,128)(2,1)S(1)}, u32[]{:S(2)}, u32[]{:S(2)}) collective-permute-start(bf16[128,320]{1,0:T(8,128)(2,1)S(1)} %get-tuple-element.133), channel_id=1, source_target_pairs={{0,30},{1,31},{2,28},{3,29},{4,26},{5,27},{6,24},{7,25},{8,22},{9,... | collective-permute-start | bytes 245768 | tf_op jit(solution)/shard_map/ppermute | solution.py:688
  51.9 10.0 %collective-permute-start.14 = (bf16[128,320]{1,0:T(8,128)(2,1)S(1)}, bf16[128,320]{1,0:T(8,128)(2,1)S(1)}, u32[]{:S(2)}, u32[]{:S(2)}) collective-permute-start(bf16[128,320]{1,0:T(8,128)(2,1)S(1)} %get-tuple-element.131.refs_9_.refs_6_), channel_id=1, source_target_pairs={{0,2},{1,3},{2,4},{3,5},{4,6},{5,7},{6,8},{7,9},{8,10},{9,11},{10,... | collective-permute-start | bytes 245768 | tf_op jit(solution)/shard_map/ppermute | solution.py:688
  54.7 6.3 %collective-permute-start.17 = (bf16[32,640]{1,0:T(8,128)(2,1)S(1)}, bf16[32,640]{1,0:T(8,128)(2,1)S(1)}, u32[]{:S(2)}, u32[]{:S(2)}) collective-permute-start(bf16[32,640]{1,0:T(8,128)(2,1)S(1)} %get-tuple-element.137), channel_id=1, source_target_pairs={{0,30},{1,31},{2,0},{3,1},{4,2},{5,3},{6,4},{7,5},{8,6},{9,7},{10,... | collective-permute-start | bytes 122888 | tf_op jit(solution)/shard_map/ppermute | solution.py:688
  58.5 3.4 %collective-permute-start.18 = (bf16[32,640]{1,0:T(8,128)(2,1)S(1)}, bf16[32,640]{1,0:T(8,128)(2,1)S(1)}, u32[]{:S(2)}, u32[]{:S(2)}) collective-permute-start(bf16[32,640]{1,0:T(8,128)(2,1)S(1)} %get-tuple-element.138), channel_id=1, source_target_pairs={{0,31},{1,30},{2,1},{3,0},{4,3},{5,2},{6,5},{7,4},{8,7},{9,6},{10,... | collective-permute-start | bytes 122888 | tf_op jit(solution)/shard_map/ppermute | solution.py:688
